TPU v7x, 32 devices: a whole 2x2x4 slice. The times are simulated.
32 devices in a mesh: dp: 8 (over y, x, core), expert: 4 (over z).
Axes of the slice: x: 2, y: 2, z: 4, core: 2. Of those that a mesh axis runs over, the one named last changes fastest.
Arguments:
- tokens: bfloat16 [16384, 1024], P(('dp', 'expert')), may hold values from -6 to 6
- selections: int32 [8, 4, 4, 16], P('dp', 'expert'), may hold values from 0 to 511, as said below
- router: bfloat16 [4, 1024], P('expert'), may hold values from -0.1875 to 0.1875
- w_gate: bfloat16 [4, 1024, 512], P('expert', 'dp'), may hold values from -0.1875 to 0.1875
- w_up: bfloat16 [4, 1024, 512], P('expert', 'dp'), may hold values from -0.1875 to 0.1875
- w_down: bfloat16 [4, 512, 1024], P('expert', 'dp'), may hold values from -0.25 to 0.25
- cotangent: bfloat16 [16384, 1024], P(('dp', 'expert')), may hold values from -6 to 6
Outputs:
- mixed: bfloat16 [16384, 1024], P(('dp', 'expert'))
- grad_tokens: bfloat16 [16384, 1024], P(('dp', 'expert'))
- grad_gate: float32 [4, 1024, 512], P('expert', 'dp')
- grad_up: float32 [4, 1024, 512], P('expert', 'dp')
- grad_down: float32 [4, 512, 1024], P('expert', 'dp')
- grad_router: float32 [4, 1024], P('expert')
Inputs may be any that keep to these rules, and one draw needn't show every extreme that they name: `selections`: for every block of 512 tokens and every computed expert, the 16 positions are different.
All inputs are finite; a program needn't handle non-finite values.
Results may differ from a plain program's by a relative error of at most 0.0095.
Values may be sent and summed in bfloat16 or wider, within the bound.
No kernel may reach another device: no remote copies, remote signals or barrier semaphores. Data moves between devices by JAX's collectives and lax.ppermute only.
A program may use at most 64 MiB of HBM per device.

v0:
```python
import jax
import jax.numpy as jnp
from jax import lax
from jax.sharding import PartitionSpec as P


def contract_rows(left, right):
    return lax.dot_general(
        left, right, (((0,), (0,)), ((), ())), preferred_element_type=jnp.float32
    )


def contract_cols(left, right):
    return lax.dot_general(
        left, right, (((1,), (1,)), ((), ())), preferred_element_type=jnp.float32
    )


def local(tokens, selections, router, w_gate, w_up, w_down, cotangent):
    chosen = selections[0, 0]
    experts_here, slot_rows = chosen.shape
    width = tokens.shape[1]
    hidden_width = w_gate.shape[2]
    replicas = lax.axis_size("dp")
    chosen_flat = chosen.reshape(-1)
    send_rows = jnp.take(tokens, chosen_flat, axis=0).reshape(experts_here, slot_rows, width)
    positions = jnp.arange(tokens.shape[0], dtype=jnp.int32)
    one_hot = (positions[:, None] == chosen_flat[None, :]).astype(jnp.bfloat16)

    def combine(returned):
        return jnp.dot(
            one_hot, returned.reshape(-1, width), preferred_element_type=jnp.float32
        ).astype(jnp.bfloat16)

    x_rows = lax.all_to_all(send_rows, "expert", split_axis=0, concat_axis=1, tiled=True)
    x_rows = x_rows[0]
    router_vec = router[0]
    router_full = router_vec.astype(jnp.float32)
    gate_val = jax.nn.sigmoid(jnp.dot(x_rows, router_vec, preferred_element_type=jnp.float32))
    joined = jnp.concatenate([w_gate[0], w_up[0]], axis=1)
    down_part = w_down[0]
    columns = x_rows
    both_acts = jnp.dot(
        columns,
        lax.all_gather(joined, "dp", axis=0, tiled=True),
        preferred_element_type=jnp.float32,
    )
    act_gate = both_acts[:, :hidden_width]
    act_up = both_acts[:, hidden_width:]
    silu_gate = jax.nn.silu(act_gate)
    hidden = (silu_gate * act_up).astype(jnp.bfloat16)
    columns = hidden
    projected = jnp.dot(
        columns,
        lax.all_gather(down_part, "dp", axis=0, tiled=True),
        preferred_element_type=jnp.float32,
    )
    expert_out = (gate_val[:, None] * projected).astype(jnp.bfloat16)
    returned_out = lax.all_to_all(
        expert_out[None], "expert", split_axis=1, concat_axis=0, tiled=True
    )
    mixed = combine(returned_out)
    send_grads = jnp.take(cotangent, chosen_flat, axis=0).reshape(experts_here, slot_rows, width)
    d_rows = lax.all_to_all(send_grads, "expert", split_axis=0, concat_axis=1, tiled=True)[0]
    d_full = d_rows.astype(jnp.float32)
    gate_grad = jnp.sum(d_full * projected, axis=1)
    logit_grad = gate_grad * gate_val * (1.0 - gate_val)
    back_out = (gate_val[:, None] * d_full).astype(jnp.bfloat16)
    hidden_grad = contract_cols(back_out, lax.all_gather(down_part, "dp", axis=0, tiled=True))
    sigma = jax.nn.sigmoid(act_gate)
    grad_act_gate = (hidden_grad * act_up * sigma * (1.0 + act_gate * (1.0 - sigma))).astype(
        jnp.bfloat16
    )
    grad_act_up = (hidden_grad * silu_gate).astype(jnp.bfloat16)
    grad_joined = jnp.concatenate([grad_act_gate, grad_act_up], axis=1)
    input_grads = contract_cols(grad_joined, lax.all_gather(joined, "dp", axis=0, tiled=True))
    row_grads = (input_grads + logit_grad[:, None] * router_full[None, :]).astype(jnp.bfloat16)
    returned_grads = lax.all_to_all(
        row_grads[None], "expert", split_axis=1, concat_axis=0, tiled=True
    )
    grad_tokens = combine(returned_grads)
    columns = x_rows
    summed_joined = (
        lax.psum_scatter(
            contract_rows(columns, grad_joined).astype(jnp.bfloat16),
            "dp",
            scatter_dimension=0,
            tiled=True,
        ).astype(jnp.float32)
        / replicas
    )
    columns = hidden
    grad_down = (
        lax.psum_scatter(
            contract_rows(columns, back_out).astype(jnp.bfloat16),
            "dp",
            scatter_dimension=0,
            tiled=True,
        ).astype(jnp.float32)
        / replicas
    )
    router_term = jnp.dot(logit_grad, x_rows.astype(jnp.float32))
    grad_router = lax.psum(router_term, "dp") / replicas
    grad_gate = summed_joined[:, :hidden_width][None]
    grad_up = summed_joined[:, hidden_width:][None]
    return (mixed, grad_tokens, grad_gate, grad_up, grad_down[None], grad_router[None])


def solution(mesh):
    return jax.shard_map(
        local,
        mesh=mesh,
        in_specs=(
            P(("dp", "expert"), None),
            P("dp", "expert", None, None),
            P("expert", None),
            P("expert", "dp", None),
            P("expert", "dp", None),
            P("expert", "dp", None),
            P(("dp", "expert"), None),
        ),
        out_specs=(
            P(("dp", "expert"), None),
            P(("dp", "expert"), None),
            P("expert", "dp", None),
            P("expert", "dp", None),
            P("expert", "dp", None),
            P("expert", None),
        ),
        check_vma=False,
    )
```

profile of v0, /device:TPU:0, one launch (start us, length us, event | category | flops | bytes accessed | tf_op | source)
XLA Modules:
  0.0 159.3 jit_solution(18015640628581184012)
XLA Ops:
  7.2 0.0 copy-start
  7.2 0.0 copy-start.2
  7.2 0.0 all-gather.4.cloned.1.call-start
  7.2 0.0 copy-start.6
  7.2 1.8 %pad_maximum_fusion = bf16[128,1024]{1,0:T(8,128)(2,1)} fusion(bf16[128,512]{1,0:T(8,128)(2,1)} %bitcast.88, bf16[128,512]{1,0:T(8,128)(2,1)} %bitcast.89), kind=kLoop, calls=%fused_computation.25 | loop fusion | flops 524288 | bytes 524288 | tf_op jit(solution)/shard_map/concatenate | solution.py:40
  9.1 0.0 all-gather.4.cloned.1.call-update
  9.1 0.0 all-gather.6.cloned.1.call-start
  9.2 0.7 all-gather.6.cloned.1.call-update
  9.9 0.8 eq.16
  10.6 0.0 copy-done
  10.6 0.7 gather_fusion.1
  11.4 0.0 copy-done.2
  11.4 0.7 gather_fusion
  12.1 0.7 broadcast_select_fusion
  12.8 12.2 %all_to_all.16 = bf16[4,16,1024]{2,1,0:T(8,128)(2,1)S(1)} all-to-all(bf16[4,16,1024]{2,1,0:T(8,128)(2,1)S(1)} %bitcast.87), channel_id=1, replica_groups=mesh['dp'=8,'expert'=4] {'expert'}, dimensions={0} | all-to-all | bytes 262144 | tf_op jit(solution)/shard_map/all_to_all | solution.py:35
  25.0 3.3 %all-to-all-start.2 = ((bf16[4,16,1024]{2,1,0:T(8,128)(2,1)}), bf16[4,16,1024]{2,1,0:T(8,128)(2,1)S(1)}, u32[]{:S(2)}, u32[]{:S(2)}) async-start(bf16[4,16,1024]{2,1,0:T(8,128)(2,1)} %bitcast.7), calls=%async_computation.2 | async-start | bytes 262144 | tf_op jit(solution)/shard_map/all_to_all | solution.py:64
  28.3 0.0 reduce-scatter.5.cloned.1.call-start
  28.4 0.0 copy-done.6
  28.4 0.1 fusion.5
  28.6 5.7 %all-to-all-done.2 = bf16[4,16,1024]{2,1,0:T(8,128)(2,1)S(1)} async-done(((bf16[4,16,1024]{2,1,0:T(8,128)(2,1)}), bf16[4,16,1024]{2,1,0:T(8,128)(2,1)S(1)}, u32[]{:S(2)}, u32[]{:S(2)}) %all-to-all-start.2) | async-done | bytes 131104 | tf_op jit(solution)/shard_map/all_to_all | solution.py:64
  34.2 0.1 fusion.10
  34.3 6.8 %all-gather.4.cloned.1.call-done = bf16[1024,1024]{1,0:T(8,128)(2,1)} async-done(((bf16[128,1024]{1,0:T(8,128)(2,1)}), bf16[1024,1024]{1,0:T(8,128)(2,1)}) %all-gather.4.cloned.1.call-update) | async-done | bytes 2097168 | tf_op jit(solution)/shard_map/all_gather | solution.py:45
  41.2 2.1 %fusion.31 = f32[64,1024]{1,0:T(8,128)S(1)} fusion(bf16[64,1024]{1,0:T(8,128)(2,1)S(1)} %bitcast.80, bf16[1024,1024]{1,0:T(8,128)(2,1)} %all-gather.4.cloned.1.call-done), kind=kOutput, calls=%fused_computation.58 | convolution fusion | flops 134217728 | bytes 2490368 | tf_op jit(solution)/shard_map/dot_general | solution.py:43
  43.2 23.3 %all-gather.6.cloned.1.call-done = bf16[1,512,1024]{2,1,0:T(8,128)(2,1)} async-done(((bf16[1,64,1024]{2,1,0:T(8,128)(2,1)}), bf16[1,512,1024]{2,1,0:T(8,128)(2,1)}) %all-gather.6.cloned.1.call-update) | async-done | bytes 1048592 | tf_op jit(solution)/shard_map/all_gather | solution.py:55
  66.5 1.7 %multiply_convert_fusion.2 = (bf16[64,512]{1,0:T(8,128)(2,1)S(1)}, bf16[64,512]{1,0:T(8,128)(2,1)S(1)}, bf16[64,512]{1,0:T(8,128)(2,1)S(1)}) fusion(f32[64,1024]{1,0:T(8,128)S(1)} %fusion.31, bf16[64,1024]{1,0:T(8,128)(2,1)S(1)} %fusion.10, bf16[1,512,1024]{2,1,0:T(8,128)(2,1)} %all-gather.6.cloned.1.call-done), kind=kOutput, calls=%fused_computation.36 | convolution fusion | flops 67600384 | bytes 1638400 | tf_op jit(solution)/shard_map/dot_general | solution.py:14
  68.2 0.0 copy-start.3
  68.2 0.0 copy-start.4
  68.2 0.0 copy-start.5
  68.3 0.6 copy-done.3
  68.8 1.4 convolution_convert_fusion.1
  70.3 0.0 reduce-scatter.5.cloned.1.call-update
  70.3 0.0 reduce-scatter.3.cloned.1.call-start
  70.3 0.0 copy-done.4
  70.3 0.0 copy-done.5
  70.4 2.0 %convolution_convert_fusion = bf16[1024,1024]{1,0:T(8,128)(2,1)} fusion(bf16[64,1024]{1,0:T(8,128)(2,1)S(1)} %bitcast.81, bf16[64,512]{1,0:T(8,128)(2,1)S(1)} %get-tuple-element.10, bf16[64,512]{1,0:T(8,128)(2,1)S(1)} %get-tuple-element.9), kind=kOutput, calls=%fused_computation.2 | convolution fusion | flops 135528448 | bytes 2359296 | tf_op jit(solution)/shard_map/dot_general | solution.py:8
  72.4 0.0 copy-start.1
  72.4 0.0 reduce-scatter.3.cloned.1.call-update
  72.5 1.8 %fusion.11 = (f32[64]{0:T(128)S(1)}, bf16[1,64,1024]{2,1,0:T(8,128)(2,1)S(1)}) fusion(bf16[4,16,1024]{2,1,0:T(8,128)(2,1)S(1)} %all-to-all-done.2, f32[64]{0:T(128)S(1)} %fusion.5, bf16[64,512]{1,0:T(8,128)(2,1)} %copy-done.3, bf16[1,512,1024]{2,1,0:T(8,128)(2,1)} %all-gather.6.cloned.1.call-done), kind=kOutput, calls=%fused_computation.22 | convolution fusion | flops 67436480 | bytes 1376768 | tf_op jit(solution)/shard_map/dot_general | solution.py:53
  74.3 0.1 copy-done.1
  74.3 1.6 %fusion.1 = bf16[1,64,1024]{2,1,0:T(8,128)(2,1)S(1)} fusion(bf16[1024,1024]{1,0:T(8,128)(2,1)S(1)} %copy-done.1, f32[1024]{0:T(1024)S(1)} %mul.75, f32[64]{0:T(128)S(1)} %subtract_multiply_fusion, bf16[64,512]{1,0:T(8,128)(2,1)} %copy-done.5, bf16[64,512]{1,0:T(8,128)(2,1)} %copy-done.4), kind=kOutput, calls=%fused_computation.8 | convolution fusion | flops 134676480 | bytes 2363648 | tf_op jit(solution)/shard_map/dot_general | solution.py:14
  76.0 0.2 copy.29
  76.2 0.5 broadcast.24
  76.7 1.4 reduce.2
  78.1 0.7 reshape.86
  78.8 4.6 %all-to-all-start.3 = ((bf16[4,2,8192]{2,1,0:T(2,128)(2,1)}), bf16[4,2,8192]{2,1,0:T(2,128)(2,1)S(1)}, u32[]{:S(2)}, u32[]{:S(2)}) async-start(bf16[4,2,8192]{2,1,0:T(2,128)(2,1)} %reshape.86), calls=%async_computation.3 | async-start | bytes 262144 | tf_op jit(solution)/shard_map/all_to_all | solution.py:78
  83.4 0.2 copy.30
  83.6 1.4 reduce.1
  85.0 0.7 reshape.84
  85.7 0.1 fusion.28
  85.9 12.9 %psum.7 = f32[1024]{0:T(1024)S(1)} all-reduce(f32[1024]{0:T(1024)S(1)} %bitcast.90), channel_id=1, replica_groups=mesh['dp'=8,'expert'=4] {'dp'}, use_global_device_ids=true, to_apply=%region_3.5 | all-reduce | flops 1024 | bytes 8192 | tf_op jit(solution)/shard_map/psum | solution.py:103
  98.8 0.0 all-to-all-done.3
  98.8 4.8 %all-to-all-start.1 = ((bf16[4,2,8192]{2,1,0:T(2,128)(2,1)}), bf16[4,2,8192]{2,1,0:T(2,128)(2,1)S(1)}, u32[]{:S(2)}, u32[]{:S(2)}) async-start(bf16[4,2,8192]{2,1,0:T(2,128)(2,1)} %reshape.84), calls=%async_computation.1 | async-start | bytes 262144 | tf_op jit(solution)/shard_map/all_to_all | solution.py:59
  103.6 0.6 broadcast_multiply_fusion
  104.2 0.1 reshape.87
  104.4 5.2 %all-to-all-done.1 = bf16[4,2,8192]{2,1,0:T(2,128)(2,1)S(1)} async-done(((bf16[4,2,8192]{2,1,0:T(2,128)(2,1)}), bf16[4,2,8192]{2,1,0:T(2,128)(2,1)S(1)}, u32[]{:S(2)}, u32[]{:S(2)}) %all-to-all-start.1) | async-done | bytes 131104 | tf_op jit(solution)/shard_map/all_to_all | solution.py:59
  109.6 0.1 reshape.85
  109.7 1.4 convolution_convert_fusion.3
  111.1 1.4 convolution_convert_fusion.2
  112.5 0.0 reduce-scatter.5.cloned.1.call-done
  112.5 1.6 %multiply_bitcast_fusion = f32[1,64,1024]{2,1,0:T(8,128)} fusion(bf16[64,1024]{1,0:T(8,128)(2,1)} %reduce-scatter.5.cloned.1.call-done), kind=kLoop, calls=%fused_computation.26 | loop fusion | flops 131072 | bytes 393216 | tf_op jit(solution)/shard_map/broadcast_in_dim | solution.py:106
  114.1 36.8 %reduce-scatter.3.cloned.1.call-done = bf16[128,1024]{1,0:T(8,128)(2,1)} async-done(((bf16[1024,1024]{1,0:T(8,128)(2,1)}), bf16[128,1024]{1,0:T(8,128)(2,1)}) %reduce-scatter.3.cloned.1.call-update) | async-done | bytes 262160 | tf_op jit(solution)/shard_map/reduce_scatter | solution.py:84
  151.0 1.0 convert_multiply_fusion
  152.0 0.8 slice_bitcast_fusion
  (6 shorter events, 0.1 us)
Async XLA Ops:
  7.2 3.5 %copy-start = (bf16[512,1024]{1,0:T(8,128)(2,1)S(1)}, bf16[512,1024]{1,0:T(8,128)(2,1)}, u32[]{:S(2)}) copy-start(bf16[512,1024]{1,0:T(8,128)(2,1)} %param.15) | copy-start | bytes 3145732
  7.2 4.2 %copy-start.2 = (bf16[512,1024]{1,0:T(8,128)(2,1)S(1)}, bf16[512,1024]{1,0:T(8,128)(2,1)}, u32[]{:S(2)}) copy-start(bf16[512,1024]{1,0:T(8,128)(2,1)} %param.9) | copy-start | bytes 3145732
  7.2 34.0 %all-gather.4.cloned.1.call-start = ((), (), s32[]{:S(2)}) async-start(), calls=%async_computation.6 | async-start | bytes 2359296 | tf_op jit(solution)/shard_map/all_gather | solution.py:45
  7.2 21.2 %copy-start.6 = (bf16[1,1024]{1,0:T(2,128)(2,1)S(1)}, bf16[1,1024]{1,0:T(2,128)(2,1)}, u32[]{:S(2)}) copy-start(bf16[1,1024]{1,0:T(2,128)(2,1)} %param.11) | copy-start | bytes 6148
  9.1 57.4 %all-gather.6.cloned.1.call-start = ((), (), s32[]{:S(2)}) async-start(), calls=%async_computation.9 | async-start | bytes 1179648 | tf_op jit(solution)/shard_map/all_gather | solution.py:55
  25.0 9.2 %all-to-all-start.2 = ((bf16[4,16,1024]{2,1,0:T(8,128)(2,1)}), bf16[4,16,1024]{2,1,0:T(8,128)(2,1)S(1)}, u32[]{:S(2)}, u32[]{:S(2)}) async-start(bf16[4,16,1024]{2,1,0:T(8,128)(2,1)} %bitcast.7), calls=%async_computation.2 | async-start | bytes 262144 | tf_op jit(solution)/shard_map/all_to_all | solution.py:64
  28.3 84.1 %reduce-scatter.5.cloned.1.call-start = ((), (), s32[]{:S(2)}) async-start(), calls=%async_computation.8 | async-start | bytes 1179648 | tf_op jit(solution)/shard_map/reduce_scatter | solution.py:94
  68.2 0.6 copy-start.3
  68.2 2.1 %copy-start.4 = (bf16[64,512]{1,0:T(8,128)(2,1)}, bf16[64,512]{1,0:T(8,128)(2,1)S(1)}, u32[]{:S(2)}) copy-start(bf16[64,512]{1,0:T(8,128)(2,1)S(1)} %get-tuple-element.9) | copy-start | bytes 196612
  68.2 2.1 %copy-start.5 = (bf16[64,512]{1,0:T(8,128)(2,1)}, bf16[64,512]{1,0:T(8,128)(2,1)S(1)}, u32[]{:S(2)}) copy-start(bf16[64,512]{1,0:T(8,128)(2,1)S(1)} %get-tuple-element.10) | copy-start | bytes 196612
  70.3 80.7 %reduce-scatter.3.cloned.1.call-start = ((), (), s32[]{:S(2)}) async-start(), calls=%async_computation.7 | async-start | bytes 2359296 | tf_op jit(solution)/shard_map/reduce_scatter | solution.py:84
  72.4 1.9 %copy-start.1 = (bf16[1024,1024]{1,0:T(8,128)(2,1)S(1)}, bf16[1024,1024]{1,0:T(8,128)(2,1)}, u32[]{:S(2)}) copy-start(bf16[1024,1024]{1,0:T(8,128)(2,1)} %all-gather.4.cloned.1.call-done) | copy-start | bytes 6291460
  78.8 20.0 %all-to-all-start.3 = ((bf16[4,2,8192]{2,1,0:T(2,128)(2,1)}), bf16[4,2,8192]{2,1,0:T(2,128)(2,1)S(1)}, u32[]{:S(2)}, u32[]{:S(2)}) async-start(bf16[4,2,8192]{2,1,0:T(2,128)(2,1)} %reshape.86), calls=%async_computation.3 | async-start | bytes 262144 | tf_op jit(solution)/shard_map/all_to_all | solution.py:78
  98.8 10.7 %all-to-all-start.1 = ((bf16[4,2,8192]{2,1,0:T(2,128)(2,1)}), bf16[4,2,8192]{2,1,0:T(2,128)(2,1)S(1)}, u32[]{:S(2)}, u32[]{:S(2)}) async-start(bf16[4,2,8192]{2,1,0:T(2,128)(2,1)} %reshape.84), calls=%async_computation.1 | async-start | bytes 262144 | tf_op jit(solution)/shard_map/all_to_all | solution.py:59
Sparse Core Ops, SparseCore 0:
  10.5 30.6 all-gather.3
  43.0 23.4 all-gather.5
  70.4 36.0 reduce-scatter.4
  109.7 41.2 reduce-scatter.2
where the time goes:
time: 160 us; the launch traced here: 159 us
  waiting for transfers between devices  78.6 us (49%)
  blocking collectives  25.1 us (16%)
  between operations  14 us (9%)
  matrix products  13.7 us (9%)
  starting transfers between devices  12.9 us (8%)
  other arithmetic  8.71 us (5%)
  local copies, waits for them, and re-layouts  6.33 us (4%)
    reduce_scatter x1, waiting for transfers between devices, local(): lax.psum_scatter(contract_rows(columns, grad_joined).astype(jnp.bfloat16)...  36.8 us
    all_gather x1, waiting for transfers between devices, local(): lax.all_gather(down_part, 'dp', axis=0, tiled=True)  23.3 us
    psum x1, blocking collectives, local(): grad_router = lax.psum(router_term, 'dp') / replicas  12.9 us
    all_to_all x1, blocking collectives, local(): lax.all_to_all(send_rows, 'expert', split_axis=0, concat_axis=1, tiled=True)  12.2 us
    all_gather x1, waiting for transfers between devices, local(): lax.all_gather(joined, 'dp', axis=0, tiled=True)  6.83 us
    all_to_all x1, waiting for transfers between devices, local(): lax.all_to_all(send_grads, 'expert', split_axis=0, concat_axis=1, tiled=T...  5.68 us
    all_to_all x1, waiting for transfers between devices, local(): lax.all_to_all(expert_out[None], 'expert', split_axis=1, concat_axis=0, t...  5.2 us
    all_to_all x1, starting transfers between devices, local(): lax.all_to_all(expert_out[None], 'expert', split_axis=1, concat_axis=0, t...  4.82 us
  transfers between devices with their start and end apart: 7, of which 5 were waited for; matrix products, arithmetic and copies ran while one was open for 13% of the time, Pallas kernels for 0%

commit v1 on v0

v1 whole, which is shorter than its diff:
```python
import functools

import jax
import jax.numpy as jnp
from jax import lax
from jax.experimental import pallas as pl
from jax.experimental.pallas import tpu as pltpu
from jax.sharding import PartitionSpec as P

BF16 = jnp.bfloat16
F32 = jnp.float32
VMEM = pl.BlockSpec(memory_space=pltpu.VMEM)


def dot(left, right):
    return jnp.dot(left, right, preferred_element_type=F32)


def dot_rows(left, right):
    return lax.dot_general(left, right, (((0,), (0,)), ((), ())), preferred_element_type=F32)


def dot_cols(left, right):
    return lax.dot_general(left, right, (((1,), (1,)), ((), ())), preferred_element_type=F32)


def swap(value, axis, step):
    size = lax.axis_size(axis)
    return lax.ppermute(value, axis, [(i, i ^ step) for i in range(size)])


def shape(rows, columns, kind):
    return jax.ShapeDtypeStruct((rows, columns), kind)


def call(body, out_shape, args, scratch=(), flops=0, moved=0):
    return pl.pallas_call(
        body,
        out_shape=out_shape,
        in_specs=[VMEM] * len(args),
        out_specs=jax.tree.map(lambda _: VMEM, out_shape),
        scratch_shapes=list(scratch),
        compiler_params=pltpu.CompilerParams(vmem_limit_bytes=40 << 20),
        cost_estimate=pl.CostEstimate(flops=flops, bytes_accessed=moved, transcendentals=0),
    )(*args)


def pack_weights(gate_ref, up_ref, down_ref, first_ref, second_ref):
    rows = gate_ref.shape[1]
    half = gate_ref.shape[2]
    first_ref[:rows, :] = gate_ref[0]
    second_ref[:rows, :] = up_ref[0]
    first_ref[rows:, :] = down_ref[0, :, :half]
    second_ref[rows:, :] = down_ref[0, :, half:]


def take_rows(slots, chosen_ref, tokens_ref, cotangent_ref, *refs):
    out_refs, x_ref, d_ref = refs[:-2], refs[-2], refs[-1]
    picked = lax.broadcasted_iota(jnp.int32, (chosen_ref.shape[0], tokens_ref.shape[0]), 1)
    one_hot = jnp.where(picked == chosen_ref[...], 1.0, 0.0).astype(BF16)
    x_ref[...] = dot(one_hot, tokens_ref[...]).astype(BF16)
    d_ref[...] = dot(one_hot, cotangent_ref[...]).astype(BF16)
    me = lax.axis_index("expert")
    for k, out_ref in enumerate(out_refs):
        at = pl.ds(pl.multiple_of((me ^ k) * slots, slots), slots)
        out_ref[:slots, :] = x_ref[at, :]
        out_ref[slots:, :] = d_ref[at, :]


def prepare(slots, experts, chips, block, router_ref, *refs):
    got = refs[:experts]
    x_ref, d_ref = refs[experts], refs[experts + 1]
    out_refs = refs[experts + 2 :]
    for k, ref in enumerate(got):
        x_ref[k * slots : (k + 1) * slots, :] = ref[:slots, :]
        d_ref[k * slots : (k + 1) * slots, :] = ref[slots:, :]
    gate_val = gate_of(x_ref, router_ref)
    back = (gate_val * d_ref[...].astype(F32)).astype(BF16)
    width = back.shape[1]
    mine = lax.axis_index("dp") // 2
    for k, ref in enumerate(out_refs):
        start = ((mine ^ k) * (width // chips)) // block * block
        ref[:, :width] = back
        ref[:, width:] = x_ref[:, pl.ds(pl.multiple_of(start, 128), block)]


def gate_of(x_ref, router_ref):
    logit = jnp.sum(
        x_ref[...].astype(F32) * router_ref[...].astype(F32), axis=1, keepdims=True
    )
    return jax.nn.sigmoid(logit)


def expert(slots, experts, chips, block, *refs):
    devices = 2 * chips
    x_ref, d_ref, router_ref = refs[:3]
    firsts = refs[3 : 3 + devices]
    seconds = refs[3 + devices : 3 + 2 * devices]
    outs = refs[3 + 2 * devices :]
    return_refs, late_refs = outs[:experts], outs[experts : experts + chips]
    gate_w, up_w, down_w, hidden_ref = outs[experts + chips :]
    width = x_ref.shape[1]
    half = gate_w.shape[1]
    rows = width // devices
    down_rows = half // devices
    me = lax.axis_index("dp")
    for r in range(devices):
        at = pl.ds(pl.multiple_of((me ^ r) * rows, rows), rows)
        gate_w[at, :] = firsts[r][:rows, :]
        up_w[at, :] = seconds[r][:rows, :]
        at = pl.ds(pl.multiple_of((me ^ r) * down_rows, down_rows), down_rows)
        down_w[at, :half] = firsts[r][rows:, :]
        down_w[at, half:] = seconds[r][rows:, :]
    x = x_ref[...]
    d = d_ref[...]
    gate_val = gate_of(x_ref, router_ref)
    act_gate = dot(x, gate_w[...])
    act_up = dot(x, up_w[...])
    sigma = jax.nn.sigmoid(act_gate)
    silu = act_gate * sigma
    hidden = (silu * act_up).astype(BF16)
    hidden_ref[...] = hidden
    raw = dot_cols(d, down_w[...])
    gate_grad = jnp.sum(hidden.astype(F32) * raw, axis=1, keepdims=True)
    logit_grad = gate_grad * gate_val * (1.0 - gate_val)
    hidden_grad = gate_val * raw
    grad_gate = (hidden_grad * act_up * sigma * (1.0 + act_gate * (1.0 - sigma))).astype(BF16)
    grad_up = (hidden_grad * silu).astype(BF16)
    projected = dot(hidden, down_w[...])
    out_rows = (gate_val * projected).astype(BF16)
    row_grads = dot_cols(grad_gate, gate_w[...]) + dot_cols(grad_up, up_w[...])
    row_grads = (row_grads + logit_grad * router_ref[...].astype(F32)).astype(BF16)
    for k, ref in enumerate(return_refs):
        ref[:slots, :] = out_rows[k * slots : (k + 1) * slots, :]
        ref[slots:, :] = row_grads[k * slots : (k + 1) * slots, :]
    term = jnp.sum(logit_grad * x.astype(F32), axis=0, keepdims=True)
    high = term.astype(BF16).astype(F32)
    low = term - high
    tall = x.shape[0]
    mine = me // 2
    parts = width // block
    each = tall // parts
    tail = late_refs[0].shape[0] - tall
    for k, ref in enumerate(late_refs):
        start = ((mine ^ k) * (half // chips)) // block * block
        cut = hidden_ref[:, pl.ds(pl.multiple_of(start, 128), block)].astype(F32)
        lines = jnp.concatenate([cut[i * each : (i + 1) * each, :] for i in range(parts)], axis=1)
        empty = jnp.zeros((tail - each - 2, width), F32)
        ref[:tall, :half] = grad_gate
        ref[:tall, half:] = grad_up
        ref[tall:, :] = jnp.concatenate([lines, high, low, empty], axis=0).astype(BF16)


def weight_grads(chips, block, hidden_block, *refs):
    devices = 2 * chips
    mids, lates = refs[:devices], refs[devices : 2 * devices]
    gate_ref, up_ref, down_ref, router_ref, sum_ref, down_sum_ref = refs[2 * devices :]
    width = router_ref.shape[1]
    half = gate_ref.shape[2]
    tall = mids[0].shape[0]
    scale = 1.0 / devices
    parts = width // hidden_block
    each = tall // parts
    me = lax.axis_index("dp")
    feats = jnp.concatenate([m[:, width:] for m in mids], axis=0)
    backs = jnp.concatenate([m[:, :width] for m in mids], axis=0)
    grads = jnp.concatenate([t[:tall, :] for t in lates], axis=0)
    sum_ref[...] = dot_rows(feats, grads)
    rows = gate_ref.shape[1]
    at = pl.ds(pl.multiple_of((me * rows) % block, rows), rows)
    gate_ref[0] = sum_ref[at, :half] * scale
    up_ref[0] = sum_ref[at, half:] * scale
    tails = [t[tall:, :].astype(F32) for t in lates]
    hidden = jnp.concatenate(
        [t[:each, i * hidden_block : (i + 1) * hidden_block] for t in tails for i in range(parts)],
        axis=0,
    ).astype(BF16)
    down_sum_ref[...] = dot_rows(hidden, backs)
    rows = down_ref.shape[1]
    at = pl.ds(pl.multiple_of((me * rows) % hidden_block, rows), rows)
    down_ref[0] = down_sum_ref[at, :] * scale
    total = tails[0]
    for t in tails[1:]:
        total = total + t
    router_ref[...] = (total[each : each + 1, :] + total[each + 1 : each + 2, :]) * scale


def combine(slots, chosen_ref, *refs):
    got, (mixed_ref, grad_ref, out_ref, back_ref) = refs[:-4], refs[-4:]
    me = lax.axis_index("expert")
    for k, ref in enumerate(got):
        at = pl.ds(pl.multiple_of((me ^ k) * slots, slots), slots)
        out_ref[at, :] = ref[:slots, :]
        back_ref[at, :] = ref[slots:, :]
    picked = lax.broadcasted_iota(jnp.int32, (chosen_ref.shape[0], mixed_ref.shape[0]), 1)
    one_hot = jnp.where(picked == chosen_ref[...], 1.0, 0.0).astype(BF16)
    mixed_ref[...] = dot_rows(one_hot, out_ref[...]).astype(BF16)
    grad_ref[...] = dot_rows(one_hot, back_ref[...]).astype(BF16)


def local(tokens, selections, router, w_gate, w_up, w_down, cotangent):
    devices = lax.axis_size("dp")
    experts = lax.axis_size("expert")
    chips = devices // 2
    slots = selections.shape[3]
    taken = experts * slots
    held, width = tokens.shape
    rows, half = w_gate.shape[1:]
    down_rows = w_down.shape[1]
    block = max(128, 2 * rows)
    hidden_block = max(128, 2 * down_rows)
    chosen = selections.reshape(taken, 1)

    piece = shape(rows + down_rows, half, BF16)
    first, second = call(pack_weights, (piece, piece), (w_gate, w_up, w_down))
    firsts, seconds = [None] * devices, [None] * devices
    firsts[0], seconds[0] = first, second
    for k in range(1, chips):
        firsts[2 * k] = swap(first, "dp", 2 * k)
        seconds[2 * k] = swap(second, "dp", 2 * k)
    for k in range(chips):
        firsts[2 * k + 1] = swap(firsts[2 * k], "dp", 1)
        seconds[2 * k + 1] = swap(seconds[2 * k], "dp", 1)

    sent = call(
        functools.partial(take_rows, slots),
        (shape(2 * slots, width, BF16),) * experts,
        (chosen, tokens, cotangent),
        [pltpu.VMEM((taken, width), BF16)] * 2,
    )
    got = [sent[0]] + [swap(sent[k], "expert", k) for k in range(1, experts)]
    x_rows, d_rows, *mids = call(
        functools.partial(prepare, slots, experts, chips, block),
        (shape(taken, width, BF16),) * 2 + (shape(taken, width + block, BF16),) * chips,
        (router, *got),
    )
    mids = [mids[0]] + [swap(mids[k], "dp", 2 * k) for k in range(1, chips)]
    mids = mids + [swap(m, "dp", 1) for m in mids]

    lines = taken * hidden_block // width
    late_rows = taken + -(-(lines + 2) // 16) * 16
    outs = call(
        functools.partial(expert, slots, experts, chips, hidden_block),
        (shape(2 * slots, width, BF16),) * experts + (shape(late_rows, width, BF16),) * chips,
        (x_rows, d_rows, router, *firsts, *seconds),
        [
            pltpu.VMEM((width, half), BF16),
            pltpu.VMEM((width, half), BF16),
            pltpu.VMEM((half, width), BF16),
            pltpu.VMEM((taken, half), BF16),
        ],
    )
    returned, lates = outs[:experts], outs[experts:]
    returned = [returned[0]] + [swap(returned[k], "expert", k) for k in range(1, experts)]
    mixed, grad_tokens = call(
        functools.partial(combine, slots),
        (shape(held, width, BF16),) * 2,
        (chosen, *returned),
        [pltpu.VMEM((taken, width), BF16)] * 2,
    )
    lates = [lates[0]] + [swap(lates[k], "dp", 2 * k) for k in range(1, chips)]
    lates = lates + [swap(t, "dp", 1) for t in lates]
    grad_gate, grad_up, grad_down, grad_router = call(
        functools.partial(weight_grads, chips, block, hidden_block),
        (
            jax.ShapeDtypeStruct(w_gate.shape, F32),
            jax.ShapeDtypeStruct(w_up.shape, F32),
            jax.ShapeDtypeStruct(w_down.shape, F32),
            jax.ShapeDtypeStruct(router.shape, F32),
        ),
        (*mids, *lates),
        [pltpu.VMEM((block, 2 * half), F32), pltpu.VMEM((hidden_block, width), F32)],
    )
    return mixed, grad_tokens, grad_gate, grad_up, grad_down, grad_router


def solution(mesh):
    return jax.shard_map(
        local,
        mesh=mesh,
        in_specs=(
            P(("dp", "expert"), None),
            P("dp", "expert", None, None),
            P("expert", None),
            P("expert", "dp", None),
            P("expert", "dp", None),
            P("expert", "dp", None),
            P(("dp", "expert"), None),
        ),
        out_specs=(
            P(("dp", "expert"), None),
            P(("dp", "expert"), None),
            P("expert", "dp", None),
            P("expert", "dp", None),
            P("expert", "dp", None),
            P("expert", None),
        ),
        check_vma=False,
    )
```

time: 160 us -> 60.8 us (0.38)
  waiting for transfers between devices: 78.6 us -> 18.8 us
  blocking collectives: 25.1 us -> 0 us
  starting transfers between devices: 12.9 us -> 30 us
  matrix products: 13.7 us -> 0 us
  between operations: 14 us -> 0.76 us
  other arithmetic: 8.71 us -> 0 us
  Pallas kernels: 0 us -> 5.75 us
    reduce_scatter x2 -> x0, waiting for transfers between devices: 36.9 us -> none  [the longest x1 36.8 us: local(): lax.psum_scatter(contract_rows(columns, grad_joined).astype(jnp.bfloat16)...]
    all_gather x2 -> x0, waiting for transfers between devices: 30.1 us -> none  [the longest x1 23.3 us: local(): lax.all_gather(down_part, 'dp', axis=0, tiled=True)]
    ppermute x0 -> x34, starting transfers between devices: none -> 30 us  [swap(): return lax.ppermute(value, axis, [(i, i ^ step) for i in range(size)])]
    ppermute x0 -> x34, waiting for transfers between devices: none -> 18.8 us  [swap(): return lax.ppermute(value, axis, [(i, i ^ step) for i in range(size)])]
    dot_general x10 -> x0, matrix products: 13.7 us -> none  [the longest x2 3.46 us: contract_rows(): lax.dot_general(left, right, (((0,), (0,)), ((), ())), preferred_element_...]
    psum x1 -> x0, blocking collectives: 12.9 us -> none  [local(): grad_router = lax.psum(router_term, 'dp') / replicas]
    all_to_all x3 -> x0, starting transfers between devices: 12.7 us -> none  [the longest x1 4.82 us: local(): lax.all_to_all(expert_out[None], 'expert', split_axis=1, concat_axis=0, t...]
    all_to_all x1 -> x0, blocking collectives: 12.2 us -> none  [local(): lax.all_to_all(send_rows, 'expert', split_axis=0, concat_axis=1, tiled=True)]
  transfers between devices with their start and end apart: 7 -> 34, of which waited for: 5 -> 9; matrix products, arithmetic and copies ran while one was open for 13% -> 0% of each run, Pallas kernels for 0% -> 7%
where the time goes in v1:
time: 60.8 us; the launch traced here: 60.5 us
  starting transfers between devices  30 us (49%)
  waiting for transfers between devices  18.8 us (31%)
  Pallas kernels  5.75 us (9%)
  local copies, waits for them, and re-layouts  5.24 us (9%)
  between operations  0.76 us (1%)
    ppermute x34, starting transfers between devices, swap(): return lax.ppermute(value, axis, [(i, i ^ step) for i in range(size)])  30 us
    ppermute x34, waiting for transfers between devices, swap(): return lax.ppermute(value, axis, [(i, i ^ step) for i in range(size)])  18.8 us
    pallas_call x6, Pallas kernels, call(): pl.pallas_call(body, out_shape=out_shape, in_specs=[VMEM] * len(args), ou...  5.75 us
    unnamed x14, local copies, waits for them, and re-layouts  5.16 us
  transfers between devices with their start and end apart: 34, of which 9 were waited for; matrix products, arithmetic and copies ran while one was open for 0% of the time, Pallas kernels for 7%

profile of v1, /device:TPU:0, one launch (start us, length us, event | category | flops | bytes accessed | tf_op | source)
XLA Modules:
  0.0 60.5 jit_solution(13726549069578864595)
XLA Ops:
  0.6 0.9 %copy-done.2 = bf16[1,128,512]{2,1,0:T(8,128)(2,1)S(1)} copy-done((bf16[1,128,512]{2,1,0:T(8,128)(2,1)S(1)}, bf16[1,128,512]{2,1,0:T(8,128)(2,1)}, u32[]{:S(2)}) %copy-start.2) | copy-done | bytes 131096
  1.5 0.9 %copy-done.3 = bf16[1,128,512]{2,1,0:T(8,128)(2,1)S(1)} copy-done((bf16[1,128,512]{2,1,0:T(8,128)(2,1)S(1)}, bf16[1,128,512]{2,1,0:T(8,128)(2,1)}, u32[]{:S(2)}) %copy-start.3) | copy-done | bytes 131096
  2.4 0.9 %copy-done.4 = bf16[1,64,1024]{2,1,0:T(8,128)(2,1)S(1)} copy-done((bf16[1,64,1024]{2,1,0:T(8,128)(2,1)S(1)}, bf16[1,64,1024]{2,1,0:T(8,128)(2,1)}, u32[]{:S(2)}) %copy-start.4) | copy-done | bytes 131096
  3.4 4.0 %collective-permute-start.8 = (bf16[192,512]{1,0:T(8,128)(2,1)S(1)}, bf16[192,512]{1,0:T(8,128)(2,1)S(1)}, u32[]{:S(2)}, u32[]{:S(2)}) collective-permute-start(bf16[192,512]{1,0:T(8,128)(2,1)S(1)} %get-tuple-element.38.refs_3_), channel_id=1, source_target_pairs={{0,24},{4,28},{8,16},{12,20},{16,8},{20,12},{24,0},{28,4},{1,25},{... | collective-permute-start | bytes 589832 | tf_op jit(solution)/shard_map/ppermute | solution.py:29
  7.3 0.1 reshape.16.chosen_ref
  7.4 0.0 copy-start
  7.4 1.2 %copy-done = bf16[512,1024]{1,0:T(8,128)(2,1)S(1)} copy-done((bf16[512,1024]{1,0:T(8,128)(2,1)S(1)}, bf16[512,1024]{1,0:T(8,128)(2,1)}, u32[]{:S(2)}) %copy-start) | copy-done | bytes 1048600
  8.7 1.2 %copy-done.1 = bf16[512,1024]{1,0:T(8,128)(2,1)S(1)} copy-done((bf16[512,1024]{1,0:T(8,128)(2,1)S(1)}, bf16[512,1024]{1,0:T(8,128)(2,1)}, u32[]{:S(2)}) %copy-start.1) | copy-done | bytes 1048600
  9.9 0.5 shard_map.118
  10.4 0.0 copy-start.5
  10.4 1.6 %collective-permute-start = (bf16[32,1024]{1,0:T(8,128)(2,1)S(1)}, bf16[32,1024]{1,0:T(8,128)(2,1)S(1)}, u32[]{:S(2)}, u32[]{:S(2)}) collective-permute-start(bf16[32,1024]{1,0:T(8,128)(2,1)S(1)} %get-tuple-element.33), channel_id=1, source_target_pairs={{0,1},{1,0},{2,3},{3,2},{4,5},{5,4},{6,7},{7,6},{8,9},{9,8},{10,11... | collective-permute-start | bytes 196616 | tf_op jit(solution)/shard_map/ppermute | solution.py:29
  12.1 2.6 %collective-permute-start.1 = (bf16[32,1024]{1,0:T(8,128)(2,1)S(1)}, bf16[32,1024]{1,0:T(8,128)(2,1)S(1)}, u32[]{:S(2)}, u32[]{:S(2)}) collective-permute-start(bf16[32,1024]{1,0:T(8,128)(2,1)S(1)} %get-tuple-element.34), channel_id=1, source_target_pairs={{0,2},{1,3},{2,0},{3,1},{4,6},{5,7},{6,4},{7,5},{8,10},{9,11},{10,... | collective-permute-start | bytes 196616 | tf_op jit(solution)/shard_map/ppermute | solution.py:29
  14.7 0.5 collective-permute-start.6
  15.2 0.6 %collective-permute-start.4 = (bf16[192,512]{1,0:T(8,128)(2,1)S(1)}, bf16[192,512]{1,0:T(8,128)(2,1)S(1)}, u32[]{:S(2)}, u32[]{:S(2)}) collective-permute-start(bf16[192,512]{1,0:T(8,128)(2,1)S(1)} %get-tuple-element.38.refs_3_), channel_id=1, source_target_pairs={{0,8},{4,12},{8,0},{12,4},{16,24},{20,28},{24,16},{28,20},{1,9},{5... | collective-permute-start | bytes 589832 | tf_op jit(solution)/shard_map/ppermute | solution.py:29
  15.8 2.9 %collective-permute-start.2 = (bf16[32,1024]{1,0:T(8,128)(2,1)S(1)}, bf16[32,1024]{1,0:T(8,128)(2,1)S(1)}, u32[]{:S(2)}, u32[]{:S(2)}) collective-permute-start(bf16[32,1024]{1,0:T(8,128)(2,1)S(1)} %get-tuple-element.35), channel_id=1, source_target_pairs={{0,3},{1,2},{2,1},{3,0},{4,7},{5,6},{6,5},{7,4},{8,11},{9,10},{10,... | collective-permute-start | bytes 196616 | tf_op jit(solution)/shard_map/ppermute | solution.py:29
  18.7 3.1 %collective-permute-done.2.refs_3_ = bf16[32,1024]{1,0:T(8,128)(2,1)S(1)} collective-permute-done((bf16[32,1024]{1,0:T(8,128)(2,1)S(1)}, bf16[32,1024]{1,0:T(8,128)(2,1)S(1)}, u32[]{:S(2)}, u32[]{:S(2)}) %collective-permute-start.2) | collective-permute-done | bytes 65568 | tf_op jit(solution)/shard_map/ppermute | solution.py:29
  21.9 2.3 %collective-permute-start.15 = (bf16[192,512]{1,0:T(8,128)(2,1)S(1)}, bf16[192,512]{1,0:T(8,128)(2,1)S(1)}, u32[]{:S(2)}, u32[]{:S(2)}) collective-permute-start(bf16[192,512]{1,0:T(8,128)(2,1)S(1)} %get-tuple-element.39.refs_11_), channel_id=1, source_target_pairs={{0,24},{4,28},{8,16},{12,20},{16,8},{20,12},{24,0},{28,4},{1,25},{... | collective-permute-start | bytes 589832 | tf_op jit(solution)/shard_map/ppermute | solution.py:29
  24.2 0.0 collective-permute-done.8.refs_9_
  24.2 0.5 collective-permute-start.13
  24.7 0.0 collective-permute-done.6.refs_7_
  24.7 0.6 %collective-permute-start.11 = (bf16[192,512]{1,0:T(8,128)(2,1)S(1)}, bf16[192,512]{1,0:T(8,128)(2,1)S(1)}, u32[]{:S(2)}, u32[]{:S(2)}) collective-permute-start(bf16[192,512]{1,0:T(8,128)(2,1)S(1)} %get-tuple-element.39.refs_11_), channel_id=1, source_target_pairs={{0,8},{4,12},{8,0},{12,4},{16,24},{20,28},{24,16},{28,20},{1,9},{5... | collective-permute-start | bytes 589832 | tf_op jit(solution)/shard_map/ppermute | solution.py:29
  25.4 0.0 collective-permute-done.4.refs_5_
  25.4 0.1 shard_map.119
  25.5 0.0 collective-permute-done.3.refs_4_
  25.5 1.5 %collective-permute-start.20 = (bf16[64,1280]{1,0:T(8,128)(2,1)S(1)}, bf16[64,1280]{1,0:T(8,128)(2,1)S(1)}, u32[]{:S(2)}, u32[]{:S(2)}) collective-permute-start(bf16[64,1280]{1,0:T(8,128)(2,1)S(1)} %get-tuple-element.47), channel_id=1, source_target_pairs={{0,8},{4,12},{8,0},{12,4},{16,24},{20,28},{24,16},{28,20},{1,9},{5... | collective-permute-start | bytes 491528 | tf_op jit(solution)/shard_map/ppermute | solution.py:29
  27.0 2.4 %collective-permute-done.15.refs_17_ = bf16[192,512]{1,0:T(8,128)(2,1)S(1)} collective-permute-done((bf16[192,512]{1,0:T(8,128)(2,1)S(1)}, bf16[192,512]{1,0:T(8,128)(2,1)S(1)}, u32[]{:S(2)}, u32[]{:S(2)}) %collective-permute-start.15) | collective-permute-done | bytes 196640 | tf_op jit(solution)/shard_map/ppermute | solution.py:29
  29.4 1.3 %collective-permute-start.21 = (bf16[64,1280]{1,0:T(8,128)(2,1)S(1)}, bf16[64,1280]{1,0:T(8,128)(2,1)S(1)}, u32[]{:S(2)}, u32[]{:S(2)}) collective-permute-start(bf16[64,1280]{1,0:T(8,128)(2,1)S(1)} %get-tuple-element.48), channel_id=1, source_target_pairs={{0,16},{4,20},{8,24},{12,28},{16,0},{20,4},{24,8},{28,12},{1,17},{... | collective-permute-start | bytes 491528 | tf_op jit(solution)/shard_map/ppermute | solution.py:29
  30.7 2.2 %collective-permute-done.13.refs_15_ = bf16[192,512]{1,0:T(8,128)(2,1)S(1)} collective-permute-done((bf16[192,512]{1,0:T(8,128)(2,1)S(1)}, bf16[192,512]{1,0:T(8,128)(2,1)S(1)}, u32[]{:S(2)}, u32[]{:S(2)}) %collective-permute-start.13) | collective-permute-done | bytes 196640 | tf_op jit(solution)/shard_map/ppermute | solution.py:29
  32.9 0.0 collective-permute-start.9
  32.9 0.0 collective-permute-done.11.refs_13_
  32.9 0.5 collective-permute-start.7
  33.4 0.0 collective-permute-done.10.refs_12_
  33.4 0.1 collective-permute-start.5
  33.5 1.1 %collective-permute-done.20.refs_1_ = bf16[64,1280]{1,0:T(8,128)(2,1)S(1)} collective-permute-done((bf16[64,1280]{1,0:T(8,128)(2,1)S(1)}, bf16[64,1280]{1,0:T(8,128)(2,1)S(1)}, u32[]{:S(2)}, u32[]{:S(2)}) %collective-permute-start.20) | collective-permute-done | bytes 163872 | tf_op jit(solution)/shard_map/ppermute | solution.py:29
  34.6 0.0 collective-permute-start.16
  34.6 0.3 collective-permute-done.21.refs_2_
  34.9 0.2 collective-permute-start.14
  35.2 0.0 collective-permute-done.9.refs_10_
  35.2 0.3 collective-permute-start.12
  35.4 0.0 collective-permute-done.7.refs_8_
  35.4 2.2 %collective-permute-start.22 = (bf16[64,1280]{1,0:T(8,128)(2,1)S(1)}, bf16[64,1280]{1,0:T(8,128)(2,1)S(1)}, u32[]{:S(2)}, u32[]{:S(2)}) collective-permute-start(bf16[64,1280]{1,0:T(8,128)(2,1)S(1)} %get-tuple-element.49), channel_id=1, source_target_pairs={{0,24},{4,28},{8,16},{12,20},{16,8},{20,12},{24,0},{28,4},{1,25},{... | collective-permute-start | bytes 491528 | tf_op jit(solution)/shard_map/ppermute | solution.py:29
  37.6 0.0 collective-permute-start.23
  37.6 0.0 collective-permute-done.16.refs_18_
  37.6 0.5 collective-permute-start.24
  38.1 0.1 collective-permute-start.25
  38.2 1.8 %shard_map.121 = (bf16[32,1024]{1,0:T(8,128)(2,1)S(1)}, bf16[32,1024]{1,0:T(8,128)(2,1)S(1)}, bf16[32,1024]{1,0:T(8,128)(2,1)S(1)}, bf16[32,1024]{1,0:T(8,128)(2...) custom-call(bf16[64,1024]{1,0:T(8,128)(2,1)S(1)} %get-tuple-element., ...), custom_call_target="tpu_custom_call" | custom-call | tf_op jit(solution)/shard_map/pallas_call | solution.py:37
  40.0 0.5 collective-permute-start.27
  40.5 2.1 %collective-permute-done.22.refs_3_ = bf16[64,1280]{1,0:T(8,128)(2,1)S(1)} collective-permute-done((bf16[64,1280]{1,0:T(8,128)(2,1)S(1)}, bf16[64,1280]{1,0:T(8,128)(2,1)S(1)}, u32[]{:S(2)}, u32[]{:S(2)}) %collective-permute-start.22) | collective-permute-done | bytes 163872 | tf_op jit(solution)/shard_map/ppermute | solution.py:29
  42.7 1.0 %collective-permute-start.28 = (bf16[80,1024]{1,0:T(8,128)(2,1)S(1)}, bf16[80,1024]{1,0:T(8,128)(2,1)S(1)}, u32[]{:S(2)}, u32[]{:S(2)}) collective-permute-start(bf16[80,1024]{1,0:T(8,128)(2,1)S(1)} %get-tuple-element.52), channel_id=1, source_target_pairs={{0,16},{4,20},{8,24},{12,28},{16,0},{20,4},{24,8},{28,12},{1,17},{... | collective-permute-start | bytes 491528 | tf_op jit(solution)/shard_map/ppermute | solution.py:29
  43.6 0.0 collective-permute-done.23.refs_4_
  43.6 2.2 %collective-permute-start.29 = (bf16[80,1024]{1,0:T(8,128)(2,1)S(1)}, bf16[80,1024]{1,0:T(8,128)(2,1)S(1)}, u32[]{:S(2)}, u32[]{:S(2)}) collective-permute-start(bf16[80,1024]{1,0:T(8,128)(2,1)S(1)} %get-tuple-element.53), channel_id=1, source_target_pairs={{0,24},{4,28},{8,16},{12,20},{16,8},{20,12},{24,0},{28,4},{1,25},{... | collective-permute-start | bytes 491528 | tf_op jit(solution)/shard_map/ppermute | solution.py:29
  45.9 0.0 collective-permute-done.25.refs_6_
  45.9 1.7 %collective-permute-start.18 = (bf16[32,1024]{1,0:T(8,128)(2,1)S(1)}, bf16[32,1024]{1,0:T(8,128)(2,1)S(1)}, u32[]{:S(2)}, u32[]{:S(2)}) collective-permute-start(bf16[32,1024]{1,0:T(8,128)(2,1)S(1)} %get-tuple-element.42), channel_id=1, source_target_pairs={{0,2},{1,3},{2,0},{3,1},{4,6},{5,7},{6,4},{7,5},{8,10},{9,11},{10,... | collective-permute-start | bytes 196616 | tf_op jit(solution)/shard_map/ppermute | solution.py:29
  47.6 2.5 %collective-permute-done.17.refs_1_ = bf16[32,1024]{1,0:T(8,128)(2,1)S(1)} collective-permute-done((bf16[32,1024]{1,0:T(8,128)(2,1)S(1)}, bf16[32,1024]{1,0:T(8,128)(2,1)S(1)}, u32[]{:S(2)}, u32[]{:S(2)}) %collective-permute-start.17) | collective-permute-done | bytes 65568 | tf_op jit(solution)/shard_map/ppermute | solution.py:29
  50.1 1.2 %collective-permute-start.19 = (bf16[32,1024]{1,0:T(8,128)(2,1)S(1)}, bf16[32,1024]{1,0:T(8,128)(2,1)S(1)}, u32[]{:S(2)}, u32[]{:S(2)}) collective-permute-start(bf16[32,1024]{1,0:T(8,128)(2,1)S(1)} %get-tuple-element.43), channel_id=1, source_target_pairs={{0,3},{1,2},{2,1},{3,0},{4,7},{5,6},{6,5},{7,4},{8,11},{9,10},{10,... | collective-permute-start | bytes 196616 | tf_op jit(solution)/shard_map/ppermute | solution.py:29
  51.3 0.5 collective-permute-done.18.refs_2_
  51.8 0.0 collective-permute-start.26
  51.8 4.4 %collective-permute-done.19.refs_3_ = bf16[32,1024]{1,0:T(8,128)(2,1)S(1)} collective-permute-done((bf16[32,1024]{1,0:T(8,128)(2,1)S(1)}, bf16[32,1024]{1,0:T(8,128)(2,1)S(1)}, u32[]{:S(2)}, u32[]{:S(2)}) %collective-permute-start.19) | collective-permute-done | bytes 65568 | tf_op jit(solution)/shard_map/ppermute | solution.py:29
  56.2 0.0 collective-permute-start.30
  56.2 0.5 collective-permute-start.31
  56.7 0.1 collective-permute-start.32
  56.8 0.4 collective-permute-start.33
  57.2 1.8 %shard_map.122 = (bf16[512,1024]{1,0:T(8,128)(2,1)}, bf16[512,1024]{1,0:T(8,128)(2,1)}) custom-call(s32[64,1]{1,0:T(8,128)S(1)} %reshape.16.chosen_ref, bf16[32,1024]{1,0:T(8,128)(2,1)S(1)} %get-tuple-element.40.refs_0_, bf16[32,1024]{1,0:T(8,128)(2,1)S(1)} %collective-permute-done.17.refs_1_, bf16[32,1024]{1,0:T(8,128)(2,1)S(1)} %collective-permute-done.18.refs_2_, ...), custom_call_target="tpu_custom_call" | custom-call | tf_op jit(solution)/shard_map/pallas_call | solution.py:37
  59.1 1.4 %shard_map.123 = (f32[1,128,512]{2,1,0:T(8,128)}, f32[1,128,512]{2,1,0:T(8,128)}, f32[1,64,1024]{2,1,0:T(8,128)}, f32[1,1024]{1,0:T(1,128)}) custom-call(bf16[64,1280]{1,0:T(8,128)(2,1)S(1)} %get-tuple-element.46.refs_0_, bf16[64,1280]{1,0:T(8,128)(2,1)S(1)} %collective-permute-done.20.refs_1_, bf16[64,1280]{1,0:T(8,128)(2,1)S(1)} %collective-permute-done.21.refs_2_, ...), custom_call_target="tpu_custom_call" | custom-call | tf_op jit(solution)/shard_map/pallas_call | solution.py:37
  (25 shorter events, 0.1 us)
Async XLA Ops:
  0.6 0.9 %copy-start.2 = (bf16[1,128,512]{2,1,0:T(8,128)(2,1)S(1)}, bf16[1,128,512]{2,1,0:T(8,128)(2,1)}, u32[]{:S(2)}) copy-start(bf16[1,128,512]{2,1,0:T(8,128)(2,1)} %gate_ref.1) | copy-start | bytes 393220
  1.5 0.9 %copy-start.3 = (bf16[1,128,512]{2,1,0:T(8,128)(2,1)S(1)}, bf16[1,128,512]{2,1,0:T(8,128)(2,1)}, u32[]{:S(2)}) copy-start(bf16[1,128,512]{2,1,0:T(8,128)(2,1)} %up_ref.1) | copy-start | bytes 393220
  2.4 0.9 %copy-start.4 = (bf16[1,64,1024]{2,1,0:T(8,128)(2,1)S(1)}, bf16[1,64,1024]{2,1,0:T(8,128)(2,1)}, u32[]{:S(2)}) copy-start(bf16[1,64,1024]{2,1,0:T(8,128)(2,1)} %down_ref.1) | copy-start | bytes 393220
  3.3 4.0 %copy-start.6 = (s32[1,1,4,16]{3,2,1,0:T(4,128)S(1)}, s32[1,1,4,16]{3,2,1,0:T(4,128)}, u32[]{:S(2)}) copy-start(s32[1,1,4,16]{3,2,1,0:T(4,128)} %param.8) | copy-start | bytes 772
  3.4 20.8 %collective-permute-start.8 = (bf16[192,512]{1,0:T(8,128)(2,1)S(1)}, bf16[192,512]{1,0:T(8,128)(2,1)S(1)}, u32[]{:S(2)}, u32[]{:S(2)}) collective-permute-start(bf16[192,512]{1,0:T(8,128)(2,1)S(1)} %get-tuple-element.38.refs_3_), channel_id=1, source_target_pairs={{0,24},{4,28},{8,16},{12,20},{16,8},{20,12},{24,0},{28,4},{1,25},{... | collective-permute-start | bytes 589832 | tf_op jit(solution)/shard_map/ppermute | solution.py:29
  7.4 1.2 %copy-start = (bf16[512,1024]{1,0:T(8,128)(2,1)S(1)}, bf16[512,1024]{1,0:T(8,128)(2,1)}, u32[]{:S(2)}) copy-start(bf16[512,1024]{1,0:T(8,128)(2,1)} %tokens_ref.1) | copy-start | bytes 3145732
  8.7 1.2 %copy-start.1 = (bf16[512,1024]{1,0:T(8,128)(2,1)S(1)}, bf16[512,1024]{1,0:T(8,128)(2,1)}, u32[]{:S(2)}) copy-start(bf16[512,1024]{1,0:T(8,128)(2,1)} %cotangent_ref.1) | copy-start | bytes 3145732
  10.4 15.0 %copy-start.5 = (bf16[1,1024]{1,0:T(2,128)(2,1)S(1)}, bf16[1,1024]{1,0:T(2,128)(2,1)}, u32[]{:S(2)}) copy-start(bf16[1,1024]{1,0:T(2,128)(2,1)} %refs_2_.1) | copy-start | bytes 6148
  10.4 5.4 %collective-permute-start = (bf16[32,1024]{1,0:T(8,128)(2,1)S(1)}, bf16[32,1024]{1,0:T(8,128)(2,1)S(1)}, u32[]{:S(2)}, u32[]{:S(2)}) collective-permute-start(bf16[32,1024]{1,0:T(8,128)(2,1)S(1)} %get-tuple-element.33), channel_id=1, source_target_pairs={{0,1},{1,0},{2,3},{3,2},{4,5},{5,4},{6,7},{7,6},{8,9},{9,8},{10,11... | collective-permute-start | bytes 196616 | tf_op jit(solution)/shard_map/ppermute | solution.py:29
  12.1 6.6 %collective-permute-start.1 = (bf16[32,1024]{1,0:T(8,128)(2,1)S(1)}, bf16[32,1024]{1,0:T(8,128)(2,1)S(1)}, u32[]{:S(2)}, u32[]{:S(2)}) collective-permute-start(bf16[32,1024]{1,0:T(8,128)(2,1)S(1)} %get-tuple-element.34), channel_id=1, source_target_pairs={{0,2},{1,3},{2,0},{3,1},{4,6},{5,7},{6,4},{7,5},{8,10},{9,11},{10,... | collective-permute-start | bytes 196616 | tf_op jit(solution)/shard_map/ppermute | solution.py:29
  14.7 10.1 %collective-permute-start.6 = (bf16[192,512]{1,0:T(8,128)(2,1)S(1)}, bf16[192,512]{1,0:T(8,128)(2,1)S(1)}, u32[]{:S(2)}, u32[]{:S(2)}) collective-permute-start(bf16[192,512]{1,0:T(8,128)(2,1)S(1)} %get-tuple-element.38.refs_3_), channel_id=1, source_target_pairs={{0,16},{4,20},{8,24},{12,28},{16,0},{20,4},{24,8},{28,12},{1,17},{... | collective-permute-start | bytes 589832 | tf_op jit(solution)/shard_map/ppermute | solution.py:29
  15.2 10.2 %collective-permute-start.4 = (bf16[192,512]{1,0:T(8,128)(2,1)S(1)}, bf16[192,512]{1,0:T(8,128)(2,1)S(1)}, u32[]{:S(2)}, u32[]{:S(2)}) collective-permute-start(bf16[192,512]{1,0:T(8,128)(2,1)S(1)} %get-tuple-element.38.refs_3_), channel_id=1, source_target_pairs={{0,8},{4,12},{8,0},{12,4},{16,24},{20,28},{24,16},{28,20},{1,9},{5... | collective-permute-start | bytes 589832 | tf_op jit(solution)/shard_map/ppermute | solution.py:29
  15.8 6.1 %collective-permute-start.2 = (bf16[32,1024]{1,0:T(8,128)(2,1)S(1)}, bf16[32,1024]{1,0:T(8,128)(2,1)S(1)}, u32[]{:S(2)}, u32[]{:S(2)}) collective-permute-start(bf16[32,1024]{1,0:T(8,128)(2,1)S(1)} %get-tuple-element.35), channel_id=1, source_target_pairs={{0,3},{1,2},{2,1},{3,0},{4,7},{5,6},{6,5},{7,4},{8,11},{9,10},{10,... | collective-permute-start | bytes 196616 | tf_op jit(solution)/shard_map/ppermute | solution.py:29
  18.7 6.8 %collective-permute-start.3 = (bf16[192,512]{1,0:T(8,128)(2,1)S(1)}, bf16[192,512]{1,0:T(8,128)(2,1)S(1)}, u32[]{:S(2)}, u32[]{:S(2)}) collective-permute-start(bf16[192,512]{1,0:T(8,128)(2,1)S(1)} %get-tuple-element.38.refs_3_), channel_id=1, source_target_pairs={{0,4},{4,0},{8,12},{12,8},{16,20},{20,16},{24,28},{28,24},{1,5},{5... | collective-permute-start | bytes 589832 | tf_op jit(solution)/shard_map/ppermute | solution.py:29
  21.9 7.5 %collective-permute-start.15 = (bf16[192,512]{1,0:T(8,128)(2,1)S(1)}, bf16[192,512]{1,0:T(8,128)(2,1)S(1)}, u32[]{:S(2)}, u32[]{:S(2)}) collective-permute-start(bf16[192,512]{1,0:T(8,128)(2,1)S(1)} %get-tuple-element.39.refs_11_), channel_id=1, source_target_pairs={{0,24},{4,28},{8,16},{12,20},{16,8},{20,12},{24,0},{28,4},{1,25},{... | collective-permute-start | bytes 589832 | tf_op jit(solution)/shard_map/ppermute | solution.py:29
  24.2 8.7 %collective-permute-start.13 = (bf16[192,512]{1,0:T(8,128)(2,1)S(1)}, bf16[192,512]{1,0:T(8,128)(2,1)S(1)}, u32[]{:S(2)}, u32[]{:S(2)}) collective-permute-start(bf16[192,512]{1,0:T(8,128)(2,1)S(1)} %get-tuple-element.39.refs_11_), channel_id=1, source_target_pairs={{0,16},{4,20},{8,24},{12,28},{16,0},{20,4},{24,8},{28,12},{1,17},{... | collective-permute-start | bytes 589832 | tf_op jit(solution)/shard_map/ppermute | solution.py:29
  24.7 8.2 %collective-permute-start.11 = (bf16[192,512]{1,0:T(8,128)(2,1)S(1)}, bf16[192,512]{1,0:T(8,128)(2,1)S(1)}, u32[]{:S(2)}, u32[]{:S(2)}) collective-permute-start(bf16[192,512]{1,0:T(8,128)(2,1)S(1)} %get-tuple-element.39.refs_11_), channel_id=1, source_target_pairs={{0,8},{4,12},{8,0},{12,4},{16,24},{20,28},{24,16},{28,20},{1,9},{5... | collective-permute-start | bytes 589832 | tf_op jit(solution)/shard_map/ppermute | solution.py:29
  25.4 8.0 %collective-permute-start.10 = (bf16[192,512]{1,0:T(8,128)(2,1)S(1)}, bf16[192,512]{1,0:T(8,128)(2,1)S(1)}, u32[]{:S(2)}, u32[]{:S(2)}) collective-permute-start(bf16[192,512]{1,0:T(8,128)(2,1)S(1)} %get-tuple-element.39.refs_11_), channel_id=1, source_target_pairs={{0,4},{4,0},{8,12},{12,8},{16,20},{20,16},{24,28},{28,24},{1,5},{5... | collective-permute-start | bytes 589832 | tf_op jit(solution)/shard_map/ppermute | solution.py:29
  25.5 9.1 %collective-permute-start.20 = (bf16[64,1280]{1,0:T(8,128)(2,1)S(1)}, bf16[64,1280]{1,0:T(8,128)(2,1)S(1)}, u32[]{:S(2)}, u32[]{:S(2)}) collective-permute-start(bf16[64,1280]{1,0:T(8,128)(2,1)S(1)} %get-tuple-element.47), channel_id=1, source_target_pairs={{0,8},{4,12},{8,0},{12,4},{16,24},{20,28},{24,16},{28,20},{1,9},{5... | collective-permute-start | bytes 491528 | tf_op jit(solution)/shard_map/ppermute | solution.py:29
  29.4 5.5 %collective-permute-start.21 = (bf16[64,1280]{1,0:T(8,128)(2,1)S(1)}, bf16[64,1280]{1,0:T(8,128)(2,1)S(1)}, u32[]{:S(2)}, u32[]{:S(2)}) collective-permute-start(bf16[64,1280]{1,0:T(8,128)(2,1)S(1)} %get-tuple-element.48), channel_id=1, source_target_pairs={{0,16},{4,20},{8,24},{12,28},{16,0},{20,4},{24,8},{28,12},{1,17},{... | collective-permute-start | bytes 491528 | tf_op jit(solution)/shard_map/ppermute | solution.py:29
  32.9 2.2 %collective-permute-start.9 = (bf16[192,512]{1,0:T(8,128)(2,1)S(1)}, bf16[192,512]{1,0:T(8,128)(2,1)S(1)}, u32[]{:S(2)}, u32[]{:S(2)}) collective-permute-start(bf16[192,512]{1,0:T(8,128)(2,1)S(1)} %collective-permute-done.8.refs_9_), channel_id=1, source_target_pairs={{0,4},{4,0},{8,12},{12,8},{16,20},{20,16},{24,28},{28,24},{1,5},{5... | collective-permute-start | bytes 589832 | tf_op jit(solution)/shard_map/ppermute | solution.py:29
  32.9 2.5 %collective-permute-start.7 = (bf16[192,512]{1,0:T(8,128)(2,1)S(1)}, bf16[192,512]{1,0:T(8,128)(2,1)S(1)}, u32[]{:S(2)}, u32[]{:S(2)}) collective-permute-start(bf16[192,512]{1,0:T(8,128)(2,1)S(1)} %collective-permute-done.6.refs_7_), channel_id=1, source_target_pairs={{0,4},{4,0},{8,12},{12,8},{16,20},{20,16},{24,28},{28,24},{1,5},{5... | collective-permute-start | bytes 589832 | tf_op jit(solution)/shard_map/ppermute | solution.py:29
  33.4 4.2 %collective-permute-start.5 = (bf16[192,512]{1,0:T(8,128)(2,1)S(1)}, bf16[192,512]{1,0:T(8,128)(2,1)S(1)}, u32[]{:S(2)}, u32[]{:S(2)}) collective-permute-start(bf16[192,512]{1,0:T(8,128)(2,1)S(1)} %collective-permute-done.4.refs_5_), channel_id=1, source_target_pairs={{0,4},{4,0},{8,12},{12,8},{16,20},{20,16},{24,28},{28,24},{1,5},{5... | collective-permute-start | bytes 589832 | tf_op jit(solution)/shard_map/ppermute | solution.py:29
  34.6 3.0 %collective-permute-start.16 = (bf16[192,512]{1,0:T(8,128)(2,1)S(1)}, bf16[192,512]{1,0:T(8,128)(2,1)S(1)}, u32[]{:S(2)}, u32[]{:S(2)}) collective-permute-start(bf16[192,512]{1,0:T(8,128)(2,1)S(1)} %collective-permute-done.15.refs_17_), channel_id=1, source_target_pairs={{0,4},{4,0},{8,12},{12,8},{16,20},{20,16},{24,28},{28,24},{1,5},{5... | collective-permute-start | bytes 589832 | tf_op jit(solution)/shard_map/ppermute | solution.py:29
  34.9 3.2 %collective-permute-start.14 = (bf16[192,512]{1,0:T(8,128)(2,1)S(1)}, bf16[192,512]{1,0:T(8,128)(2,1)S(1)}, u32[]{:S(2)}, u32[]{:S(2)}) collective-permute-start(bf16[192,512]{1,0:T(8,128)(2,1)S(1)} %collective-permute-done.13.refs_15_), channel_id=1, source_target_pairs={{0,4},{4,0},{8,12},{12,8},{16,20},{20,16},{24,28},{28,24},{1,5},{5... | collective-permute-start | bytes 589832 | tf_op jit(solution)/shard_map/ppermute | solution.py:29
  35.2 3.1 %collective-permute-start.12 = (bf16[192,512]{1,0:T(8,128)(2,1)S(1)}, bf16[192,512]{1,0:T(8,128)(2,1)S(1)}, u32[]{:S(2)}, u32[]{:S(2)}) collective-permute-start(bf16[192,512]{1,0:T(8,128)(2,1)S(1)} %collective-permute-done.11.refs_13_), channel_id=1, source_target_pairs={{0,4},{4,0},{8,12},{12,8},{16,20},{20,16},{24,28},{28,24},{1,5},{5... | collective-permute-start | bytes 589832 | tf_op jit(solution)/shard_map/ppermute | solution.py:29
  35.4 7.3 %collective-permute-start.22 = (bf16[64,1280]{1,0:T(8,128)(2,1)S(1)}, bf16[64,1280]{1,0:T(8,128)(2,1)S(1)}, u32[]{:S(2)}, u32[]{:S(2)}) collective-permute-start(bf16[64,1280]{1,0:T(8,128)(2,1)S(1)} %get-tuple-element.49), channel_id=1, source_target_pairs={{0,24},{4,28},{8,16},{12,20},{16,8},{20,12},{24,0},{28,4},{1,25},{... | collective-permute-start | bytes 491528 | tf_op jit(solution)/shard_map/ppermute | solution.py:29
  37.6 6.0 %collective-permute-start.23 = (bf16[64,1280]{1,0:T(8,128)(2,1)S(1)}, bf16[64,1280]{1,0:T(8,128)(2,1)S(1)}, u32[]{:S(2)}, u32[]{:S(2)}) collective-permute-start(bf16[64,1280]{1,0:T(8,128)(2,1)S(1)} %get-tuple-element.46.refs_0_), channel_id=1, source_target_pairs={{0,4},{4,0},{8,12},{12,8},{16,20},{20,16},{24,28},{28,24},{1,5},{5... | collective-permute-start | bytes 491528 | tf_op jit(solution)/shard_map/ppermute | solution.py:29
  37.6 8.2 %collective-permute-start.24 = (bf16[64,1280]{1,0:T(8,128)(2,1)S(1)}, bf16[64,1280]{1,0:T(8,128)(2,1)S(1)}, u32[]{:S(2)}, u32[]{:S(2)}) collective-permute-start(bf16[64,1280]{1,0:T(8,128)(2,1)S(1)} %collective-permute-done.20.refs_1_), channel_id=1, source_target_pairs={{0,4},{4,0},{8,12},{12,8},{16,20},{20,16},{24,28},{28,24},{1,5},{5... | collective-permute-start | bytes 491528 | tf_op jit(solution)/shard_map/ppermute | solution.py:29
  38.1 7.7 %collective-permute-start.25 = (bf16[64,1280]{1,0:T(8,128)(2,1)S(1)}, bf16[64,1280]{1,0:T(8,128)(2,1)S(1)}, u32[]{:S(2)}, u32[]{:S(2)}) collective-permute-start(bf16[64,1280]{1,0:T(8,128)(2,1)S(1)} %collective-permute-done.21.refs_2_), channel_id=1, source_target_pairs={{0,4},{4,0},{8,12},{12,8},{16,20},{20,16},{24,28},{28,24},{1,5},{5... | collective-permute-start | bytes 491528 | tf_op jit(solution)/shard_map/ppermute | solution.py:29
  40.0 16.2 %collective-permute-start.27 = (bf16[80,1024]{1,0:T(8,128)(2,1)S(1)}, bf16[80,1024]{1,0:T(8,128)(2,1)S(1)}, u32[]{:S(2)}, u32[]{:S(2)}) collective-permute-start(bf16[80,1024]{1,0:T(8,128)(2,1)S(1)} %get-tuple-element.51), channel_id=1, source_target_pairs={{0,8},{4,12},{8,0},{12,4},{16,24},{20,28},{24,16},{28,20},{1,9},{5... | collective-permute-start | bytes 491528 | tf_op jit(solution)/shard_map/ppermute | solution.py:29
  42.7 14.1 %collective-permute-start.28 = (bf16[80,1024]{1,0:T(8,128)(2,1)S(1)}, bf16[80,1024]{1,0:T(8,128)(2,1)S(1)}, u32[]{:S(2)}, u32[]{:S(2)}) collective-permute-start(bf16[80,1024]{1,0:T(8,128)(2,1)S(1)} %get-tuple-element.52), channel_id=1, source_target_pairs={{0,16},{4,20},{8,24},{12,28},{16,0},{20,4},{24,8},{28,12},{1,17},{... | collective-permute-start | bytes 491528 | tf_op jit(solution)/shard_map/ppermute | solution.py:29
  43.6 13.2 %collective-permute-start.29 = (bf16[80,1024]{1,0:T(8,128)(2,1)S(1)}, bf16[80,1024]{1,0:T(8,128)(2,1)S(1)}, u32[]{:S(2)}, u32[]{:S(2)}) collective-permute-start(bf16[80,1024]{1,0:T(8,128)(2,1)S(1)} %get-tuple-element.53), channel_id=1, source_target_pairs={{0,24},{4,28},{8,16},{12,20},{16,8},{20,12},{24,0},{28,4},{1,25},{... | collective-permute-start | bytes 491528 | tf_op jit(solution)/shard_map/ppermute | solution.py:29
  45.9 4.3 %collective-permute-start.17 = (bf16[32,1024]{1,0:T(8,128)(2,1)S(1)}, bf16[32,1024]{1,0:T(8,128)(2,1)S(1)}, u32[]{:S(2)}, u32[]{:S(2)}) collective-permute-start(bf16[32,1024]{1,0:T(8,128)(2,1)S(1)} %get-tuple-element.41), channel_id=1, source_target_pairs={{0,1},{1,0},{2,3},{3,2},{4,5},{5,4},{6,7},{7,6},{8,9},{9,8},{10,11... | collective-permute-start | bytes 196616 | tf_op jit(solution)/shard_map/ppermute | solution.py:29
  45.9 5.9 %collective-permute-start.18 = (bf16[32,1024]{1,0:T(8,128)(2,1)S(1)}, bf16[32,1024]{1,0:T(8,128)(2,1)S(1)}, u32[]{:S(2)}, u32[]{:S(2)}) collective-permute-start(bf16[32,1024]{1,0:T(8,128)(2,1)S(1)} %get-tuple-element.42), channel_id=1, source_target_pairs={{0,2},{1,3},{2,0},{3,1},{4,6},{5,7},{6,4},{7,5},{8,10},{9,11},{10,... | collective-permute-start | bytes 196616 | tf_op jit(solution)/shard_map/ppermute | solution.py:29
  50.1 6.1 %collective-permute-start.19 = (bf16[32,1024]{1,0:T(8,128)(2,1)S(1)}, bf16[32,1024]{1,0:T(8,128)(2,1)S(1)}, u32[]{:S(2)}, u32[]{:S(2)}) collective-permute-start(bf16[32,1024]{1,0:T(8,128)(2,1)S(1)} %get-tuple-element.43), channel_id=1, source_target_pairs={{0,3},{1,2},{2,1},{3,0},{4,7},{5,6},{6,5},{7,4},{8,11},{9,10},{10,... | collective-permute-start | bytes 196616 | tf_op jit(solution)/shard_map/ppermute | solution.py:29
  51.8 7.3 %collective-permute-start.26 = (bf16[64,1280]{1,0:T(8,128)(2,1)S(1)}, bf16[64,1280]{1,0:T(8,128)(2,1)S(1)}, u32[]{:S(2)}, u32[]{:S(2)}) collective-permute-start(bf16[64,1280]{1,0:T(8,128)(2,1)S(1)} %collective-permute-done.22.refs_3_), channel_id=1, source_target_pairs={{0,4},{4,0},{8,12},{12,8},{16,20},{20,16},{24,28},{28,24},{1,5},{5... | collective-permute-start | bytes 491528 | tf_op jit(solution)/shard_map/ppermute | solution.py:29
  56.2 2.9 %collective-permute-start.30 = (bf16[80,1024]{1,0:T(8,128)(2,1)S(1)}, bf16[80,1024]{1,0:T(8,128)(2,1)S(1)}, u32[]{:S(2)}, u32[]{:S(2)}) collective-permute-start(bf16[80,1024]{1,0:T(8,128)(2,1)S(1)} %get-tuple-element.50.refs_8_), channel_id=1, source_target_pairs={{0,4},{4,0},{8,12},{12,8},{16,20},{20,16},{24,28},{28,24},{1,5},{5... | collective-permute-start | bytes 491528 | tf_op jit(solution)/shard_map/ppermute | solution.py:29
  56.2 2.9 %collective-permute-start.31 = (bf16[80,1024]{1,0:T(8,128)(2,1)S(1)}, bf16[80,1024]{1,0:T(8,128)(2,1)S(1)}, u32[]{:S(2)}, u32[]{:S(2)}) collective-permute-start(bf16[80,1024]{1,0:T(8,128)(2,1)S(1)} %collective-permute-done.27.refs_9_), channel_id=1, source_target_pairs={{0,4},{4,0},{8,12},{12,8},{16,20},{20,16},{24,28},{28,24},{1,5},{5... | collective-permute-start | bytes 491528 | tf_op jit(solution)/shard_map/ppermute | solution.py:29
  56.7 2.4 %collective-permute-start.32 = (bf16[80,1024]{1,0:T(8,128)(2,1)S(1)}, bf16[80,1024]{1,0:T(8,128)(2,1)S(1)}, u32[]{:S(2)}, u32[]{:S(2)}) collective-permute-start(bf16[80,1024]{1,0:T(8,128)(2,1)S(1)} %collective-permute-done.28.refs_10_), channel_id=1, source_target_pairs={{0,4},{4,0},{8,12},{12,8},{16,20},{20,16},{24,28},{28,24},{1,5},{5... | collective-permute-start | bytes 491528 | tf_op jit(solution)/shard_map/ppermute | solution.py:29
  56.8 2.3 %collective-permute-start.33 = (bf16[80,1024]{1,0:T(8,128)(2,1)S(1)}, bf16[80,1024]{1,0:T(8,128)(2,1)S(1)}, u32[]{:S(2)}, u32[]{:S(2)}) collective-permute-start(bf16[80,1024]{1,0:T(8,128)(2,1)S(1)} %collective-permute-done.29.refs_11_), channel_id=1, source_target_pairs={{0,4},{4,0},{8,12},{12,8},{16,20},{20,16},{24,28},{28,24},{1,5},{5... | collective-permute-start | bytes 491528 | tf_op jit(solution)/shard_map/ppermute | solution.py:29

commit v2 on v1

--- a/solution.py
+++ b/solution.py
@@ -29,18 +29,22 @@
     return lax.ppermute(value, axis, [(i, i ^ step) for i in range(size)])
 
 
+def after(values, *others):
+    return list(lax.optimization_barrier((*values, *others))[: len(values)])
+
+
 def shape(rows, columns, kind):
     return jax.ShapeDtypeStruct((rows, columns), kind)
 
 
-def call(body, out_shape, args, scratch=(), flops=0, moved=0):
+def call(body, out_shape, args, scratch=(), flops=0, moved=0, limit=16):
     return pl.pallas_call(
         body,
         out_shape=out_shape,
         in_specs=[VMEM] * len(args),
         out_specs=jax.tree.map(lambda _: VMEM, out_shape),
         scratch_shapes=list(scratch),
-        compiler_params=pltpu.CompilerParams(vmem_limit_bytes=40 << 20),
+        compiler_params=pltpu.CompilerParams(vmem_limit_bytes=limit << 20),
         cost_estimate=pl.CostEstimate(flops=flops, bytes_accessed=moved, transcendentals=0),
     )(*args)
 
@@ -54,26 +58,20 @@
     second_ref[rows:, :] = down_ref[0, :, half:]
 
 
-def take_rows(slots, chosen_ref, tokens_ref, cotangent_ref, *refs):
-    out_refs, x_ref, d_ref = refs[:-2], refs[-2], refs[-1]
-    picked = lax.broadcasted_iota(jnp.int32, (chosen_ref.shape[0], tokens_ref.shape[0]), 1)
-    one_hot = jnp.where(picked == chosen_ref[...], 1.0, 0.0).astype(BF16)
-    x_ref[...] = dot(one_hot, tokens_ref[...]).astype(BF16)
-    d_ref[...] = dot(one_hot, cotangent_ref[...]).astype(BF16)
+def join(x_ref, d_ref, sent_ref):
+    experts = sent_ref.shape[0]
+    slots = x_ref.shape[0] // experts
+    for e in range(experts):
+        sent_ref[e, :slots, :] = x_ref[e * slots : (e + 1) * slots, :]
+        sent_ref[e, slots:, :] = d_ref[e * slots : (e + 1) * slots, :]
+
+
+def prepare(slots, experts, chips, block, router_ref, *refs):
+    got_ref, x_ref, d_ref, *out_refs = refs
     me = lax.axis_index("expert")
-    for k, out_ref in enumerate(out_refs):
-        at = pl.ds(pl.multiple_of((me ^ k) * slots, slots), slots)
-        out_ref[:slots, :] = x_ref[at, :]
-        out_ref[slots:, :] = d_ref[at, :]
-
-
-def prepare(slots, experts, chips, block, router_ref, *refs):
-    got = refs[:experts]
-    x_ref, d_ref = refs[experts], refs[experts + 1]
-    out_refs = refs[experts + 2 :]
-    for k, ref in enumerate(got):
-        x_ref[k * slots : (k + 1) * slots, :] = ref[:slots, :]
-        d_ref[k * slots : (k + 1) * slots, :] = ref[slots:, :]
+    for k in range(experts):
+        x_ref[k * slots : (k + 1) * slots, :] = got_ref[me ^ k, :slots, :]
+        d_ref[k * slots : (k + 1) * slots, :] = got_ref[me ^ k, slots:, :]
     gate_val = gate_of(x_ref, router_ref)
     back = (gate_val * d_ref[...].astype(F32)).astype(BF16)
     width = back.shape[1]
@@ -97,7 +95,8 @@
     firsts = refs[3 : 3 + devices]
     seconds = refs[3 + devices : 3 + 2 * devices]
     outs = refs[3 + 2 * devices :]
-    return_refs, late_refs = outs[:experts], outs[experts : experts + chips]
+    return_refs = outs[:experts]
+    late_refs = outs[experts : experts + chips]
     gate_w, up_w, down_w, hidden_ref = outs[experts + chips :]
     width = x_ref.shape[1]
     half = gate_w.shape[1]
@@ -137,6 +136,7 @@
     high = term.astype(BF16).astype(F32)
     low = term - high
     tall = x.shape[0]
+    tall = x.shape[0]
     mine = me // 2
     parts = width // block
     each = tall // parts
@@ -162,26 +162,36 @@
     parts = width // hidden_block
     each = tall // parts
     me = lax.axis_index("dp")
-    feats = jnp.concatenate([m[:, width:] for m in mids], axis=0)
-    backs = jnp.concatenate([m[:, :width] for m in mids], axis=0)
-    grads = jnp.concatenate([t[:tall, :] for t in lates], axis=0)
-    sum_ref[...] = dot_rows(feats, grads)
+    total = None
+    count = devices if devices * tall <= 1024 else chips
+    for c in range(devices // count):
+        mid = mids[c * count : (c + 1) * count]
+        late = lates[c * count : (c + 1) * count]
+        feats = jnp.concatenate([m[:, width:] for m in mid], axis=0)
+        backs = jnp.concatenate([m[:, :width] for m in mid], axis=0)
+        grads = jnp.concatenate([t[:tall, :] for t in late], axis=0)
+        term = dot_rows(feats, grads)
+        sum_ref[...] = term if c == 0 else sum_ref[...] + term
+        tails = [t[tall:, :].astype(F32) for t in late]
+        hidden = jnp.concatenate(
+            [
+                t[:each, i * hidden_block : (i + 1) * hidden_block]
+                for t in tails
+                for i in range(parts)
+            ],
+            axis=0,
+        ).astype(BF16)
+        term = dot_rows(hidden, backs)
+        down_sum_ref[...] = term if c == 0 else down_sum_ref[...] + term
+        for t in tails:
+            total = t if total is None else total + t
     rows = gate_ref.shape[1]
     at = pl.ds(pl.multiple_of((me * rows) % block, rows), rows)
     gate_ref[0] = sum_ref[at, :half] * scale
     up_ref[0] = sum_ref[at, half:] * scale
-    tails = [t[tall:, :].astype(F32) for t in lates]
-    hidden = jnp.concatenate(
-        [t[:each, i * hidden_block : (i + 1) * hidden_block] for t in tails for i in range(parts)],
-        axis=0,
-    ).astype(BF16)
-    down_sum_ref[...] = dot_rows(hidden, backs)
     rows = down_ref.shape[1]
     at = pl.ds(pl.multiple_of((me * rows) % hidden_block, rows), rows)
     down_ref[0] = down_sum_ref[at, :] * scale
-    total = tails[0]
-    for t in tails[1:]:
-        total = total + t
     router_ref[...] = (total[each : each + 1, :] + total[each + 1 : each + 2, :]) * scale
 
 
@@ -192,10 +202,12 @@
         at = pl.ds(pl.multiple_of((me ^ k) * slots, slots), slots)
         out_ref[at, :] = ref[:slots, :]
         back_ref[at, :] = ref[slots:, :]
-    picked = lax.broadcasted_iota(jnp.int32, (chosen_ref.shape[0], mixed_ref.shape[0]), 1)
-    one_hot = jnp.where(picked == chosen_ref[...], 1.0, 0.0).astype(BF16)
-    mixed_ref[...] = dot_rows(one_hot, out_ref[...]).astype(BF16)
-    grad_ref[...] = dot_rows(one_hot, back_ref[...]).astype(BF16)
+    chosen = chosen_ref[...]
+    line = jnp.concatenate([chosen[e : e + 1, :] for e in range(len(got))], axis=1)
+    picked = lax.broadcasted_iota(jnp.int32, (mixed_ref.shape[0], line.shape[1]), 0)
+    one_hot = jnp.where(picked == line, 1.0, 0.0).astype(BF16)
+    mixed_ref[...] = dot(one_hot, out_ref[...]).astype(BF16)
+    grad_ref[...] = dot(one_hot, back_ref[...]).astype(BF16)
 
 
 def local(tokens, selections, router, w_gate, w_up, w_down, cotangent):
@@ -209,33 +221,44 @@
     down_rows = w_down.shape[1]
     block = max(128, 2 * rows)
     hidden_block = max(128, 2 * down_rows)
-    chosen = selections.reshape(taken, 1)
-
+
+    flat = selections.reshape(taken)
+    x_sent = tokens.at[flat].get(mode="promise_in_bounds")
+    d_sent = cotangent.at[flat].get(mode="promise_in_bounds")
+    held_weights = lax.optimization_barrier((w_gate, w_up, w_down, x_sent, d_sent))
+    x_sent, d_sent = held_weights[3:]
     piece = shape(rows + down_rows, half, BF16)
-    first, second = call(pack_weights, (piece, piece), (w_gate, w_up, w_down))
+    first, second = call(pack_weights, (piece, piece), held_weights[:3])
     firsts, seconds = [None] * devices, [None] * devices
     firsts[0], seconds[0] = first, second
-    for k in range(1, chips):
-        firsts[2 * k] = swap(first, "dp", 2 * k)
-        seconds[2 * k] = swap(second, "dp", 2 * k)
+    if chips == 4:
+        firsts[2] = swap(first, "dp", 2)
+        seconds[4] = swap(second, "dp", 4)
+        firsts[4] = swap(first, "dp", 4)
+        seconds[2] = swap(second, "dp", 2)
+        firsts[6] = swap(firsts[2], "dp", 4)
+        seconds[6] = swap(seconds[4], "dp", 2)
+    else:
+        for k in range(1, chips):
+            firsts[2 * k] = swap(first, "dp", 2 * k)
+            seconds[2 * k] = swap(second, "dp", 2 * k)
     for k in range(chips):
         firsts[2 * k + 1] = swap(firsts[2 * k], "dp", 1)
         seconds[2 * k + 1] = swap(seconds[2 * k], "dp", 1)
 
     sent = call(
-        functools.partial(take_rows, slots),
-        (shape(2 * slots, width, BF16),) * experts,
-        (chosen, tokens, cotangent),
-        [pltpu.VMEM((taken, width), BF16)] * 2,
-    )
-    got = [sent[0]] + [swap(sent[k], "expert", k) for k in range(1, experts)]
+        join,
+        jax.ShapeDtypeStruct((experts, 2 * slots, width), BF16),
+        (x_sent, d_sent),
+    )
+    got = [lax.all_to_all(sent, "expert", 0, 0, tiled=True)]
+    got = after(got, firsts[3], firsts[5], firsts[6], seconds[3], seconds[5], seconds[6])
     x_rows, d_rows, *mids = call(
         functools.partial(prepare, slots, experts, chips, block),
         (shape(taken, width, BF16),) * 2 + (shape(taken, width + block, BF16),) * chips,
         (router, *got),
     )
     mids = [mids[0]] + [swap(mids[k], "dp", 2 * k) for k in range(1, chips)]
-    mids = mids + [swap(m, "dp", 1) for m in mids]
 
     lines = taken * hidden_block // width
     late_rows = taken + -(-(lines + 2) // 16) * 16
@@ -249,16 +272,20 @@
             pltpu.VMEM((half, width), BF16),
             pltpu.VMEM((taken, half), BF16),
         ],
-    )
-    returned, lates = outs[:experts], outs[experts:]
+        limit=16 if taken <= 64 else 40,
+    )
+    returned, lates = list(outs[:experts]), list(outs[experts:])
+    own_late = lates[0]
     returned = [returned[0]] + [swap(returned[k], "expert", k) for k in range(1, experts)]
     mixed, grad_tokens = call(
         functools.partial(combine, slots),
         (shape(held, width, BF16),) * 2,
-        (chosen, *returned),
+        (selections[0, 0], *returned),
         [pltpu.VMEM((taken, width), BF16)] * 2,
     )
     lates = [lates[0]] + [swap(lates[k], "dp", 2 * k) for k in range(1, chips)]
+    mids = after(mids, own_late)
+    mids = mids + [swap(m, "dp", 1) for m in mids]
     lates = lates + [swap(t, "dp", 1) for t in lates]
     grad_gate, grad_up, grad_down, grad_router = call(
         functools.partial(weight_grads, chips, block, hidden_block),
@@ -270,6 +297,7 @@
         ),
         (*mids, *lates),
         [pltpu.VMEM((block, 2 * half), F32), pltpu.VMEM((hidden_block, width), F32)],
+        limit=16 if taken <= 64 else 40,
     )
     return mixed, grad_tokens, grad_gate, grad_up, grad_down, grad_router
 

time: 60.8 us -> 51 us (0.84)
  waiting for transfers between devices: 18.8 us -> 9.92 us
  local copies, waits for them, and re-layouts: 5.24 us -> 2.95 us
  Pallas kernels: 5.75 us -> 7.13 us
    ppermute x34 -> x31, waiting for transfers between devices: 18.8 us -> 9.92 us  [swap(): return lax.ppermute(value, axis, [(i, i ^ step) for i in range(size)])]
    ppermute x34 -> x31, starting transfers between devices: 30 us -> 24.5 us  [swap(): return lax.ppermute(value, axis, [(i, i ^ step) for i in range(size)])]
    all_to_all x0 -> x1, starting transfers between devices: none -> 5.43 us  [local(): got = [lax.all_to_all(sent, 'expert', 0, 0, tiled=True)]]
    unnamed x14, local copies, waits for them, and re-layouts: 5.16 us -> 0.62 us
    gather x0 -> x2, local copies, waits for them, and re-layouts: none -> 1.41 us  [the longest x1 0.71 us: local(): x_sent = tokens.at[flat].get(mode='promise_in_bounds')]
    pallas_call x6, Pallas kernels: 5.75 us -> 7.13 us  [call(): pl.pallas_call(body, out_shape=out_shape, in_specs=[VMEM] * len(args), ou...]
    reshape x1, local copies, waits for them, and re-layouts: 0.08 us -> 0.91 us  [local(): flat = selections.reshape(taken)]
  transfers between devices with their start and end apart: 34 -> 32, of which waited for: 9 -> 5; matrix products, arithmetic and copies ran while one was open for 0% -> 0% of each run, Pallas kernels for 7% -> 11%
where the time goes in v2:
time: 51 us; the launch traced here: 50.7 us
  starting transfers between devices  29.9 us (59%)
  waiting for transfers between devices  9.92 us (19%)
  Pallas kernels  7.13 us (14%)
  local copies, waits for them, and re-layouts  2.95 us (6%)
  between operations  0.77 us (2%)
    ppermute x31, starting transfers between devices, swap(): return lax.ppermute(value, axis, [(i, i ^ step) for i in range(size)])  24.5 us
    ppermute x31, waiting for transfers between devices, swap(): return lax.ppermute(value, axis, [(i, i ^ step) for i in range(size)])  9.92 us
    pallas_call x6, Pallas kernels, call(): pl.pallas_call(body, out_shape=out_shape, in_specs=[VMEM] * len(args), ou...  7.13 us
    all_to_all x1, starting transfers between devices, local(): got = [lax.all_to_all(sent, 'expert', 0, 0, tiled=True)]  5.43 us
  transfers between devices with their start and end apart: 32, of which 5 were waited for; matrix products, arithmetic and copies ran while one was open for 0% of the time, Pallas kernels for 11%

profile of v2, /device:TPU:0, one launch (start us, length us, event | category | flops | bytes accessed | tf_op | source)
XLA Modules:
  0.0 50.7 jit_solution(151779569463699832)
XLA Ops:
  0.6 0.0 copy-start
  0.7 0.9 %reshape.43 = s32[64,1]{0,1:T(1,128)S(1)} reshape(s32[1,1,4,16]{3,2,1,0:T(4,128)} %param.8) | data formatting | bytes 512 | tf_op jit(solution)/shard_map/reshape | solution.py:225
  1.6 0.3 copy-done
  1.9 0.7 %gather_fusion.1 = bf16[64,1024]{1,0:T(8,128)(2,1)S(1)} fusion(bf16[512,1024]{1,0:T(8,128)(2,1)S(1)} %copy-done, s32[1024]{0:T(1024)S(1)} %pad_clamp_fusion), kind=kCustom, calls=%fused_computation.1 | custom fusion | bytes 262400 | tf_op jit(solution)/shard_map/gather | solution.py:227
  2.6 0.0 copy-start.1
  2.6 0.0 copy-start.2
  2.6 0.0 copy-start.3
  2.6 0.7 %gather_fusion = bf16[64,1024]{1,0:T(8,128)(2,1)S(1)} fusion(bf16[512,1024]{1,0:T(8,128)(2,1)S(1)} %copy-done.6, s32[1024]{0:T(1024)S(1)} %pad_clamp_fusion), kind=kCustom, calls=%fused_computation | custom fusion | bytes 262400 | tf_op jit(solution)/shard_map/gather | solution.py:226
  3.3 0.2 copy-done.1
  3.5 0.1 copy-done.2
  3.6 0.1 copy-done.3
  3.7 3.0 %collective-permute-start.2 = (bf16[192,512]{1,0:T(8,128)(2,1)S(1)}, bf16[192,512]{1,0:T(8,128)(2,1)S(1)}, u32[]{:S(2)}, u32[]{:S(2)}) collective-permute-start(bf16[192,512]{1,0:T(8,128)(2,1)S(1)} %get-tuple-element.43.refs_3_), channel_id=1, source_target_pairs={{0,16},{4,20},{8,24},{12,28},{16,0},{20,4},{24,8},{28,12},{1,17},{... | collective-permute-start | bytes 589832 | tf_op jit(solution)/shard_map/ppermute | solution.py:29
  6.7 1.5 %collective-permute-start = (bf16[192,512]{1,0:T(8,128)(2,1)S(1)}, bf16[192,512]{1,0:T(8,128)(2,1)S(1)}, u32[]{:S(2)}, u32[]{:S(2)}) collective-permute-start(bf16[192,512]{1,0:T(8,128)(2,1)S(1)} %get-tuple-element.43.refs_3_), channel_id=1, source_target_pairs={{0,8},{4,12},{8,0},{12,4},{16,24},{20,28},{24,16},{28,20},{1,9},{5... | collective-permute-start | bytes 589832 | tf_op jit(solution)/shard_map/ppermute | solution.py:29
  8.2 0.5 collective-permute-start.7
  8.7 0.1 collective-permute-start.5
  8.8 0.7 %shard_map.118 = bf16[4,32,1024]{2,1,0:T(8,128)(2,1)} custom-call(bf16[64,1024]{1,0:T(8,128)(2,1)S(1)} %gather_fusion, bf16[64,1024]{1,0:T(8,128)(2,1)S(1)} %gather_fusion.1), custom_call_target="tpu_custom_call" | custom-call | tf_op jit(solution)/shard_map/pallas_call | solution.py:41
  9.5 5.4 %all-to-all-start = ((bf16[4,32,1024]{2,1,0:T(8,128)(2,1)}), bf16[4,32,1024]{2,1,0:T(8,128)(2,1)S(1)}, u32[]{:S(2)}, u32[]{:S(2)}) async-start(bf16[4,32,1024]{2,1,0:T(8,128)(2,1)} %shard_map.118), calls=%async_computation | async-start | bytes 524288 | tf_op jit(solution)/shard_map/all_to_all | solution.py:254
  15.0 0.0 collective-permute-done.refs_5_
  15.0 1.6 %collective-permute-start.4 = (bf16[192,512]{1,0:T(8,128)(2,1)S(1)}, bf16[192,512]{1,0:T(8,128)(2,1)S(1)}, u32[]{:S(2)}, u32[]{:S(2)}) collective-permute-start(bf16[192,512]{1,0:T(8,128)(2,1)S(1)} %collective-permute-done.refs_5_), channel_id=1, source_target_pairs={{0,16},{4,20},{8,24},{12,28},{16,0},{20,4},{24,8},{28,12},{1,17},{... | collective-permute-start | bytes 589832 | tf_op jit(solution)/shard_map/ppermute | solution.py:29
  16.6 0.2 collective-permute-start.1
  16.7 0.0 collective-permute-done.7.refs_15_
  16.7 1.5 %collective-permute-start.9 = (bf16[192,512]{1,0:T(8,128)(2,1)S(1)}, bf16[192,512]{1,0:T(8,128)(2,1)S(1)}, u32[]{:S(2)}, u32[]{:S(2)}) collective-permute-start(bf16[192,512]{1,0:T(8,128)(2,1)S(1)} %collective-permute-done.7.refs_15_), channel_id=1, source_target_pairs={{0,8},{4,12},{8,0},{12,4},{16,24},{20,28},{24,16},{28,20},{1,9},{5... | collective-permute-start | bytes 589832 | tf_op jit(solution)/shard_map/ppermute | solution.py:29
  18.2 0.1 collective-permute-start.8
  18.3 0.4 collective-permute-start.6
  18.7 3.6 %collective-permute-done.4.refs_9_ = bf16[192,512]{1,0:T(8,128)(2,1)S(1)} collective-permute-done((bf16[192,512]{1,0:T(8,128)(2,1)S(1)}, bf16[192,512]{1,0:T(8,128)(2,1)S(1)}, u32[]{:S(2)}, u32[]{:S(2)}) %collective-permute-start.4) | collective-permute-done | bytes 196640 | tf_op jit(solution)/shard_map/ppermute | solution.py:29
  22.3 0.0 collective-permute-start.10
  22.3 0.0 collective-permute-done.1.refs_6_
  22.3 0.5 %collective-permute-start.12 = (bf16[192,512]{1,0:T(8,128)(2,1)S(1)}, bf16[192,512]{1,0:T(8,128)(2,1)}, u32[]{:S(2)}, u32[]{:S(2)}) collective-permute-start(bf16[192,512]{1,0:T(8,128)(2,1)S(1)} %get-tuple-element.44.refs_11_), channel_id=1, source_target_pairs={{0,4},{4,0},{8,12},{12,8},{16,20},{20,16},{24,28},{28,24},{1,5},{5... | collective-permute-start | bytes 589832 | tf_op jit(solution)/shard_map/ppermute | solution.py:29
  22.8 1.1 %collective-permute-done.9.refs_17_ = bf16[192,512]{1,0:T(8,128)(2,1)S(1)} collective-permute-done((bf16[192,512]{1,0:T(8,128)(2,1)S(1)}, bf16[192,512]{1,0:T(8,128)(2,1)S(1)}, u32[]{:S(2)}, u32[]{:S(2)}) %collective-permute-start.9) | collective-permute-done | bytes 196640 | tf_op jit(solution)/shard_map/ppermute | solution.py:29
  23.9 0.0 collective-permute-done.8.refs_16_
  23.9 0.5 %collective-permute-start.13 = (bf16[192,512]{1,0:T(8,128)(2,1)S(1)}, bf16[192,512]{1,0:T(8,128)(2,1)}, u32[]{:S(2)}, u32[]{:S(2)}) collective-permute-start(bf16[192,512]{1,0:T(8,128)(2,1)S(1)} %collective-permute-done.9.refs_17_), channel_id=1, source_target_pairs={{0,4},{4,0},{8,12},{12,8},{16,20},{20,16},{24,28},{28,24},{1,5},{5... | collective-permute-start | bytes 589832 | tf_op jit(solution)/shard_map/ppermute | solution.py:29
  24.4 0.0 all-to-all-done.refs_0_
  24.4 0.0 collective-permute-done.6.refs_14_
  24.4 0.1 shard_map.120
  24.6 1.6 %collective-permute-start.17 = (bf16[64,1280]{1,0:T(8,128)(2,1)S(1)}, bf16[64,1280]{1,0:T(8,128)(2,1)S(1)}, u32[]{:S(2)}, u32[]{:S(2)}) collective-permute-start(bf16[64,1280]{1,0:T(8,128)(2,1)S(1)} %get-tuple-element.55), channel_id=1, source_target_pairs={{0,8},{4,12},{8,0},{12,4},{16,24},{20,28},{24,16},{28,20},{1,9},{5... | collective-permute-start | bytes 491528 | tf_op jit(solution)/shard_map/ppermute | solution.py:29
  26.1 0.0 collective-permute-done.10.refs_4_
  26.1 0.5 collective-permute-start.18
  26.6 0.0 collective-permute-done.12.refs_12_
  26.6 1.5 %collective-permute-start.19 = (bf16[64,1280]{1,0:T(8,128)(2,1)S(1)}, bf16[64,1280]{1,0:T(8,128)(2,1)S(1)}, u32[]{:S(2)}, u32[]{:S(2)}) collective-permute-start(bf16[64,1280]{1,0:T(8,128)(2,1)S(1)} %get-tuple-element.57), channel_id=1, source_target_pairs={{0,24},{4,28},{8,16},{12,20},{16,8},{20,12},{24,0},{28,4},{1,25},{... | collective-permute-start | bytes 491528 | tf_op jit(solution)/shard_map/ppermute | solution.py:29
  28.1 0.0 collective-permute-done.11.refs_10_
  28.1 0.0 collective-permute-done.13.refs_18_
  28.1 3.1 %shard_map.121 = (bf16[32,1024]{1,0:T(8,128)(2,1)S(1)}, bf16[32,1024]{1,0:T(8,128)(2,1)S(1)}, bf16[32,1024]{1,0:T(8,128)(2,1)S(1)}, bf16[32,1024]{1,0:T(8,128)(2...) custom-call(bf16[64,1024]{1,0:T(8,128)(2,1)S(1)} %get-tuple-element., ...), custom_call_target="tpu_custom_call" | custom-call | tf_op jit(solution)/shard_map/pallas_call | solution.py:41
  31.2 1.6 %collective-permute-start.24 = (bf16[80,1024]{1,0:T(8,128)(2,1)S(1)}, bf16[80,1024]{1,0:T(8,128)(2,1)S(1)}, u32[]{:S(2)}, u32[]{:S(2)}) collective-permute-start(bf16[80,1024]{1,0:T(8,128)(2,1)S(1)} %get-tuple-element.63), channel_id=1, source_target_pairs={{0,8},{4,12},{8,0},{12,4},{16,24},{20,28},{24,16},{28,20},{1,9},{5... | collective-permute-start | bytes 491528 | tf_op jit(solution)/shard_map/ppermute | solution.py:29
  32.7 2.0 %collective-permute-start.14 = (bf16[32,1024]{1,0:T(8,128)(2,1)S(1)}, bf16[32,1024]{1,0:T(8,128)(2,1)S(1)}, u32[]{:S(2)}, u32[]{:S(2)}) collective-permute-start(bf16[32,1024]{1,0:T(8,128)(2,1)S(1)} %get-tuple-element.49), channel_id=1, source_target_pairs={{0,1},{1,0},{2,3},{3,2},{4,5},{5,4},{6,7},{7,6},{8,9},{9,8},{10,11... | collective-permute-start | bytes 196616 | tf_op jit(solution)/shard_map/ppermute | solution.py:29
  34.8 2.4 %collective-permute-start.15 = (bf16[32,1024]{1,0:T(8,128)(2,1)S(1)}, bf16[32,1024]{1,0:T(8,128)(2,1)S(1)}, u32[]{:S(2)}, u32[]{:S(2)}) collective-permute-start(bf16[32,1024]{1,0:T(8,128)(2,1)S(1)} %get-tuple-element.50), channel_id=1, source_target_pairs={{0,2},{1,3},{2,0},{3,1},{4,6},{5,7},{6,4},{7,5},{8,10},{9,11},{10,... | collective-permute-start | bytes 196616 | tf_op jit(solution)/shard_map/ppermute | solution.py:29
  37.1 0.0 collective-permute-done.18.refs_2_
  37.1 2.1 %collective-permute-start.16 = (bf16[32,1024]{1,0:T(8,128)(2,1)S(1)}, bf16[32,1024]{1,0:T(8,128)(2,1)S(1)}, u32[]{:S(2)}, u32[]{:S(2)}) collective-permute-start(bf16[32,1024]{1,0:T(8,128)(2,1)S(1)} %get-tuple-element.51), channel_id=1, source_target_pairs={{0,3},{1,2},{2,1},{3,0},{4,7},{5,6},{6,5},{7,4},{8,11},{9,10},{10,... | collective-permute-start | bytes 196616 | tf_op jit(solution)/shard_map/ppermute | solution.py:29
  39.3 0.0 collective-permute-start.25
  39.3 0.0 collective-permute-done.14.refs_1_
  39.3 0.0 copy-start.5
  39.3 1.3 %collective-permute-start.26 = (bf16[80,1024]{1,0:T(8,128)(2,1)S(1)}, bf16[80,1024]{1,0:T(8,128)(2,1)S(1)}, u32[]{:S(2)}, u32[]{:S(2)}) collective-permute-start(bf16[80,1024]{1,0:T(8,128)(2,1)S(1)} %get-tuple-element.65), channel_id=1, source_target_pairs={{0,24},{4,28},{8,16},{12,20},{16,8},{20,12},{24,0},{28,4},{1,25},{... | collective-permute-start | bytes 491528 | tf_op jit(solution)/shard_map/ppermute | solution.py:29
  40.6 0.7 %collective-permute-done.15.refs_2_ = bf16[32,1024]{1,0:T(8,128)(2,1)S(1)} collective-permute-done((bf16[32,1024]{1,0:T(8,128)(2,1)S(1)}, bf16[32,1024]{1,0:T(8,128)(2,1)S(1)}, u32[]{:S(2)}, u32[]{:S(2)}) %collective-permute-start.15) | collective-permute-done | bytes 65568 | tf_op jit(solution)/shard_map/ppermute | solution.py:29
  41.3 1.9 %collective-permute-done.16.refs_3_ = bf16[32,1024]{1,0:T(8,128)(2,1)S(1)} collective-permute-done((bf16[32,1024]{1,0:T(8,128)(2,1)S(1)}, bf16[32,1024]{1,0:T(8,128)(2,1)S(1)}, u32[]{:S(2)}, u32[]{:S(2)}) %collective-permute-start.16) | collective-permute-done | bytes 65568 | tf_op jit(solution)/shard_map/ppermute | solution.py:29
  43.2 0.0 collective-permute-start.20
  43.2 0.5 %collective-permute-start.21 = (bf16[64,1280]{1,0:T(8,128)(2,1)S(1)}, bf16[64,1280]{1,0:T(8,128)(2,1)S(1)}, u32[]{:S(2)}, u32[]{:S(2)}) collective-permute-start(bf16[64,1280]{1,0:T(8,128)(2,1)S(1)} %collective-permute-done.17.refs_1_), channel_id=1, source_target_pairs={{0,4},{4,0},{8,12},{12,8},{16,20},{20,16},{24,28},{28,24},{1,5},{5... | collective-permute-start | bytes 491528 | tf_op jit(solution)/shard_map/ppermute | solution.py:29
  43.7 2.6 %collective-permute-done.25.refs_10_ = bf16[80,1024]{1,0:T(8,128)(2,1)S(1)} collective-permute-done((bf16[80,1024]{1,0:T(8,128)(2,1)S(1)}, bf16[80,1024]{1,0:T(8,128)(2,1)S(1)}, u32[]{:S(2)}, u32[]{:S(2)}) %collective-permute-start.25) | collective-permute-done | bytes 163872 | tf_op jit(solution)/shard_map/ppermute | solution.py:29
  46.4 0.0 collective-permute-start.22
  46.4 0.5 %collective-permute-start.23 = (bf16[64,1280]{1,0:T(8,128)(2,1)S(1)}, bf16[64,1280]{1,0:T(8,128)(2,1)S(1)}, u32[]{:S(2)}, u32[]{:S(2)}) collective-permute-start(bf16[64,1280]{1,0:T(8,128)(2,1)S(1)} %collective-permute-done.19.refs_3_), channel_id=1, source_target_pairs={{0,4},{4,0},{8,12},{12,8},{16,20},{20,16},{24,28},{28,24},{1,5},{5... | collective-permute-start | bytes 491528 | tf_op jit(solution)/shard_map/ppermute | solution.py:29
  46.9 0.1 collective-permute-start.28
  46.9 0.0 collective-permute-done.20.refs_4_
  47.0 0.4 collective-permute-start.29
  47.4 0.1 collective-permute-start.30
  47.5 1.8 %shard_map.122 = (bf16[512,1024]{1,0:T(8,128)(2,1)}, bf16[512,1024]{1,0:T(8,128)(2,1)}) custom-call(s32[4,16]{1,0:T(4,128)S(1)} %bitcast.3, bf16[32,1024]{1,0:T(8,128)(2,1)S(1)} %get-tuple-element.48.refs_0_, bf16[32,1024]{1,0:T(8,128)(2,1)S(1)} %collective-permute-done.14.refs_1_, bf16[32,1024]{1,0:T(8,128)(2,1)S(1)} %collective-permute-done.15.refs_2_, ...), custom_call_target="tpu_custom_call" | custom-call | tf_op jit(solution)/shard_map/pallas_call | solution.py:41
  49.3 1.4 %shard_map.123 = (f32[1,128,512]{2,1,0:T(8,128)}, f32[1,128,512]{2,1,0:T(8,128)}, f32[1,64,1024]{2,1,0:T(8,128)}, f32[1,1024]{1,0:T(1,128)}) custom-call(bf16[64,1280]{1,0:T(8,128)(2,1)S(1)} %get-tuple-element.59.refs_0_, bf16[64,1280]{1,0:T(8,128)(2,1)S(1)} %collective-permute-done.17.refs_1_, bf16[64,1280]{1,0:T(8,128)(2,1)S(1)} %collective-permute-done.18.refs_2_, ...), custom_call_target="tpu_custom_call" | custom-call | tf_op jit(solution)/shard_map/pallas_call | solution.py:41
  (25 shorter events, 0.1 us)
Async XLA Ops:
  0.6 1.2 %copy-start = (bf16[512,1024]{1,0:T(8,128)(2,1)S(1)}, bf16[512,1024]{1,0:T(8,128)(2,1)}, u32[]{:S(2)}) copy-start(bf16[512,1024]{1,0:T(8,128)(2,1)} %param.13) | copy-start | bytes 3145732
  0.6 1.9 %copy-start.6 = (bf16[512,1024]{1,0:T(8,128)(2,1)S(1)}, bf16[512,1024]{1,0:T(8,128)(2,1)}, u32[]{:S(2)}) copy-start(bf16[512,1024]{1,0:T(8,128)(2,1)} %param.7) | copy-start | bytes 3145732
  2.6 0.9 %copy-start.1 = (bf16[1,128,512]{2,1,0:T(8,128)(2,1)S(1)}, bf16[1,128,512]{2,1,0:T(8,128)(2,1)}, u32[]{:S(2)}) copy-start(bf16[1,128,512]{2,1,0:T(8,128)(2,1)} %gate_ref) | copy-start | bytes 393220
  2.6 1.0 %copy-start.2 = (bf16[1,128,512]{2,1,0:T(8,128)(2,1)S(1)}, bf16[1,128,512]{2,1,0:T(8,128)(2,1)}, u32[]{:S(2)}) copy-start(bf16[1,128,512]{2,1,0:T(8,128)(2,1)} %up_ref) | copy-start | bytes 393220
  2.6 1.0 %copy-start.3 = (bf16[1,64,1024]{2,1,0:T(8,128)(2,1)S(1)}, bf16[1,64,1024]{2,1,0:T(8,128)(2,1)}, u32[]{:S(2)}) copy-start(bf16[1,64,1024]{2,1,0:T(8,128)(2,1)} %down_ref) | copy-start | bytes 393220
  3.7 11.3 %collective-permute-start.2 = (bf16[192,512]{1,0:T(8,128)(2,1)S(1)}, bf16[192,512]{1,0:T(8,128)(2,1)S(1)}, u32[]{:S(2)}, u32[]{:S(2)}) collective-permute-start(bf16[192,512]{1,0:T(8,128)(2,1)S(1)} %get-tuple-element.43.refs_3_), channel_id=1, source_target_pairs={{0,16},{4,20},{8,24},{12,28},{16,0},{20,4},{24,8},{28,12},{1,17},{... | collective-permute-start | bytes 589832 | tf_op jit(solution)/shard_map/ppermute | solution.py:29
  6.7 8.3 %collective-permute-start = (bf16[192,512]{1,0:T(8,128)(2,1)S(1)}, bf16[192,512]{1,0:T(8,128)(2,1)S(1)}, u32[]{:S(2)}, u32[]{:S(2)}) collective-permute-start(bf16[192,512]{1,0:T(8,128)(2,1)S(1)} %get-tuple-element.43.refs_3_), channel_id=1, source_target_pairs={{0,8},{4,12},{8,0},{12,4},{16,24},{20,28},{24,16},{28,20},{1,9},{5... | collective-permute-start | bytes 589832 | tf_op jit(solution)/shard_map/ppermute | solution.py:29
  8.2 8.5 %collective-permute-start.7 = (bf16[192,512]{1,0:T(8,128)(2,1)S(1)}, bf16[192,512]{1,0:T(8,128)(2,1)S(1)}, u32[]{:S(2)}, u32[]{:S(2)}) collective-permute-start(bf16[192,512]{1,0:T(8,128)(2,1)S(1)} %get-tuple-element.44.refs_11_), channel_id=1, source_target_pairs={{0,16},{4,20},{8,24},{12,28},{16,0},{20,4},{24,8},{28,12},{1,17},{... | collective-permute-start | bytes 589832 | tf_op jit(solution)/shard_map/ppermute | solution.py:29
  8.7 9.5 %collective-permute-start.5 = (bf16[192,512]{1,0:T(8,128)(2,1)S(1)}, bf16[192,512]{1,0:T(8,128)(2,1)S(1)}, u32[]{:S(2)}, u32[]{:S(2)}) collective-permute-start(bf16[192,512]{1,0:T(8,128)(2,1)S(1)} %get-tuple-element.44.refs_11_), channel_id=1, source_target_pairs={{0,8},{4,12},{8,0},{12,4},{16,24},{20,28},{24,16},{28,20},{1,9},{5... | collective-permute-start | bytes 589832 | tf_op jit(solution)/shard_map/ppermute | solution.py:29
  9.5 14.9 %copy-start.4 = (bf16[1,1024]{1,0:T(2,128)(2,1)S(1)}, bf16[1,1024]{1,0:T(2,128)(2,1)}, u32[]{:S(2)}) copy-start(bf16[1,1024]{1,0:T(2,128)(2,1)} %refs_2_.1) | copy-start | bytes 6148
  9.5 14.9 %all-to-all-start = ((bf16[4,32,1024]{2,1,0:T(8,128)(2,1)}), bf16[4,32,1024]{2,1,0:T(8,128)(2,1)S(1)}, u32[]{:S(2)}, u32[]{:S(2)}) async-start(bf16[4,32,1024]{2,1,0:T(8,128)(2,1)} %shard_map.118), calls=%async_computation | async-start | bytes 524288 | tf_op jit(solution)/shard_map/all_to_all | solution.py:254
  15.0 3.3 %collective-permute-start.3 = (bf16[192,512]{1,0:T(8,128)(2,1)S(1)}, bf16[192,512]{1,0:T(8,128)(2,1)S(1)}, u32[]{:S(2)}, u32[]{:S(2)}) collective-permute-start(bf16[192,512]{1,0:T(8,128)(2,1)S(1)} %collective-permute-done.2.refs_7_), channel_id=1, source_target_pairs={{0,4},{4,0},{8,12},{12,8},{16,20},{20,16},{24,28},{28,24},{1,5},{5... | collective-permute-start | bytes 589832 | tf_op jit(solution)/shard_map/ppermute | solution.py:29
  15.0 7.3 %collective-permute-start.4 = (bf16[192,512]{1,0:T(8,128)(2,1)S(1)}, bf16[192,512]{1,0:T(8,128)(2,1)S(1)}, u32[]{:S(2)}, u32[]{:S(2)}) collective-permute-start(bf16[192,512]{1,0:T(8,128)(2,1)S(1)} %collective-permute-done.refs_5_), channel_id=1, source_target_pairs={{0,16},{4,20},{8,24},{12,28},{16,0},{20,4},{24,8},{28,12},{1,17},{... | collective-permute-start | bytes 589832 | tf_op jit(solution)/shard_map/ppermute | solution.py:29
  16.6 5.7 %collective-permute-start.1 = (bf16[192,512]{1,0:T(8,128)(2,1)S(1)}, bf16[192,512]{1,0:T(8,128)(2,1)S(1)}, u32[]{:S(2)}, u32[]{:S(2)}) collective-permute-start(bf16[192,512]{1,0:T(8,128)(2,1)S(1)} %collective-permute-done.refs_5_), channel_id=1, source_target_pairs={{0,4},{4,0},{8,12},{12,8},{16,20},{20,16},{24,28},{28,24},{1,5},{5... | collective-permute-start | bytes 589832 | tf_op jit(solution)/shard_map/ppermute | solution.py:29
  16.7 7.2 %collective-permute-start.9 = (bf16[192,512]{1,0:T(8,128)(2,1)S(1)}, bf16[192,512]{1,0:T(8,128)(2,1)S(1)}, u32[]{:S(2)}, u32[]{:S(2)}) collective-permute-start(bf16[192,512]{1,0:T(8,128)(2,1)S(1)} %collective-permute-done.7.refs_15_), channel_id=1, source_target_pairs={{0,8},{4,12},{8,0},{12,4},{16,24},{20,28},{24,16},{28,20},{1,9},{5... | collective-permute-start | bytes 589832 | tf_op jit(solution)/shard_map/ppermute | solution.py:29
  18.2 5.7 %collective-permute-start.8 = (bf16[192,512]{1,0:T(8,128)(2,1)S(1)}, bf16[192,512]{1,0:T(8,128)(2,1)S(1)}, u32[]{:S(2)}, u32[]{:S(2)}) collective-permute-start(bf16[192,512]{1,0:T(8,128)(2,1)S(1)} %collective-permute-done.7.refs_15_), channel_id=1, source_target_pairs={{0,4},{4,0},{8,12},{12,8},{16,20},{20,16},{24,28},{28,24},{1,5},{5... | collective-permute-start | bytes 589832 | tf_op jit(solution)/shard_map/ppermute | solution.py:29
  18.3 6.1 %collective-permute-start.6 = (bf16[192,512]{1,0:T(8,128)(2,1)S(1)}, bf16[192,512]{1,0:T(8,128)(2,1)}, u32[]{:S(2)}, u32[]{:S(2)}) collective-permute-start(bf16[192,512]{1,0:T(8,128)(2,1)S(1)} %collective-permute-done.5.refs_13_), channel_id=1, source_target_pairs={{0,4},{4,0},{8,12},{12,8},{16,20},{20,16},{24,28},{28,24},{1,5},{5... | collective-permute-start | bytes 589832 | tf_op jit(solution)/shard_map/ppermute | solution.py:29
  22.3 3.8 %collective-permute-start.10 = (bf16[192,512]{1,0:T(8,128)(2,1)S(1)}, bf16[192,512]{1,0:T(8,128)(2,1)}, u32[]{:S(2)}, u32[]{:S(2)}) collective-permute-start(bf16[192,512]{1,0:T(8,128)(2,1)S(1)} %get-tuple-element.43.refs_3_), channel_id=1, source_target_pairs={{0,4},{4,0},{8,12},{12,8},{16,20},{20,16},{24,28},{28,24},{1,5},{5... | collective-permute-start | bytes 589832 | tf_op jit(solution)/shard_map/ppermute | solution.py:29
  22.3 4.3 %collective-permute-start.12 = (bf16[192,512]{1,0:T(8,128)(2,1)S(1)}, bf16[192,512]{1,0:T(8,128)(2,1)}, u32[]{:S(2)}, u32[]{:S(2)}) collective-permute-start(bf16[192,512]{1,0:T(8,128)(2,1)S(1)} %get-tuple-element.44.refs_11_), channel_id=1, source_target_pairs={{0,4},{4,0},{8,12},{12,8},{16,20},{20,16},{24,28},{28,24},{1,5},{5... | collective-permute-start | bytes 589832 | tf_op jit(solution)/shard_map/ppermute | solution.py:29
  23.9 4.2 %collective-permute-start.11 = (bf16[192,512]{1,0:T(8,128)(2,1)S(1)}, bf16[192,512]{1,0:T(8,128)(2,1)}, u32[]{:S(2)}, u32[]{:S(2)}) collective-permute-start(bf16[192,512]{1,0:T(8,128)(2,1)S(1)} %collective-permute-done.4.refs_9_), channel_id=1, source_target_pairs={{0,4},{4,0},{8,12},{12,8},{16,20},{20,16},{24,28},{28,24},{1,5},{5... | collective-permute-start | bytes 589832 | tf_op jit(solution)/shard_map/ppermute | solution.py:29
  23.9 4.2 %collective-permute-start.13 = (bf16[192,512]{1,0:T(8,128)(2,1)S(1)}, bf16[192,512]{1,0:T(8,128)(2,1)}, u32[]{:S(2)}, u32[]{:S(2)}) collective-permute-start(bf16[192,512]{1,0:T(8,128)(2,1)S(1)} %collective-permute-done.9.refs_17_), channel_id=1, source_target_pairs={{0,4},{4,0},{8,12},{12,8},{16,20},{20,16},{24,28},{28,24},{1,5},{5... | collective-permute-start | bytes 589832 | tf_op jit(solution)/shard_map/ppermute | solution.py:29
  24.6 10.2 %collective-permute-start.17 = (bf16[64,1280]{1,0:T(8,128)(2,1)S(1)}, bf16[64,1280]{1,0:T(8,128)(2,1)S(1)}, u32[]{:S(2)}, u32[]{:S(2)}) collective-permute-start(bf16[64,1280]{1,0:T(8,128)(2,1)S(1)} %get-tuple-element.55), channel_id=1, source_target_pairs={{0,8},{4,12},{8,0},{12,4},{16,24},{20,28},{24,16},{28,20},{1,9},{5... | collective-permute-start | bytes 491528 | tf_op jit(solution)/shard_map/ppermute | solution.py:29
  26.1 11.0 %collective-permute-start.18 = (bf16[64,1280]{1,0:T(8,128)(2,1)S(1)}, bf16[64,1280]{1,0:T(8,128)(2,1)S(1)}, u32[]{:S(2)}, u32[]{:S(2)}) collective-permute-start(bf16[64,1280]{1,0:T(8,128)(2,1)S(1)} %get-tuple-element.56), channel_id=1, source_target_pairs={{0,16},{4,20},{8,24},{12,28},{16,0},{20,4},{24,8},{28,12},{1,17},{... | collective-permute-start | bytes 491528 | tf_op jit(solution)/shard_map/ppermute | solution.py:29
  26.6 12.7 %collective-permute-start.19 = (bf16[64,1280]{1,0:T(8,128)(2,1)S(1)}, bf16[64,1280]{1,0:T(8,128)(2,1)S(1)}, u32[]{:S(2)}, u32[]{:S(2)}) collective-permute-start(bf16[64,1280]{1,0:T(8,128)(2,1)S(1)} %get-tuple-element.57), channel_id=1, source_target_pairs={{0,24},{4,28},{8,16},{12,20},{16,8},{20,12},{24,0},{28,4},{1,25},{... | collective-permute-start | bytes 491528 | tf_op jit(solution)/shard_map/ppermute | solution.py:29
  31.2 12.0 %collective-permute-start.24 = (bf16[80,1024]{1,0:T(8,128)(2,1)S(1)}, bf16[80,1024]{1,0:T(8,128)(2,1)S(1)}, u32[]{:S(2)}, u32[]{:S(2)}) collective-permute-start(bf16[80,1024]{1,0:T(8,128)(2,1)S(1)} %get-tuple-element.63), channel_id=1, source_target_pairs={{0,8},{4,12},{8,0},{12,4},{16,24},{20,28},{24,16},{28,20},{1,9},{5... | collective-permute-start | bytes 491528 | tf_op jit(solution)/shard_map/ppermute | solution.py:29
  32.7 6.5 %collective-permute-start.14 = (bf16[32,1024]{1,0:T(8,128)(2,1)S(1)}, bf16[32,1024]{1,0:T(8,128)(2,1)S(1)}, u32[]{:S(2)}, u32[]{:S(2)}) collective-permute-start(bf16[32,1024]{1,0:T(8,128)(2,1)S(1)} %get-tuple-element.49), channel_id=1, source_target_pairs={{0,1},{1,0},{2,3},{3,2},{4,5},{5,4},{6,7},{7,6},{8,9},{9,8},{10,11... | collective-permute-start | bytes 196616 | tf_op jit(solution)/shard_map/ppermute | solution.py:29
  34.8 6.6 %collective-permute-start.15 = (bf16[32,1024]{1,0:T(8,128)(2,1)S(1)}, bf16[32,1024]{1,0:T(8,128)(2,1)S(1)}, u32[]{:S(2)}, u32[]{:S(2)}) collective-permute-start(bf16[32,1024]{1,0:T(8,128)(2,1)S(1)} %get-tuple-element.50), channel_id=1, source_target_pairs={{0,2},{1,3},{2,0},{3,1},{4,6},{5,7},{6,4},{7,5},{8,10},{9,11},{10,... | collective-permute-start | bytes 196616 | tf_op jit(solution)/shard_map/ppermute | solution.py:29
  37.1 6.1 %collective-permute-start.16 = (bf16[32,1024]{1,0:T(8,128)(2,1)S(1)}, bf16[32,1024]{1,0:T(8,128)(2,1)S(1)}, u32[]{:S(2)}, u32[]{:S(2)}) collective-permute-start(bf16[32,1024]{1,0:T(8,128)(2,1)S(1)} %get-tuple-element.51), channel_id=1, source_target_pairs={{0,3},{1,2},{2,1},{3,0},{4,7},{5,6},{6,5},{7,4},{8,11},{9,10},{10,... | collective-permute-start | bytes 196616 | tf_op jit(solution)/shard_map/ppermute | solution.py:29
  39.3 7.1 %collective-permute-start.25 = (bf16[80,1024]{1,0:T(8,128)(2,1)S(1)}, bf16[80,1024]{1,0:T(8,128)(2,1)S(1)}, u32[]{:S(2)}, u32[]{:S(2)}) collective-permute-start(bf16[80,1024]{1,0:T(8,128)(2,1)S(1)} %get-tuple-element.64), channel_id=1, source_target_pairs={{0,16},{4,20},{8,24},{12,28},{16,0},{20,4},{24,8},{28,12},{1,17},{... | collective-permute-start | bytes 491528 | tf_op jit(solution)/shard_map/ppermute | solution.py:29
  39.3 8.2 %copy-start.5 = (s32[1,1,4,16]{3,2,1,0:T(4,128)S(1)}, s32[1,1,4,16]{3,2,1,0:T(4,128)}, u32[]{:S(2)}) copy-start(s32[1,1,4,16]{3,2,1,0:T(4,128)} %param.8) | copy-start | bytes 772
  39.3 7.1 %collective-permute-start.26 = (bf16[80,1024]{1,0:T(8,128)(2,1)S(1)}, bf16[80,1024]{1,0:T(8,128)(2,1)S(1)}, u32[]{:S(2)}, u32[]{:S(2)}) collective-permute-start(bf16[80,1024]{1,0:T(8,128)(2,1)S(1)} %get-tuple-element.65), channel_id=1, source_target_pairs={{0,24},{4,28},{8,16},{12,20},{16,8},{20,12},{24,0},{28,4},{1,25},{... | collective-permute-start | bytes 491528 | tf_op jit(solution)/shard_map/ppermute | solution.py:29
  41.3 5.5 %collective-permute-start.27 = (bf16[80,1024]{1,0:T(8,128)(2,1)S(1)}, bf16[80,1024]{1,0:T(8,128)(2,1)S(1)}, u32[]{:S(2)}, u32[]{:S(2)}) collective-permute-start(bf16[80,1024]{1,0:T(8,128)(2,1)S(1)} %get-tuple-element.58.refs_8_), channel_id=1, source_target_pairs={{0,4},{4,0},{8,12},{12,8},{16,20},{20,16},{24,28},{28,24},{1,5},{5... | collective-permute-start | bytes 491528 | tf_op jit(solution)/shard_map/ppermute | solution.py:29
  43.2 3.8 %collective-permute-start.20 = (bf16[64,1280]{1,0:T(8,128)(2,1)S(1)}, bf16[64,1280]{1,0:T(8,128)(2,1)S(1)}, u32[]{:S(2)}, u32[]{:S(2)}) collective-permute-start(bf16[64,1280]{1,0:T(8,128)(2,1)S(1)} %get-tuple-element.59.refs_0_), channel_id=1, source_target_pairs={{0,4},{4,0},{8,12},{12,8},{16,20},{20,16},{24,28},{28,24},{1,5},{5... | collective-permute-start | bytes 491528 | tf_op jit(solution)/shard_map/ppermute | solution.py:29
  43.2 4.2 %collective-permute-start.21 = (bf16[64,1280]{1,0:T(8,128)(2,1)S(1)}, bf16[64,1280]{1,0:T(8,128)(2,1)S(1)}, u32[]{:S(2)}, u32[]{:S(2)}) collective-permute-start(bf16[64,1280]{1,0:T(8,128)(2,1)S(1)} %collective-permute-done.17.refs_1_), channel_id=1, source_target_pairs={{0,4},{4,0},{8,12},{12,8},{16,20},{20,16},{24,28},{28,24},{1,5},{5... | collective-permute-start | bytes 491528 | tf_op jit(solution)/shard_map/ppermute | solution.py:29
  46.4 2.9 %collective-permute-start.22 = (bf16[64,1280]{1,0:T(8,128)(2,1)S(1)}, bf16[64,1280]{1,0:T(8,128)(2,1)S(1)}, u32[]{:S(2)}, u32[]{:S(2)}) collective-permute-start(bf16[64,1280]{1,0:T(8,128)(2,1)S(1)} %collective-permute-done.18.refs_2_), channel_id=1, source_target_pairs={{0,4},{4,0},{8,12},{12,8},{16,20},{20,16},{24,28},{28,24},{1,5},{5... | collective-permute-start | bytes 491528 | tf_op jit(solution)/shard_map/ppermute | solution.py:29
  46.4 2.9 %collective-permute-start.23 = (bf16[64,1280]{1,0:T(8,128)(2,1)S(1)}, bf16[64,1280]{1,0:T(8,128)(2,1)S(1)}, u32[]{:S(2)}, u32[]{:S(2)}) collective-permute-start(bf16[64,1280]{1,0:T(8,128)(2,1)S(1)} %collective-permute-done.19.refs_3_), channel_id=1, source_target_pairs={{0,4},{4,0},{8,12},{12,8},{16,20},{20,16},{24,28},{28,24},{1,5},{5... | collective-permute-start | bytes 491528 | tf_op jit(solution)/shard_map/ppermute | solution.py:29
  46.9 2.4 %collective-permute-start.28 = (bf16[80,1024]{1,0:T(8,128)(2,1)S(1)}, bf16[80,1024]{1,0:T(8,128)(2,1)S(1)}, u32[]{:S(2)}, u32[]{:S(2)}) collective-permute-start(bf16[80,1024]{1,0:T(8,128)(2,1)S(1)} %collective-permute-done.24.refs_9_), channel_id=1, source_target_pairs={{0,4},{4,0},{8,12},{12,8},{16,20},{20,16},{24,28},{28,24},{1,5},{5... | collective-permute-start | bytes 491528 | tf_op jit(solution)/shard_map/ppermute | solution.py:29
  47.0 2.3 %collective-permute-start.29 = (bf16[80,1024]{1,0:T(8,128)(2,1)S(1)}, bf16[80,1024]{1,0:T(8,128)(2,1)S(1)}, u32[]{:S(2)}, u32[]{:S(2)}) collective-permute-start(bf16[80,1024]{1,0:T(8,128)(2,1)S(1)} %collective-permute-done.25.refs_10_), channel_id=1, source_target_pairs={{0,4},{4,0},{8,12},{12,8},{16,20},{20,16},{24,28},{28,24},{1,5},{5... | collective-permute-start | bytes 491528 | tf_op jit(solution)/shard_map/ppermute | solution.py:29
  47.4 1.9 %collective-permute-start.30 = (bf16[80,1024]{1,0:T(8,128)(2,1)S(1)}, bf16[80,1024]{1,0:T(8,128)(2,1)S(1)}, u32[]{:S(2)}, u32[]{:S(2)}) collective-permute-start(bf16[80,1024]{1,0:T(8,128)(2,1)S(1)} %collective-permute-done.26.refs_11_), channel_id=1, source_target_pairs={{0,4},{4,0},{8,12},{12,8},{16,20},{20,16},{24,28},{28,24},{1,5},{5... | collective-permute-start | bytes 491528 | tf_op jit(solution)/shard_map/ppermute | solution.py:29

commit v3 on v2

--- a/solution.py
+++ b/solution.py
@@ -49,13 +49,11 @@
     )(*args)
 
 
-def pack_weights(gate_ref, up_ref, down_ref, first_ref, second_ref):
-    rows = gate_ref.shape[1]
-    half = gate_ref.shape[2]
-    first_ref[:rows, :] = gate_ref[0]
-    second_ref[:rows, :] = up_ref[0]
-    first_ref[rows:, :] = down_ref[0, :, :half]
-    second_ref[rows:, :] = down_ref[0, :, half:]
+def pack_weights(gate_ref, up_ref, down_ref, out_ref):
+    rows, half = gate_ref.shape[1:]
+    out_ref[:rows, :half] = gate_ref[0]
+    out_ref[:rows, half:] = up_ref[0]
+    out_ref[rows:, :] = down_ref[0]
 
 
 def join(x_ref, d_ref, sent_ref):
@@ -89,15 +87,13 @@
     return jax.nn.sigmoid(logit)
 
 
-def expert(slots, experts, chips, block, *refs):
+def hidden_part(slots, experts, chips, block, *refs):
     devices = 2 * chips
     x_ref, d_ref, router_ref = refs[:3]
-    firsts = refs[3 : 3 + devices]
-    seconds = refs[3 + devices : 3 + 2 * devices]
-    outs = refs[3 + 2 * devices :]
-    return_refs = outs[:experts]
-    late_refs = outs[experts : experts + chips]
-    gate_w, up_w, down_w, hidden_ref = outs[experts + chips :]
+    parts = refs[3 : 3 + devices]
+    outs = refs[3 + devices :]
+    late_refs = outs[:chips]
+    hidden_ref, logit_ref, gate_w, up_w, down_w = outs[chips:]
     width = x_ref.shape[1]
     half = gate_w.shape[1]
     rows = width // devices
@@ -105,11 +101,10 @@
     me = lax.axis_index("dp")
     for r in range(devices):
         at = pl.ds(pl.multiple_of((me ^ r) * rows, rows), rows)
-        gate_w[at, :] = firsts[r][:rows, :]
-        up_w[at, :] = seconds[r][:rows, :]
+        gate_w[at, :] = parts[r][:rows, :half]
+        up_w[at, :] = parts[r][:rows, half:]
         at = pl.ds(pl.multiple_of((me ^ r) * down_rows, down_rows), down_rows)
-        down_w[at, :half] = firsts[r][rows:, :]
-        down_w[at, half:] = seconds[r][rows:, :]
+        down_w[at, :] = parts[r][rows:, :]
     x = x_ref[...]
     d = d_ref[...]
     gate_val = gate_of(x_ref, router_ref)
@@ -125,13 +120,7 @@
     hidden_grad = gate_val * raw
     grad_gate = (hidden_grad * act_up * sigma * (1.0 + act_gate * (1.0 - sigma))).astype(BF16)
     grad_up = (hidden_grad * silu).astype(BF16)
-    projected = dot(hidden, down_w[...])
-    out_rows = (gate_val * projected).astype(BF16)
-    row_grads = dot_cols(grad_gate, gate_w[...]) + dot_cols(grad_up, up_w[...])
-    row_grads = (row_grads + logit_grad * router_ref[...].astype(F32)).astype(BF16)
-    for k, ref in enumerate(return_refs):
-        ref[:slots, :] = out_rows[k * slots : (k + 1) * slots, :]
-        ref[slots:, :] = row_grads[k * slots : (k + 1) * slots, :]
+    logit_ref[...] = jnp.broadcast_to(logit_grad, logit_ref.shape)
     term = jnp.sum(logit_grad * x.astype(F32), axis=0, keepdims=True)
     high = term.astype(BF16).astype(F32)
     low = term - high
@@ -149,6 +138,19 @@
         ref[:tall, :half] = grad_gate
         ref[:tall, half:] = grad_up
         ref[tall:, :] = jnp.concatenate([lines, high, low, empty], axis=0).astype(BF16)
+
+
+def row_part(slots, x_ref, router_ref, late_ref, hidden_ref, logit_ref, gate_w, up_w, down_w, *outs):
+    tall = x_ref.shape[0]
+    half = gate_w.shape[1]
+    gate_val = gate_of(x_ref, router_ref)
+    out_rows = (gate_val * dot(hidden_ref[...], down_w[...])).astype(BF16)
+    row_grads = dot_cols(late_ref[:tall, :half], gate_w[...])
+    row_grads = row_grads + dot_cols(late_ref[:tall, half:], up_w[...])
+    row_grads = (row_grads + logit_ref[:, :1] * router_ref[...].astype(F32)).astype(BF16)
+    for k, ref in enumerate(outs):
+        ref[:slots, :] = out_rows[k * slots : (k + 1) * slots, :]
+        ref[slots:, :] = row_grads[k * slots : (k + 1) * slots, :]
 
 
 def weight_grads(chips, block, hidden_block, *refs):
@@ -225,26 +227,15 @@
     flat = selections.reshape(taken)
     x_sent = tokens.at[flat].get(mode="promise_in_bounds")
     d_sent = cotangent.at[flat].get(mode="promise_in_bounds")
-    held_weights = lax.optimization_barrier((w_gate, w_up, w_down, x_sent, d_sent))
-    x_sent, d_sent = held_weights[3:]
-    piece = shape(rows + down_rows, half, BF16)
-    first, second = call(pack_weights, (piece, piece), held_weights[:3])
-    firsts, seconds = [None] * devices, [None] * devices
-    firsts[0], seconds[0] = first, second
-    if chips == 4:
-        firsts[2] = swap(first, "dp", 2)
-        seconds[4] = swap(second, "dp", 4)
-        firsts[4] = swap(first, "dp", 4)
-        seconds[2] = swap(second, "dp", 2)
-        firsts[6] = swap(firsts[2], "dp", 4)
-        seconds[6] = swap(seconds[4], "dp", 2)
-    else:
-        for k in range(1, chips):
-            firsts[2 * k] = swap(first, "dp", 2 * k)
-            seconds[2 * k] = swap(second, "dp", 2 * k)
+    held_weights = lax.optimization_barrier((w_gate, w_up, w_down, x_sent))
+    x_sent = held_weights[3]
+    held_part = call(pack_weights, shape(rows + down_rows, width, BF16), held_weights[:3])
+    parts = [None] * devices
+    parts[0] = held_part
+    for k in range(1, chips):
+        parts[2 * k] = swap(held_part, "dp", 2 * k)
     for k in range(chips):
-        firsts[2 * k + 1] = swap(firsts[2 * k], "dp", 1)
-        seconds[2 * k + 1] = swap(seconds[2 * k], "dp", 1)
+        parts[2 * k + 1] = swap(parts[2 * k], "dp", 1)
 
     sent = call(
         join,
@@ -252,7 +243,6 @@
         (x_sent, d_sent),
     )
     got = [lax.all_to_all(sent, "expert", 0, 0, tiled=True)]
-    got = after(got, firsts[3], firsts[5], firsts[6], seconds[3], seconds[5], seconds[6])
     x_rows, d_rows, *mids = call(
         functools.partial(prepare, slots, experts, chips, block),
         (shape(taken, width, BF16),) * 2 + (shape(taken, width + block, BF16),) * chips,
@@ -263,18 +253,25 @@
     lines = taken * hidden_block // width
     late_rows = taken + -(-(lines + 2) // 16) * 16
     outs = call(
-        functools.partial(expert, slots, experts, chips, hidden_block),
-        (shape(2 * slots, width, BF16),) * experts + (shape(late_rows, width, BF16),) * chips,
-        (x_rows, d_rows, router, *firsts, *seconds),
-        [
-            pltpu.VMEM((width, half), BF16),
-            pltpu.VMEM((width, half), BF16),
-            pltpu.VMEM((half, width), BF16),
-            pltpu.VMEM((taken, half), BF16),
-        ],
+        functools.partial(hidden_part, slots, experts, chips, hidden_block),
+        (shape(late_rows, width, BF16),) * chips
+        + (
+            shape(taken, half, BF16),
+            shape(taken, 128, F32),
+            shape(width, half, BF16),
+            shape(width, half, BF16),
+            shape(half, width, BF16),
+        ),
+        (x_rows, d_rows, router, *parts),
         limit=16 if taken <= 64 else 40,
     )
-    returned, lates = list(outs[:experts]), list(outs[experts:])
+    lates = list(outs[:chips])
+    returned = call(
+        functools.partial(row_part, slots),
+        (shape(2 * slots, width, BF16),) * experts,
+        (x_rows, router, lates[0], *outs[chips:]),
+        limit=16 if taken <= 64 else 40,
+    )
     own_late = lates[0]
     returned = [returned[0]] + [swap(returned[k], "expert", k) for k in range(1, experts)]
     mixed, grad_tokens = call(
@@ -284,9 +281,11 @@
         [pltpu.VMEM((taken, width), BF16)] * 2,
     )
     lates = [lates[0]] + [swap(lates[k], "dp", 2 * k) for k in range(1, chips)]
-    mids = after(mids, own_late)
+    mids = after(mids, returned[1])
     mids = mids + [swap(m, "dp", 1) for m in mids]
-    lates = lates + [swap(t, "dp", 1) for t in lates]
+    near = after(lates[:-1], *returned)
+    far = after(lates[-1:], mixed)
+    lates = lates + [swap(t, "dp", 1) for t in near + far]
     grad_gate, grad_up, grad_down, grad_router = call(
         functools.partial(weight_grads, chips, block, hidden_block),
         (

time: 51 us -> 50.5 us (level)
  starting transfers between devices: 29.9 us -> 24.1 us
  waiting for transfers between devices: 9.92 us -> 13.6 us
  local copies, waits for them, and re-layouts: 2.95 us -> 4.41 us
    ppermute x31 -> x24, starting transfers between devices: 24.5 us -> 18.7 us  [swap(): return lax.ppermute(value, axis, [(i, i ^ step) for i in range(size)])]
    ppermute x31 -> x24, waiting for transfers between devices: 9.92 us -> 13.6 us  [swap(): return lax.ppermute(value, axis, [(i, i ^ step) for i in range(size)])]
    gather x1, local copies, waits for them, and re-layouts: 0.71 us -> 2.15 us  [local(): d_sent = cotangent.at[flat].get(mode='promise_in_bounds')]
    pallas_call x6 -> x7, Pallas kernels: 7.13 us -> 7.33 us  [call(): pl.pallas_call(body, out_shape=out_shape, in_specs=[VMEM] * len(args), ou...]
  transfers between devices with their start and end apart: 32 -> 25, of which waited for: 5 -> 11; matrix products, arithmetic and copies ran while one was open for 0% -> 4% of each run, Pallas kernels for 11% -> 12%
where the time goes in v3:
time: 50.5 us; the launch traced here: 50.1 us
  starting transfers between devices  24.1 us (48%)
  waiting for transfers between devices  13.6 us (27%)
  Pallas kernels  7.33 us (15%)
  local copies, waits for them, and re-layouts  4.41 us (9%)
  between operations  0.7 us (1%)
    ppermute x24, starting transfers between devices, swap(): return lax.ppermute(value, axis, [(i, i ^ step) for i in range(size)])  18.7 us
    ppermute x24, waiting for transfers between devices, swap(): return lax.ppermute(value, axis, [(i, i ^ step) for i in range(size)])  13.6 us
    pallas_call x7, Pallas kernels, call(): pl.pallas_call(body, out_shape=out_shape, in_specs=[VMEM] * len(args), ou...  7.33 us
    all_to_all x1, starting transfers between devices, local(): got = [lax.all_to_all(sent, 'expert', 0, 0, tiled=True)]  5.4 us
    gather x1, local copies, waits for them, and re-layouts, local(): d_sent = cotangent.at[flat].get(mode='promise_in_bounds')  2.15 us
  transfers between devices with their start and end apart: 25, of which 11 were waited for; matrix products, arithmetic and copies ran while one was open for 4% of the time, Pallas kernels for 12%

profile of v3, /device:TPU:0, one launch (start us, length us, event | category | flops | bytes accessed | tf_op | source)
XLA Modules:
  0.0 50.1 jit_solution(9112731907453802290)
XLA Ops:
  0.6 0.0 copy-start
  0.6 0.9 %reshape.43 = s32[64,1]{0,1:T(1,128)S(1)} reshape(s32[1,1,4,16]{3,2,1,0:T(4,128)} %param.8) | data formatting | bytes 512 | tf_op jit(solution)/shard_map/reshape | solution.py:227
  1.5 0.4 copy-done
  1.9 0.7 %gather_fusion = bf16[64,1024]{1,0:T(8,128)(2,1)S(1)} fusion(bf16[512,1024]{1,0:T(8,128)(2,1)S(1)} %copy-done, s32[1024]{0:T(1024)S(1)} %pad_clamp_fusion), kind=kCustom, calls=%fused_computation | custom fusion | bytes 262400 | tf_op jit(solution)/shard_map/gather | solution.py:228
  2.6 0.2 copy-done.1
  2.8 0.1 copy-done.2
  2.8 0.1 copy-done.3
  2.9 4.0 %collective-permute-start.5 = (bf16[192,1024]{1,0:T(8,128)(2,1)S(1)}, bf16[192,1024]{1,0:T(8,128)(2,1)S(1)}, u32[]{:S(2)}, u32[]{:S(2)}) collective-permute-start(bf16[192,1024]{1,0:T(8,128)(2,1)S(1)} %shard_map.120.refs_3_), channel_id=1, source_target_pairs={{0,24},{4,28},{8,16},{12,20},{16,8},{20,12},{24,0},{28,4},{1,25},{... | collective-permute-start | bytes 1179656 | tf_op jit(solution)/shard_map/ppermute | solution.py:29
  6.9 0.5 %collective-permute-start.3 = (bf16[192,1024]{1,0:T(8,128)(2,1)S(1)}, bf16[192,1024]{1,0:T(8,128)(2,1)S(1)}, u32[]{:S(2)}, u32[]{:S(2)}) collective-permute-start(bf16[192,1024]{1,0:T(8,128)(2,1)S(1)} %shard_map.120.refs_3_), channel_id=1, source_target_pairs={{0,16},{4,20},{8,24},{12,28},{16,0},{20,4},{24,8},{28,12},{1,17},{... | collective-permute-start | bytes 1179656 | tf_op jit(solution)/shard_map/ppermute | solution.py:29
  7.4 0.1 collective-permute-start.1
  7.5 2.2 %gather_fusion.1 = bf16[64,1024]{1,0:T(8,128)(2,1)S(1)} fusion(bf16[512,1024]{1,0:T(8,128)(2,1)} %param.13, s32[1024]{0:T(1024)S(1)} %pad_clamp_fusion), kind=kCustom, calls=%fused_computation.1 | custom fusion | bytes 262400 | tf_op jit(solution)/shard_map/gather | solution.py:229
  9.7 0.7 %shard_map.118 = bf16[4,32,1024]{2,1,0:T(8,128)(2,1)} custom-call(bf16[64,1024]{1,0:T(8,128)(2,1)S(1)} %gather_fusion, bf16[64,1024]{1,0:T(8,128)(2,1)S(1)} %gather_fusion.1), custom_call_target="tpu_custom_call" | custom-call | tf_op jit(solution)/shard_map/pallas_call | solution.py:41
  10.4 5.4 %all-to-all-start = ((bf16[4,32,1024]{2,1,0:T(8,128)(2,1)}), bf16[4,32,1024]{2,1,0:T(8,128)(2,1)S(1)}, u32[]{:S(2)}, u32[]{:S(2)}) async-start(bf16[4,32,1024]{2,1,0:T(8,128)(2,1)} %shard_map.118), calls=%async_computation | async-start | bytes 524288 | tf_op jit(solution)/shard_map/all_to_all | solution.py:245
  15.8 0.0 collective-permute-start
  15.8 1.1 %collective-permute-done.5.refs_9_ = bf16[192,1024]{1,0:T(8,128)(2,1)S(1)} collective-permute-done((bf16[192,1024]{1,0:T(8,128)(2,1)S(1)}, bf16[192,1024]{1,0:T(8,128)(2,1)S(1)}, u32[]{:S(2)}, u32[]{:S(2)}) %collective-permute-start.5) | collective-permute-done | bytes 393248 | tf_op jit(solution)/shard_map/ppermute | solution.py:29
  16.9 0.0 collective-permute-start.6
  16.9 7.6 %collective-permute-done.3.refs_7_ = bf16[192,1024]{1,0:T(8,128)(2,1)S(1)} collective-permute-done((bf16[192,1024]{1,0:T(8,128)(2,1)S(1)}, bf16[192,1024]{1,0:T(8,128)(2,1)S(1)}, u32[]{:S(2)}, u32[]{:S(2)}) %collective-permute-start.3) | collective-permute-done | bytes 393248 | tf_op jit(solution)/shard_map/ppermute | solution.py:29
  24.4 0.0 collective-permute-start.4
  24.5 0.3 collective-permute-done.1.refs_5_
  24.7 0.2 collective-permute-start.2
  25.0 0.0 all-to-all-done.refs_0_
  25.0 0.1 shard_map.119
  25.1 1.7 %collective-permute-start.10 = (bf16[64,1280]{1,0:T(8,128)(2,1)S(1)}, bf16[64,1280]{1,0:T(8,128)(2,1)S(1)}, u32[]{:S(2)}, u32[]{:S(2)}) collective-permute-start(bf16[64,1280]{1,0:T(8,128)(2,1)S(1)} %get-tuple-element.62), channel_id=1, source_target_pairs={{0,8},{4,12},{8,0},{12,4},{16,24},{20,28},{24,16},{28,20},{1,9},{5... | collective-permute-start | bytes 491528 | tf_op jit(solution)/shard_map/ppermute | solution.py:29
  26.8 0.0 collective-permute-done.refs_4_
  26.9 0.7 %collective-permute-start.11 = (bf16[64,1280]{1,0:T(8,128)(2,1)S(1)}, bf16[64,1280]{1,0:T(8,128)(2,1)S(1)}, u32[]{:S(2)}, u32[]{:S(2)}) collective-permute-start(bf16[64,1280]{1,0:T(8,128)(2,1)S(1)} %get-tuple-element.63), channel_id=1, source_target_pairs={{0,16},{4,20},{8,24},{12,28},{16,0},{20,4},{24,8},{28,12},{1,17},{... | collective-permute-start | bytes 491528 | tf_op jit(solution)/shard_map/ppermute | solution.py:29
  27.6 0.0 collective-permute-done.6.refs_10_
  27.6 1.1 %collective-permute-start.12 = (bf16[64,1280]{1,0:T(8,128)(2,1)S(1)}, bf16[64,1280]{1,0:T(8,128)(2,1)S(1)}, u32[]{:S(2)}, u32[]{:S(2)}) collective-permute-start(bf16[64,1280]{1,0:T(8,128)(2,1)S(1)} %get-tuple-element.64), channel_id=1, source_target_pairs={{0,24},{4,28},{8,16},{12,20},{16,8},{20,12},{24,0},{28,4},{1,25},{... | collective-permute-start | bytes 491528 | tf_op jit(solution)/shard_map/ppermute | solution.py:29
  28.7 0.0 collective-permute-done.4.refs_8_
  28.7 0.0 collective-permute-done.2.refs_6_
  28.7 2.3 %shard_map.121 = (bf16[80,1024]{1,0:T(8,128)(2,1)S(1)}, bf16[80,1024]{1,0:T(8,128)(2,1)S(1)}, bf16[80,1024]{1,0:T(8,128)(2,1)S(1)}, bf16[80,1024]{1,0:T(8,128)(2...) custom-call(bf16[64,1024]{1,0:T(8,128)(2,1)S(1)} %get-tuple-element., ...), custom_call_target="tpu_custom_call" | custom-call | tf_op jit(solution)/shard_map/pallas_call | solution.py:41
  31.0 1.7 %collective-permute-start.17 = (bf16[80,1024]{1,0:T(8,128)(2,1)S(1)}, bf16[80,1024]{1,0:T(8,128)(2,1)S(1)}, u32[]{:S(2)}, u32[]{:S(2)}) collective-permute-start(bf16[80,1024]{1,0:T(8,128)(2,1)S(1)} %get-tuple-element.69), channel_id=1, source_target_pairs={{0,8},{4,12},{8,0},{12,4},{16,24},{20,28},{24,16},{28,20},{1,9},{5... | collective-permute-start | bytes 491528 | tf_op jit(solution)/shard_map/ppermute | solution.py:29
  32.8 0.9 %shard_map.122 = (bf16[32,1024]{1,0:T(8,128)(2,1)S(1)}, bf16[32,1024]{1,0:T(8,128)(2,1)S(1)}, bf16[32,1024]{1,0:T(8,128)(2,1)S(1)}, bf16[32,1024]{1,0:T(8,128)(2,1)S(1)}) custom-call(bf16[64,1024]{1,0:T(8,128)(2,1)S(1)} %get-tuple-element.44.refs_0_.x_ref, bf16[1,1024]{1,0:T(2,128)(2,1)S(1)} %copy-done.4, ...), custom_call_target="tpu_custom_call" | custom-call | tf_op jit(solution)/shard_map/pallas_call | solution.py:41
  33.7 1.6 %collective-permute-start.7 = (bf16[32,1024]{1,0:T(8,128)(2,1)S(1)}, bf16[32,1024]{1,0:T(8,128)(2,1)S(1)}, u32[]{:S(2)}, u32[]{:S(2)}) collective-permute-start(bf16[32,1024]{1,0:T(8,128)(2,1)S(1)} %get-tuple-element.56), channel_id=1, source_target_pairs={{0,1},{1,0},{2,3},{3,2},{4,5},{5,4},{6,7},{7,6},{8,9},{9,8},{10,11... | collective-permute-start | bytes 196616 | tf_op jit(solution)/shard_map/ppermute | solution.py:29
  35.3 0.0 collective-permute-done.10.refs_1_
  35.4 2.6 %collective-permute-start.8 = (bf16[32,1024]{1,0:T(8,128)(2,1)S(1)}, bf16[32,1024]{1,0:T(8,128)(2,1)S(1)}, u32[]{:S(2)}, u32[]{:S(2)}) collective-permute-start(bf16[32,1024]{1,0:T(8,128)(2,1)S(1)} %get-tuple-element.57), channel_id=1, source_target_pairs={{0,2},{1,3},{2,0},{3,1},{4,6},{5,7},{6,4},{7,5},{8,10},{9,11},{10,... | collective-permute-start | bytes 196616 | tf_op jit(solution)/shard_map/ppermute | solution.py:29
  37.9 0.0 collective-permute-done.11.refs_2_
  37.9 1.3 %collective-permute-start.9 = (bf16[32,1024]{1,0:T(8,128)(2,1)S(1)}, bf16[32,1024]{1,0:T(8,128)(2,1)S(1)}, u32[]{:S(2)}, u32[]{:S(2)}) collective-permute-start(bf16[32,1024]{1,0:T(8,128)(2,1)S(1)} %get-tuple-element.58), channel_id=1, source_target_pairs={{0,3},{1,2},{2,1},{3,0},{4,7},{5,6},{6,5},{7,4},{8,11},{9,10},{10,... | collective-permute-start | bytes 196616 | tf_op jit(solution)/shard_map/ppermute | solution.py:29
  39.2 0.0 collective-permute-done.12.refs_3_
  39.2 1.0 %collective-permute-start.18 = (bf16[80,1024]{1,0:T(8,128)(2,1)S(1)}, bf16[80,1024]{1,0:T(8,128)(2,1)S(1)}, u32[]{:S(2)}, u32[]{:S(2)}) collective-permute-start(bf16[80,1024]{1,0:T(8,128)(2,1)S(1)} %get-tuple-element.70), channel_id=1, source_target_pairs={{0,16},{4,20},{8,24},{12,28},{16,0},{20,4},{24,8},{28,12},{1,17},{... | collective-permute-start | bytes 491528 | tf_op jit(solution)/shard_map/ppermute | solution.py:29
  40.2 0.0 collective-permute-done.7.refs_1_
  40.2 0.5 collective-permute-start.19
  40.7 1.2 %collective-permute-done.8.refs_2_ = bf16[32,1024]{1,0:T(8,128)(2,1)S(1)} collective-permute-done((bf16[32,1024]{1,0:T(8,128)(2,1)S(1)}, bf16[32,1024]{1,0:T(8,128)(2,1)S(1)}, u32[]{:S(2)}, u32[]{:S(2)}) %collective-permute-start.8) | collective-permute-done | bytes 65568 | tf_op jit(solution)/shard_map/ppermute | solution.py:29
  41.9 0.0 collective-permute-start.13
  41.9 2.1 %collective-permute-done.9.refs_3_ = bf16[32,1024]{1,0:T(8,128)(2,1)S(1)} collective-permute-done((bf16[32,1024]{1,0:T(8,128)(2,1)S(1)}, bf16[32,1024]{1,0:T(8,128)(2,1)S(1)}, u32[]{:S(2)}, u32[]{:S(2)}) %collective-permute-start.9) | collective-permute-done | bytes 65568 | tf_op jit(solution)/shard_map/ppermute | solution.py:29
  44.0 0.0 collective-permute-start.14
  44.0 0.0 collective-permute-done.17.refs_9_
  44.0 0.5 %collective-permute-start.15 = (bf16[64,1280]{1,0:T(8,128)(2,1)S(1)}, bf16[64,1280]{1,0:T(8,128)(2,1)S(1)}, u32[]{:S(2)}, u32[]{:S(2)}) collective-permute-start(bf16[64,1280]{1,0:T(8,128)(2,1)S(1)} %collective-permute-done.11.refs_2_), channel_id=1, source_target_pairs={{0,4},{4,0},{8,12},{12,8},{16,20},{20,16},{24,28},{28,24},{1,5},{5... | collective-permute-start | bytes 491528 | tf_op jit(solution)/shard_map/ppermute | solution.py:29
  44.5 1.8 %shard_map.123 = (bf16[512,1024]{1,0:T(8,128)(2,1)}, bf16[512,1024]{1,0:T(8,128)(2,1)}) custom-call(s32[4,16]{1,0:T(4,128)S(1)} %bitcast.3, bf16[32,1024]{1,0:T(8,128)(2,1)S(1)} %get-tuple-element.55.refs_0_, bf16[32,1024]{1,0:T(8,128)(2,1)S(1)} %collective-permute-done.7.refs_1_, bf16[32,1024]{1,0:T(8,128)(2,1)S(1)} %collective-permute-done.8.refs_2_, ...), custom_call_target="tpu_custom_call" | custom-call | tf_op jit(solution)/shard_map/pallas_call | solution.py:41
  46.3 0.0 collective-permute-done.18.refs_10_
  46.3 0.0 collective-permute-start.16
  46.3 0.1 collective-permute-done.19.refs_11_
  46.4 0.4 collective-permute-start.20
  46.8 0.0 collective-permute-done.13.refs_4_
  46.8 0.1 collective-permute-start.21
  47.0 0.0 collective-permute-done.14.refs_5_
  47.0 0.4 collective-permute-start.22
  47.4 0.0 collective-permute-done.15.refs_6_
  47.4 0.1 collective-permute-start.23
  47.5 0.2 collective-permute-done.16.refs_7_
  47.7 0.2 collective-permute-done.20.refs_12_
  48.0 0.3 collective-permute-done.21.refs_13_
  48.2 0.2 collective-permute-done.22.refs_14_
  48.5 0.3 collective-permute-done.23.refs_15_
  48.8 1.4 %shard_map.124 = (f32[1,128,512]{2,1,0:T(8,128)}, f32[1,128,512]{2,1,0:T(8,128)}, f32[1,64,1024]{2,1,0:T(8,128)}, f32[1,1024]{1,0:T(1,128)}) custom-call(bf16[64,1280]{1,0:T(8,128)(2,1)S(1)} %get-tuple-element.65.refs_0_, bf16[64,1280]{1,0:T(8,128)(2,1)S(1)} %collective-permute-done.10.refs_1_, bf16[64,1280]{1,0:T(8,128)(2,1)S(1)} %collective-permute-done.11.refs_2_, ...), custom_call_target="tpu_custom_call" | custom-call | tf_op jit(solution)/shard_map/pallas_call | solution.py:41
  (10 shorter events, 0.1 us)
Async XLA Ops:
  0.6 1.2 %copy-start = (bf16[512,1024]{1,0:T(8,128)(2,1)S(1)}, bf16[512,1024]{1,0:T(8,128)(2,1)}, u32[]{:S(2)}) copy-start(bf16[512,1024]{1,0:T(8,128)(2,1)} %param.7) | copy-start | bytes 3145732
  1.9 0.9 %copy-start.1 = (bf16[1,128,512]{2,1,0:T(8,128)(2,1)S(1)}, bf16[1,128,512]{2,1,0:T(8,128)(2,1)}, u32[]{:S(2)}) copy-start(bf16[1,128,512]{2,1,0:T(8,128)(2,1)} %gate_ref) | copy-start | bytes 393220
  1.9 1.0 %copy-start.2 = (bf16[1,128,512]{2,1,0:T(8,128)(2,1)S(1)}, bf16[1,128,512]{2,1,0:T(8,128)(2,1)}, u32[]{:S(2)}) copy-start(bf16[1,128,512]{2,1,0:T(8,128)(2,1)} %up_ref) | copy-start | bytes 393220
  1.9 1.0 %copy-start.3 = (bf16[1,64,1024]{2,1,0:T(8,128)(2,1)S(1)}, bf16[1,64,1024]{2,1,0:T(8,128)(2,1)}, u32[]{:S(2)}) copy-start(bf16[1,64,1024]{2,1,0:T(8,128)(2,1)} %down_ref) | copy-start | bytes 393220
  2.9 13.9 %collective-permute-start.5 = (bf16[192,1024]{1,0:T(8,128)(2,1)S(1)}, bf16[192,1024]{1,0:T(8,128)(2,1)S(1)}, u32[]{:S(2)}, u32[]{:S(2)}) collective-permute-start(bf16[192,1024]{1,0:T(8,128)(2,1)S(1)} %shard_map.120.refs_3_), channel_id=1, source_target_pairs={{0,24},{4,28},{8,16},{12,20},{16,8},{20,12},{24,0},{28,4},{1,25},{... | collective-permute-start | bytes 1179656 | tf_op jit(solution)/shard_map/ppermute | solution.py:29
  6.9 17.5 %collective-permute-start.3 = (bf16[192,1024]{1,0:T(8,128)(2,1)S(1)}, bf16[192,1024]{1,0:T(8,128)(2,1)S(1)}, u32[]{:S(2)}, u32[]{:S(2)}) collective-permute-start(bf16[192,1024]{1,0:T(8,128)(2,1)S(1)} %shard_map.120.refs_3_), channel_id=1, source_target_pairs={{0,16},{4,20},{8,24},{12,28},{16,0},{20,4},{24,8},{28,12},{1,17},{... | collective-permute-start | bytes 1179656 | tf_op jit(solution)/shard_map/ppermute | solution.py:29
  7.4 17.3 %collective-permute-start.1 = (bf16[192,1024]{1,0:T(8,128)(2,1)S(1)}, bf16[192,1024]{1,0:T(8,128)(2,1)S(1)}, u32[]{:S(2)}, u32[]{:S(2)}) collective-permute-start(bf16[192,1024]{1,0:T(8,128)(2,1)S(1)} %shard_map.120.refs_3_), channel_id=1, source_target_pairs={{0,8},{4,12},{8,0},{12,4},{16,24},{20,28},{24,16},{28,20},{1,9},{5... | collective-permute-start | bytes 1179656 | tf_op jit(solution)/shard_map/ppermute | solution.py:29
  10.4 14.5 %copy-start.4 = (bf16[1,1024]{1,0:T(2,128)(2,1)S(1)}, bf16[1,1024]{1,0:T(2,128)(2,1)}, u32[]{:S(2)}) copy-start(bf16[1,1024]{1,0:T(2,128)(2,1)} %router_ref.3) | copy-start | bytes 6148
  10.4 14.5 %all-to-all-start = ((bf16[4,32,1024]{2,1,0:T(8,128)(2,1)}), bf16[4,32,1024]{2,1,0:T(8,128)(2,1)S(1)}, u32[]{:S(2)}, u32[]{:S(2)}) async-start(bf16[4,32,1024]{2,1,0:T(8,128)(2,1)} %shard_map.118), calls=%async_computation | async-start | bytes 524288 | tf_op jit(solution)/shard_map/all_to_all | solution.py:245
  15.8 11.0 %collective-permute-start = (bf16[192,1024]{1,0:T(8,128)(2,1)S(1)}, bf16[192,1024]{1,0:T(8,128)(2,1)S(1)}, u32[]{:S(2)}, u32[]{:S(2)}) collective-permute-start(bf16[192,1024]{1,0:T(8,128)(2,1)S(1)} %shard_map.120.refs_3_), channel_id=1, source_target_pairs={{0,4},{4,0},{8,12},{12,8},{16,20},{20,16},{24,28},{28,24},{1,5},{5... | collective-permute-start | bytes 1179656 | tf_op jit(solution)/shard_map/ppermute | solution.py:29
  16.9 10.7 %collective-permute-start.6 = (bf16[192,1024]{1,0:T(8,128)(2,1)S(1)}, bf16[192,1024]{1,0:T(8,128)(2,1)}, u32[]{:S(2)}, u32[]{:S(2)}) collective-permute-start(bf16[192,1024]{1,0:T(8,128)(2,1)S(1)} %collective-permute-done.5.refs_9_), channel_id=1, source_target_pairs={{0,4},{4,0},{8,12},{12,8},{16,20},{20,16},{24,28},{28,24},{1,5},{5... | collective-permute-start | bytes 1179656 | tf_op jit(solution)/shard_map/ppermute | solution.py:29
  24.4 4.2 %collective-permute-start.4 = (bf16[192,1024]{1,0:T(8,128)(2,1)S(1)}, bf16[192,1024]{1,0:T(8,128)(2,1)}, u32[]{:S(2)}, u32[]{:S(2)}) collective-permute-start(bf16[192,1024]{1,0:T(8,128)(2,1)S(1)} %collective-permute-done.3.refs_7_), channel_id=1, source_target_pairs={{0,4},{4,0},{8,12},{12,8},{16,20},{20,16},{24,28},{28,24},{1,5},{5... | collective-permute-start | bytes 1179656 | tf_op jit(solution)/shard_map/ppermute | solution.py:29
  24.7 3.9 %collective-permute-start.2 = (bf16[192,1024]{1,0:T(8,128)(2,1)S(1)}, bf16[192,1024]{1,0:T(8,128)(2,1)}, u32[]{:S(2)}, u32[]{:S(2)}) collective-permute-start(bf16[192,1024]{1,0:T(8,128)(2,1)S(1)} %collective-permute-done.1.refs_5_), channel_id=1, source_target_pairs={{0,4},{4,0},{8,12},{12,8},{16,20},{20,16},{24,28},{28,24},{1,5},{5... | collective-permute-start | bytes 1179656 | tf_op jit(solution)/shard_map/ppermute | solution.py:29
  25.1 10.3 %collective-permute-start.10 = (bf16[64,1280]{1,0:T(8,128)(2,1)S(1)}, bf16[64,1280]{1,0:T(8,128)(2,1)S(1)}, u32[]{:S(2)}, u32[]{:S(2)}) collective-permute-start(bf16[64,1280]{1,0:T(8,128)(2,1)S(1)} %get-tuple-element.62), channel_id=1, source_target_pairs={{0,8},{4,12},{8,0},{12,4},{16,24},{20,28},{24,16},{28,20},{1,9},{5... | collective-permute-start | bytes 491528 | tf_op jit(solution)/shard_map/ppermute | solution.py:29
  26.9 11.1 %collective-permute-start.11 = (bf16[64,1280]{1,0:T(8,128)(2,1)S(1)}, bf16[64,1280]{1,0:T(8,128)(2,1)S(1)}, u32[]{:S(2)}, u32[]{:S(2)}) collective-permute-start(bf16[64,1280]{1,0:T(8,128)(2,1)S(1)} %get-tuple-element.63), channel_id=1, source_target_pairs={{0,16},{4,20},{8,24},{12,28},{16,0},{20,4},{24,8},{28,12},{1,17},{... | collective-permute-start | bytes 491528 | tf_op jit(solution)/shard_map/ppermute | solution.py:29
  27.6 11.7 %collective-permute-start.12 = (bf16[64,1280]{1,0:T(8,128)(2,1)S(1)}, bf16[64,1280]{1,0:T(8,128)(2,1)S(1)}, u32[]{:S(2)}, u32[]{:S(2)}) collective-permute-start(bf16[64,1280]{1,0:T(8,128)(2,1)S(1)} %get-tuple-element.64), channel_id=1, source_target_pairs={{0,24},{4,28},{8,16},{12,20},{16,8},{20,12},{24,0},{28,4},{1,25},{... | collective-permute-start | bytes 491528 | tf_op jit(solution)/shard_map/ppermute | solution.py:29
  31.0 13.0 %collective-permute-start.17 = (bf16[80,1024]{1,0:T(8,128)(2,1)S(1)}, bf16[80,1024]{1,0:T(8,128)(2,1)S(1)}, u32[]{:S(2)}, u32[]{:S(2)}) collective-permute-start(bf16[80,1024]{1,0:T(8,128)(2,1)S(1)} %get-tuple-element.69), channel_id=1, source_target_pairs={{0,8},{4,12},{8,0},{12,4},{16,24},{20,28},{24,16},{28,20},{1,9},{5... | collective-permute-start | bytes 491528 | tf_op jit(solution)/shard_map/ppermute | solution.py:29
  33.7 6.5 %collective-permute-start.7 = (bf16[32,1024]{1,0:T(8,128)(2,1)S(1)}, bf16[32,1024]{1,0:T(8,128)(2,1)S(1)}, u32[]{:S(2)}, u32[]{:S(2)}) collective-permute-start(bf16[32,1024]{1,0:T(8,128)(2,1)S(1)} %get-tuple-element.56), channel_id=1, source_target_pairs={{0,1},{1,0},{2,3},{3,2},{4,5},{5,4},{6,7},{7,6},{8,9},{9,8},{10,11... | collective-permute-start | bytes 196616 | tf_op jit(solution)/shard_map/ppermute | solution.py:29
  35.4 6.6 %collective-permute-start.8 = (bf16[32,1024]{1,0:T(8,128)(2,1)S(1)}, bf16[32,1024]{1,0:T(8,128)(2,1)S(1)}, u32[]{:S(2)}, u32[]{:S(2)}) collective-permute-start(bf16[32,1024]{1,0:T(8,128)(2,1)S(1)} %get-tuple-element.57), channel_id=1, source_target_pairs={{0,2},{1,3},{2,0},{3,1},{4,6},{5,7},{6,4},{7,5},{8,10},{9,11},{10,... | collective-permute-start | bytes 196616 | tf_op jit(solution)/shard_map/ppermute | solution.py:29
  37.9 6.1 %collective-permute-start.9 = (bf16[32,1024]{1,0:T(8,128)(2,1)S(1)}, bf16[32,1024]{1,0:T(8,128)(2,1)S(1)}, u32[]{:S(2)}, u32[]{:S(2)}) collective-permute-start(bf16[32,1024]{1,0:T(8,128)(2,1)S(1)} %get-tuple-element.58), channel_id=1, source_target_pairs={{0,3},{1,2},{2,1},{3,0},{4,7},{5,6},{6,5},{7,4},{8,11},{9,10},{10,... | collective-permute-start | bytes 196616 | tf_op jit(solution)/shard_map/ppermute | solution.py:29
  39.2 7.1 %collective-permute-start.18 = (bf16[80,1024]{1,0:T(8,128)(2,1)S(1)}, bf16[80,1024]{1,0:T(8,128)(2,1)S(1)}, u32[]{:S(2)}, u32[]{:S(2)}) collective-permute-start(bf16[80,1024]{1,0:T(8,128)(2,1)S(1)} %get-tuple-element.70), channel_id=1, source_target_pairs={{0,16},{4,20},{8,24},{12,28},{16,0},{20,4},{24,8},{28,12},{1,17},{... | collective-permute-start | bytes 491528 | tf_op jit(solution)/shard_map/ppermute | solution.py:29
  40.2 6.2 %collective-permute-start.19 = (bf16[80,1024]{1,0:T(8,128)(2,1)S(1)}, bf16[80,1024]{1,0:T(8,128)(2,1)S(1)}, u32[]{:S(2)}, u32[]{:S(2)}) collective-permute-start(bf16[80,1024]{1,0:T(8,128)(2,1)S(1)} %get-tuple-element.71), channel_id=1, source_target_pairs={{0,24},{4,28},{8,16},{12,20},{16,8},{20,12},{24,0},{28,4},{1,25},{... | collective-permute-start | bytes 491528 | tf_op jit(solution)/shard_map/ppermute | solution.py:29
  40.7 3.8 %copy-start.5 = (s32[1,1,4,16]{3,2,1,0:T(4,128)S(1)}, s32[1,1,4,16]{3,2,1,0:T(4,128)}, u32[]{:S(2)}) copy-start(s32[1,1,4,16]{3,2,1,0:T(4,128)} %param.8) | copy-start | bytes 772
  41.9 4.9 %collective-permute-start.13 = (bf16[64,1280]{1,0:T(8,128)(2,1)S(1)}, bf16[64,1280]{1,0:T(8,128)(2,1)S(1)}, u32[]{:S(2)}, u32[]{:S(2)}) collective-permute-start(bf16[64,1280]{1,0:T(8,128)(2,1)S(1)} %get-tuple-element.65.refs_0_), channel_id=1, source_target_pairs={{0,4},{4,0},{8,12},{12,8},{16,20},{20,16},{24,28},{28,24},{1,5},{5... | collective-permute-start | bytes 491528 | tf_op jit(solution)/shard_map/ppermute | solution.py:29
  44.0 3.0 %collective-permute-start.14 = (bf16[64,1280]{1,0:T(8,128)(2,1)S(1)}, bf16[64,1280]{1,0:T(8,128)(2,1)S(1)}, u32[]{:S(2)}, u32[]{:S(2)}) collective-permute-start(bf16[64,1280]{1,0:T(8,128)(2,1)S(1)} %collective-permute-done.10.refs_1_), channel_id=1, source_target_pairs={{0,4},{4,0},{8,12},{12,8},{16,20},{20,16},{24,28},{28,24},{1,5},{5... | collective-permute-start | bytes 491528 | tf_op jit(solution)/shard_map/ppermute | solution.py:29
  44.0 3.3 %collective-permute-start.15 = (bf16[64,1280]{1,0:T(8,128)(2,1)S(1)}, bf16[64,1280]{1,0:T(8,128)(2,1)S(1)}, u32[]{:S(2)}, u32[]{:S(2)}) collective-permute-start(bf16[64,1280]{1,0:T(8,128)(2,1)S(1)} %collective-permute-done.11.refs_2_), channel_id=1, source_target_pairs={{0,4},{4,0},{8,12},{12,8},{16,20},{20,16},{24,28},{28,24},{1,5},{5... | collective-permute-start | bytes 491528 | tf_op jit(solution)/shard_map/ppermute | solution.py:29
  46.3 1.4 %collective-permute-start.16 = (bf16[64,1280]{1,0:T(8,128)(2,1)S(1)}, bf16[64,1280]{1,0:T(8,128)(2,1)S(1)}, u32[]{:S(2)}, u32[]{:S(2)}) collective-permute-start(bf16[64,1280]{1,0:T(8,128)(2,1)S(1)} %collective-permute-done.12.refs_3_), channel_id=1, source_target_pairs={{0,4},{4,0},{8,12},{12,8},{16,20},{20,16},{24,28},{28,24},{1,5},{5... | collective-permute-start | bytes 491528 | tf_op jit(solution)/shard_map/ppermute | solution.py:29
  46.4 1.5 %collective-permute-start.20 = (bf16[80,1024]{1,0:T(8,128)(2,1)S(1)}, bf16[80,1024]{1,0:T(8,128)(2,1)S(1)}, u32[]{:S(2)}, u32[]{:S(2)}) collective-permute-start(bf16[80,1024]{1,0:T(8,128)(2,1)S(1)} %get-tuple-element.72.late_ref.refs_8_), channel_id=1, source_target_pairs={{0,4},{4,0},{8,12},{12,8},{16,20},{20,16},{24,28},{28,24},{1,5},{5... | collective-permute-start | bytes 491528 | tf_op jit(solution)/shard_map/ppermute | solution.py:29
  46.8 1.4 %collective-permute-start.21 = (bf16[80,1024]{1,0:T(8,128)(2,1)S(1)}, bf16[80,1024]{1,0:T(8,128)(2,1)S(1)}, u32[]{:S(2)}, u32[]{:S(2)}) collective-permute-start(bf16[80,1024]{1,0:T(8,128)(2,1)S(1)} %collective-permute-done.17.refs_9_), channel_id=1, source_target_pairs={{0,4},{4,0},{8,12},{12,8},{16,20},{20,16},{24,28},{28,24},{1,5},{5... | collective-permute-start | bytes 491528 | tf_op jit(solution)/shard_map/ppermute | solution.py:29
  47.0 1.5 %collective-permute-start.22 = (bf16[80,1024]{1,0:T(8,128)(2,1)S(1)}, bf16[80,1024]{1,0:T(8,128)(2,1)S(1)}, u32[]{:S(2)}, u32[]{:S(2)}) collective-permute-start(bf16[80,1024]{1,0:T(8,128)(2,1)S(1)} %collective-permute-done.18.refs_10_), channel_id=1, source_target_pairs={{0,4},{4,0},{8,12},{12,8},{16,20},{20,16},{24,28},{28,24},{1,5},{5... | collective-permute-start | bytes 491528 | tf_op jit(solution)/shard_map/ppermute | solution.py:29
  47.4 1.4 %collective-permute-start.23 = (bf16[80,1024]{1,0:T(8,128)(2,1)S(1)}, bf16[80,1024]{1,0:T(8,128)(2,1)S(1)}, u32[]{:S(2)}, u32[]{:S(2)}) collective-permute-start(bf16[80,1024]{1,0:T(8,128)(2,1)S(1)} %collective-permute-done.19.refs_11_), channel_id=1, source_target_pairs={{0,4},{4,0},{8,12},{12,8},{16,20},{20,16},{24,28},{28,24},{1,5},{5... | collective-permute-start | bytes 491528 | tf_op jit(solution)/shard_map/ppermute | solution.py:29

commit v4 on v3

--- a/solution.py
+++ b/solution.py
@@ -200,7 +200,7 @@
 def combine(slots, chosen_ref, *refs):
     got, (mixed_ref, grad_ref, out_ref, back_ref) = refs[:-4], refs[-4:]
     me = lax.axis_index("expert")
-    for k, ref in enumerate(got):
+    for k, ref in enumerate(got[::-1]):
         at = pl.ds(pl.multiple_of((me ^ k) * slots, slots), slots)
         out_ref[at, :] = ref[:slots, :]
         back_ref[at, :] = ref[slots:, :]
@@ -273,11 +273,11 @@
         limit=16 if taken <= 64 else 40,
     )
     own_late = lates[0]
-    returned = [returned[0]] + [swap(returned[k], "expert", k) for k in range(1, experts)]
+    returned = [returned[0]] + [swap(returned[k], "expert", k) for k in range(experts - 1, 0, -1)][::-1]
     mixed, grad_tokens = call(
         functools.partial(combine, slots),
         (shape(held, width, BF16),) * 2,
-        (selections[0, 0], *returned),
+        (selections[0, 0], *returned[::-1]),
         [pltpu.VMEM((taken, width), BF16)] * 2,
     )
     lates = [lates[0]] + [swap(lates[k], "dp", 2 * k) for k in range(1, chips)]

time: 50.5 us -> 50.2 us (level)
  starting transfers between devices: 24.1 us -> 23.4 us
    ppermute x24, starting transfers between devices: 18.7 us -> 18 us  [swap(): return lax.ppermute(value, axis, [(i, i ^ step) for i in range(size)])]
  transfers between devices with their start and end apart: 25 -> 25, of which waited for: 11 -> 10; matrix products, arithmetic and copies ran while one was open for 4% -> 4% of each run, Pallas kernels for 12% -> 12%
where the time goes in v4:
time: 50.2 us; the launch traced here: 49.9 us
  starting transfers between devices  23.4 us (47%)
  waiting for transfers between devices  14 us (28%)
  Pallas kernels  7.33 us (15%)
  local copies, waits for them, and re-layouts  4.41 us (9%)
  between operations  0.7 us (1%)
    ppermute x24, starting transfers between devices, swap(): return lax.ppermute(value, axis, [(i, i ^ step) for i in range(size)])  18 us
    ppermute x24, waiting for transfers between devices, swap(): return lax.ppermute(value, axis, [(i, i ^ step) for i in range(size)])  14 us
    pallas_call x7, Pallas kernels, call(): pl.pallas_call(body, out_shape=out_shape, in_specs=[VMEM] * len(args), ou...  7.33 us
    all_to_all x1, starting transfers between devices, local(): got = [lax.all_to_all(sent, 'expert', 0, 0, tiled=True)]  5.4 us
    gather x1, local copies, waits for them, and re-layouts, local(): d_sent = cotangent.at[flat].get(mode='promise_in_bounds')  2.15 us
  transfers between devices with their start and end apart: 25, of which 10 were waited for; matrix products, arithmetic and copies ran while one was open for 4% of the time, Pallas kernels for 12%

profile of v4, /device:TPU:0, one launch (start us, length us, event | category | flops | bytes accessed | tf_op | source)
XLA Modules:
  0.0 49.9 jit_solution(1072451667329081760)
XLA Ops:
  0.6 0.0 copy-start
  0.6 0.9 %reshape.43 = s32[64,1]{0,1:T(1,128)S(1)} reshape(s32[1,1,4,16]{3,2,1,0:T(4,128)} %param.8) | data formatting | bytes 512 | tf_op jit(solution)/shard_map/reshape | solution.py:227
  1.5 0.4 copy-done
  1.9 0.7 %gather_fusion = bf16[64,1024]{1,0:T(8,128)(2,1)S(1)} fusion(bf16[512,1024]{1,0:T(8,128)(2,1)S(1)} %copy-done, s32[1024]{0:T(1024)S(1)} %pad_clamp_fusion), kind=kCustom, calls=%fused_computation | custom fusion | bytes 262400 | tf_op jit(solution)/shard_map/gather | solution.py:228
  2.6 0.2 copy-done.1
  2.8 0.1 copy-done.2
  2.8 0.1 copy-done.3
  2.9 4.0 %collective-permute-start.5 = (bf16[192,1024]{1,0:T(8,128)(2,1)S(1)}, bf16[192,1024]{1,0:T(8,128)(2,1)S(1)}, u32[]{:S(2)}, u32[]{:S(2)}) collective-permute-start(bf16[192,1024]{1,0:T(8,128)(2,1)S(1)} %shard_map.120.refs_3_), channel_id=1, source_target_pairs={{0,24},{4,28},{8,16},{12,20},{16,8},{20,12},{24,0},{28,4},{1,25},{... | collective-permute-start | bytes 1179656 | tf_op jit(solution)/shard_map/ppermute | solution.py:29
  6.9 0.5 %collective-permute-start.3 = (bf16[192,1024]{1,0:T(8,128)(2,1)S(1)}, bf16[192,1024]{1,0:T(8,128)(2,1)S(1)}, u32[]{:S(2)}, u32[]{:S(2)}) collective-permute-start(bf16[192,1024]{1,0:T(8,128)(2,1)S(1)} %shard_map.120.refs_3_), channel_id=1, source_target_pairs={{0,16},{4,20},{8,24},{12,28},{16,0},{20,4},{24,8},{28,12},{1,17},{... | collective-permute-start | bytes 1179656 | tf_op jit(solution)/shard_map/ppermute | solution.py:29
  7.4 0.1 collective-permute-start.1
  7.5 2.2 %gather_fusion.1 = bf16[64,1024]{1,0:T(8,128)(2,1)S(1)} fusion(bf16[512,1024]{1,0:T(8,128)(2,1)} %param.13, s32[1024]{0:T(1024)S(1)} %pad_clamp_fusion), kind=kCustom, calls=%fused_computation.1 | custom fusion | bytes 262400 | tf_op jit(solution)/shard_map/gather | solution.py:229
  9.7 0.7 %shard_map.118 = bf16[4,32,1024]{2,1,0:T(8,128)(2,1)} custom-call(bf16[64,1024]{1,0:T(8,128)(2,1)S(1)} %gather_fusion, bf16[64,1024]{1,0:T(8,128)(2,1)S(1)} %gather_fusion.1), custom_call_target="tpu_custom_call" | custom-call | tf_op jit(solution)/shard_map/pallas_call | solution.py:41
  10.4 5.4 %all-to-all-start = ((bf16[4,32,1024]{2,1,0:T(8,128)(2,1)}), bf16[4,32,1024]{2,1,0:T(8,128)(2,1)S(1)}, u32[]{:S(2)}, u32[]{:S(2)}) async-start(bf16[4,32,1024]{2,1,0:T(8,128)(2,1)} %shard_map.118), calls=%async_computation | async-start | bytes 524288 | tf_op jit(solution)/shard_map/all_to_all | solution.py:245
  15.8 0.0 collective-permute-start
  15.8 1.1 %collective-permute-done.5.refs_9_ = bf16[192,1024]{1,0:T(8,128)(2,1)S(1)} collective-permute-done((bf16[192,1024]{1,0:T(8,128)(2,1)S(1)}, bf16[192,1024]{1,0:T(8,128)(2,1)S(1)}, u32[]{:S(2)}, u32[]{:S(2)}) %collective-permute-start.5) | collective-permute-done | bytes 393248 | tf_op jit(solution)/shard_map/ppermute | solution.py:29
  16.9 0.0 collective-permute-start.6
  16.9 7.6 %collective-permute-done.3.refs_7_ = bf16[192,1024]{1,0:T(8,128)(2,1)S(1)} collective-permute-done((bf16[192,1024]{1,0:T(8,128)(2,1)S(1)}, bf16[192,1024]{1,0:T(8,128)(2,1)S(1)}, u32[]{:S(2)}, u32[]{:S(2)}) %collective-permute-start.3) | collective-permute-done | bytes 393248 | tf_op jit(solution)/shard_map/ppermute | solution.py:29
  24.4 0.0 collective-permute-start.4
  24.5 0.3 collective-permute-done.1.refs_5_
  24.7 0.2 collective-permute-start.2
  25.0 0.0 all-to-all-done.refs_0_
  25.0 0.1 shard_map.119
  25.1 1.7 %collective-permute-start.10 = (bf16[64,1280]{1,0:T(8,128)(2,1)S(1)}, bf16[64,1280]{1,0:T(8,128)(2,1)S(1)}, u32[]{:S(2)}, u32[]{:S(2)}) collective-permute-start(bf16[64,1280]{1,0:T(8,128)(2,1)S(1)} %get-tuple-element.62), channel_id=1, source_target_pairs={{0,8},{4,12},{8,0},{12,4},{16,24},{20,28},{24,16},{28,20},{1,9},{5... | collective-permute-start | bytes 491528 | tf_op jit(solution)/shard_map/ppermute | solution.py:29
  26.8 0.0 collective-permute-done.refs_4_
  26.9 0.7 %collective-permute-start.11 = (bf16[64,1280]{1,0:T(8,128)(2,1)S(1)}, bf16[64,1280]{1,0:T(8,128)(2,1)S(1)}, u32[]{:S(2)}, u32[]{:S(2)}) collective-permute-start(bf16[64,1280]{1,0:T(8,128)(2,1)S(1)} %get-tuple-element.63), channel_id=1, source_target_pairs={{0,16},{4,20},{8,24},{12,28},{16,0},{20,4},{24,8},{28,12},{1,17},{... | collective-permute-start | bytes 491528 | tf_op jit(solution)/shard_map/ppermute | solution.py:29
  27.6 0.0 collective-permute-done.6.refs_10_
  27.6 1.1 %collective-permute-start.12 = (bf16[64,1280]{1,0:T(8,128)(2,1)S(1)}, bf16[64,1280]{1,0:T(8,128)(2,1)S(1)}, u32[]{:S(2)}, u32[]{:S(2)}) collective-permute-start(bf16[64,1280]{1,0:T(8,128)(2,1)S(1)} %get-tuple-element.64), channel_id=1, source_target_pairs={{0,24},{4,28},{8,16},{12,20},{16,8},{20,12},{24,0},{28,4},{1,25},{... | collective-permute-start | bytes 491528 | tf_op jit(solution)/shard_map/ppermute | solution.py:29
  28.7 0.0 collective-permute-done.4.refs_8_
  28.7 0.0 collective-permute-done.2.refs_6_
  28.7 2.3 %shard_map.121 = (bf16[80,1024]{1,0:T(8,128)(2,1)S(1)}, bf16[80,1024]{1,0:T(8,128)(2,1)S(1)}, bf16[80,1024]{1,0:T(8,128)(2,1)S(1)}, bf16[80,1024]{1,0:T(8,128)(2...) custom-call(bf16[64,1024]{1,0:T(8,128)(2,1)S(1)} %get-tuple-element., ...), custom_call_target="tpu_custom_call" | custom-call | tf_op jit(solution)/shard_map/pallas_call | solution.py:41
  31.0 1.7 %collective-permute-start.17 = (bf16[80,1024]{1,0:T(8,128)(2,1)S(1)}, bf16[80,1024]{1,0:T(8,128)(2,1)S(1)}, u32[]{:S(2)}, u32[]{:S(2)}) collective-permute-start(bf16[80,1024]{1,0:T(8,128)(2,1)S(1)} %get-tuple-element.69), channel_id=1, source_target_pairs={{0,8},{4,12},{8,0},{12,4},{16,24},{20,28},{24,16},{28,20},{1,9},{5... | collective-permute-start | bytes 491528 | tf_op jit(solution)/shard_map/ppermute | solution.py:29
  32.8 0.9 %shard_map.122 = (bf16[32,1024]{1,0:T(8,128)(2,1)S(1)}, bf16[32,1024]{1,0:T(8,128)(2,1)S(1)}, bf16[32,1024]{1,0:T(8,128)(2,1)S(1)}, bf16[32,1024]{1,0:T(8,128)(2,1)S(1)}) custom-call(bf16[64,1024]{1,0:T(8,128)(2,1)S(1)} %get-tuple-element.44.refs_0_.x_ref, bf16[1,1024]{1,0:T(2,128)(2,1)S(1)} %copy-done.4, ...), custom_call_target="tpu_custom_call" | custom-call | tf_op jit(solution)/shard_map/pallas_call | solution.py:41
  33.7 1.6 %collective-permute-start.9 = (bf16[32,1024]{1,0:T(8,128)(2,1)S(1)}, bf16[32,1024]{1,0:T(8,128)(2,1)S(1)}, u32[]{:S(2)}, u32[]{:S(2)}) collective-permute-start(bf16[32,1024]{1,0:T(8,128)(2,1)S(1)} %get-tuple-element.57), channel_id=1, source_target_pairs={{0,1},{1,0},{2,3},{3,2},{4,5},{5,4},{6,7},{7,6},{8,9},{9,8},{10,11... | collective-permute-start | bytes 196616 | tf_op jit(solution)/shard_map/ppermute | solution.py:29
  35.3 0.0 collective-permute-done.10.refs_1_
  35.4 2.5 %collective-permute-start.7 = (bf16[32,1024]{1,0:T(8,128)(2,1)S(1)}, bf16[32,1024]{1,0:T(8,128)(2,1)S(1)}, u32[]{:S(2)}, u32[]{:S(2)}) collective-permute-start(bf16[32,1024]{1,0:T(8,128)(2,1)S(1)} %get-tuple-element.55), channel_id=1, source_target_pairs={{0,3},{1,2},{2,1},{3,0},{4,7},{5,6},{6,5},{7,4},{8,11},{9,10},{10,... | collective-permute-start | bytes 196616 | tf_op jit(solution)/shard_map/ppermute | solution.py:29
  37.8 0.0 collective-permute-done.11.refs_2_
  37.8 0.4 collective-permute-start.8
  38.2 0.0 collective-permute-done.12.refs_3_
  38.2 1.0 %collective-permute-start.18 = (bf16[80,1024]{1,0:T(8,128)(2,1)S(1)}, bf16[80,1024]{1,0:T(8,128)(2,1)S(1)}, u32[]{:S(2)}, u32[]{:S(2)}) collective-permute-start(bf16[80,1024]{1,0:T(8,128)(2,1)S(1)} %get-tuple-element.70), channel_id=1, source_target_pairs={{0,16},{4,20},{8,24},{12,28},{16,0},{20,4},{24,8},{28,12},{1,17},{... | collective-permute-start | bytes 491528 | tf_op jit(solution)/shard_map/ppermute | solution.py:29
  39.2 0.0 collective-permute-done.9.refs_2_
  39.2 0.8 %collective-permute-start.19 = (bf16[80,1024]{1,0:T(8,128)(2,1)S(1)}, bf16[80,1024]{1,0:T(8,128)(2,1)S(1)}, u32[]{:S(2)}, u32[]{:S(2)}) collective-permute-start(bf16[80,1024]{1,0:T(8,128)(2,1)S(1)} %get-tuple-element.71), channel_id=1, source_target_pairs={{0,24},{4,28},{8,16},{12,20},{16,8},{20,12},{24,0},{28,4},{1,25},{... | collective-permute-start | bytes 491528 | tf_op jit(solution)/shard_map/ppermute | solution.py:29
  40.0 1.5 %collective-permute-done.7.refs_0_ = bf16[32,1024]{1,0:T(8,128)(2,1)S(1)} collective-permute-done((bf16[32,1024]{1,0:T(8,128)(2,1)S(1)}, bf16[32,1024]{1,0:T(8,128)(2,1)S(1)}, u32[]{:S(2)}, u32[]{:S(2)}) %collective-permute-start.7) | collective-permute-done | bytes 65568 | tf_op jit(solution)/shard_map/ppermute | solution.py:29
  41.5 0.0 collective-permute-start.13
  41.5 2.2 %collective-permute-done.8.refs_1_ = bf16[32,1024]{1,0:T(8,128)(2,1)S(1)} collective-permute-done((bf16[32,1024]{1,0:T(8,128)(2,1)S(1)}, bf16[32,1024]{1,0:T(8,128)(2,1)S(1)}, u32[]{:S(2)}, u32[]{:S(2)}) %collective-permute-start.8) | collective-permute-done | bytes 65568 | tf_op jit(solution)/shard_map/ppermute | solution.py:29
  43.7 0.0 collective-permute-start.14
  43.7 0.0 collective-permute-done.17.refs_9_
  43.7 0.5 %collective-permute-start.15 = (bf16[64,1280]{1,0:T(8,128)(2,1)S(1)}, bf16[64,1280]{1,0:T(8,128)(2,1)S(1)}, u32[]{:S(2)}, u32[]{:S(2)}) collective-permute-start(bf16[64,1280]{1,0:T(8,128)(2,1)S(1)} %collective-permute-done.11.refs_2_), channel_id=1, source_target_pairs={{0,4},{4,0},{8,12},{12,8},{16,20},{20,16},{24,28},{28,24},{1,5},{5... | collective-permute-start | bytes 491528 | tf_op jit(solution)/shard_map/ppermute | solution.py:29
  44.2 1.8 %shard_map.123 = (bf16[512,1024]{1,0:T(8,128)(2,1)}, bf16[512,1024]{1,0:T(8,128)(2,1)}) custom-call(s32[4,16]{1,0:T(4,128)S(1)} %bitcast.3, bf16[32,1024]{1,0:T(8,128)(2,1)S(1)} %collective-permute-done.7.refs_0_, bf16[32,1024]{1,0:T(8,128)(2,1)S(1)} %collective-permute-done.8.refs_1_, bf16[32,1024]{1,0:T(8,128)(2,1)S(1)} %collective-permute-done.9.refs_2_, ...), custom_call_target="tpu_custom_call" | custom-call | tf_op jit(solution)/shard_map/pallas_call | solution.py:41
  46.0 0.0 collective-permute-done.18.refs_10_
  46.1 0.0 collective-permute-start.16
  46.1 0.0 collective-permute-done.19.refs_11_
  46.1 0.5 %collective-permute-start.20 = (bf16[80,1024]{1,0:T(8,128)(2,1)S(1)}, bf16[80,1024]{1,0:T(8,128)(2,1)S(1)}, u32[]{:S(2)}, u32[]{:S(2)}) collective-permute-start(bf16[80,1024]{1,0:T(8,128)(2,1)S(1)} %get-tuple-element.72.late_ref.refs_8_), channel_id=1, source_target_pairs={{0,4},{4,0},{8,12},{12,8},{16,20},{20,16},{24,28},{28,24},{1,5},{5... | collective-permute-start | bytes 491528 | tf_op jit(solution)/shard_map/ppermute | solution.py:29
  46.6 0.0 collective-permute-done.13.refs_4_
  46.6 0.1 collective-permute-start.21
  46.6 0.0 collective-permute-done.14.refs_5_
  46.6 0.4 collective-permute-start.22
  47.1 0.0 collective-permute-done.15.refs_6_
  47.1 0.1 collective-permute-start.23
  47.2 0.3 collective-permute-done.16.refs_7_
  47.4 0.2 collective-permute-done.20.refs_12_
  47.7 0.3 collective-permute-done.21.refs_13_
  48.0 0.2 collective-permute-done.22.refs_14_
  48.2 0.3 collective-permute-done.23.refs_15_
  48.5 1.4 %shard_map.124 = (f32[1,128,512]{2,1,0:T(8,128)}, f32[1,128,512]{2,1,0:T(8,128)}, f32[1,64,1024]{2,1,0:T(8,128)}, f32[1,1024]{1,0:T(1,128)}) custom-call(bf16[64,1280]{1,0:T(8,128)(2,1)S(1)} %get-tuple-element.65.refs_0_, bf16[64,1280]{1,0:T(8,128)(2,1)S(1)} %collective-permute-done.10.refs_1_, bf16[64,1280]{1,0:T(8,128)(2,1)S(1)} %collective-permute-done.11.refs_2_, ...), custom_call_target="tpu_custom_call" | custom-call | tf_op jit(solution)/shard_map/pallas_call | solution.py:41
  (10 shorter events, 0.1 us)
Async XLA Ops:
  0.6 1.2 %copy-start = (bf16[512,1024]{1,0:T(8,128)(2,1)S(1)}, bf16[512,1024]{1,0:T(8,128)(2,1)}, u32[]{:S(2)}) copy-start(bf16[512,1024]{1,0:T(8,128)(2,1)} %param.7) | copy-start | bytes 3145732
  1.9 0.9 %copy-start.1 = (bf16[1,128,512]{2,1,0:T(8,128)(2,1)S(1)}, bf16[1,128,512]{2,1,0:T(8,128)(2,1)}, u32[]{:S(2)}) copy-start(bf16[1,128,512]{2,1,0:T(8,128)(2,1)} %gate_ref) | copy-start | bytes 393220
  1.9 1.0 %copy-start.2 = (bf16[1,128,512]{2,1,0:T(8,128)(2,1)S(1)}, bf16[1,128,512]{2,1,0:T(8,128)(2,1)}, u32[]{:S(2)}) copy-start(bf16[1,128,512]{2,1,0:T(8,128)(2,1)} %up_ref) | copy-start | bytes 393220
  1.9 1.0 %copy-start.3 = (bf16[1,64,1024]{2,1,0:T(8,128)(2,1)S(1)}, bf16[1,64,1024]{2,1,0:T(8,128)(2,1)}, u32[]{:S(2)}) copy-start(bf16[1,64,1024]{2,1,0:T(8,128)(2,1)} %down_ref) | copy-start | bytes 393220
  2.9 13.9 %collective-permute-start.5 = (bf16[192,1024]{1,0:T(8,128)(2,1)S(1)}, bf16[192,1024]{1,0:T(8,128)(2,1)S(1)}, u32[]{:S(2)}, u32[]{:S(2)}) collective-permute-start(bf16[192,1024]{1,0:T(8,128)(2,1)S(1)} %shard_map.120.refs_3_), channel_id=1, source_target_pairs={{0,24},{4,28},{8,16},{12,20},{16,8},{20,12},{24,0},{28,4},{1,25},{... | collective-permute-start | bytes 1179656 | tf_op jit(solution)/shard_map/ppermute | solution.py:29
  6.9 17.5 %collective-permute-start.3 = (bf16[192,1024]{1,0:T(8,128)(2,1)S(1)}, bf16[192,1024]{1,0:T(8,128)(2,1)S(1)}, u32[]{:S(2)}, u32[]{:S(2)}) collective-permute-start(bf16[192,1024]{1,0:T(8,128)(2,1)S(1)} %shard_map.120.refs_3_), channel_id=1, source_target_pairs={{0,16},{4,20},{8,24},{12,28},{16,0},{20,4},{24,8},{28,12},{1,17},{... | collective-permute-start | bytes 1179656 | tf_op jit(solution)/shard_map/ppermute | solution.py:29
  7.4 17.3 %collective-permute-start.1 = (bf16[192,1024]{1,0:T(8,128)(2,1)S(1)}, bf16[192,1024]{1,0:T(8,128)(2,1)S(1)}, u32[]{:S(2)}, u32[]{:S(2)}) collective-permute-start(bf16[192,1024]{1,0:T(8,128)(2,1)S(1)} %shard_map.120.refs_3_), channel_id=1, source_target_pairs={{0,8},{4,12},{8,0},{12,4},{16,24},{20,28},{24,16},{28,20},{1,9},{5... | collective-permute-start | bytes 1179656 | tf_op jit(solution)/shard_map/ppermute | solution.py:29
  10.4 14.5 %copy-start.4 = (bf16[1,1024]{1,0:T(2,128)(2,1)S(1)}, bf16[1,1024]{1,0:T(2,128)(2,1)}, u32[]{:S(2)}) copy-start(bf16[1,1024]{1,0:T(2,128)(2,1)} %router_ref.3) | copy-start | bytes 6148
  10.4 14.5 %all-to-all-start = ((bf16[4,32,1024]{2,1,0:T(8,128)(2,1)}), bf16[4,32,1024]{2,1,0:T(8,128)(2,1)S(1)}, u32[]{:S(2)}, u32[]{:S(2)}) async-start(bf16[4,32,1024]{2,1,0:T(8,128)(2,1)} %shard_map.118), calls=%async_computation | async-start | bytes 524288 | tf_op jit(solution)/shard_map/all_to_all | solution.py:245
  15.8 11.0 %collective-permute-start = (bf16[192,1024]{1,0:T(8,128)(2,1)S(1)}, bf16[192,1024]{1,0:T(8,128)(2,1)S(1)}, u32[]{:S(2)}, u32[]{:S(2)}) collective-permute-start(bf16[192,1024]{1,0:T(8,128)(2,1)S(1)} %shard_map.120.refs_3_), channel_id=1, source_target_pairs={{0,4},{4,0},{8,12},{12,8},{16,20},{20,16},{24,28},{28,24},{1,5},{5... | collective-permute-start | bytes 1179656 | tf_op jit(solution)/shard_map/ppermute | solution.py:29
  16.9 10.7 %collective-permute-start.6 = (bf16[192,1024]{1,0:T(8,128)(2,1)S(1)}, bf16[192,1024]{1,0:T(8,128)(2,1)}, u32[]{:S(2)}, u32[]{:S(2)}) collective-permute-start(bf16[192,1024]{1,0:T(8,128)(2,1)S(1)} %collective-permute-done.5.refs_9_), channel_id=1, source_target_pairs={{0,4},{4,0},{8,12},{12,8},{16,20},{20,16},{24,28},{28,24},{1,5},{5... | collective-permute-start | bytes 1179656 | tf_op jit(solution)/shard_map/ppermute | solution.py:29
  24.4 4.2 %collective-permute-start.4 = (bf16[192,1024]{1,0:T(8,128)(2,1)S(1)}, bf16[192,1024]{1,0:T(8,128)(2,1)}, u32[]{:S(2)}, u32[]{:S(2)}) collective-permute-start(bf16[192,1024]{1,0:T(8,128)(2,1)S(1)} %collective-permute-done.3.refs_7_), channel_id=1, source_target_pairs={{0,4},{4,0},{8,12},{12,8},{16,20},{20,16},{24,28},{28,24},{1,5},{5... | collective-permute-start | bytes 1179656 | tf_op jit(solution)/shard_map/ppermute | solution.py:29
  24.7 3.9 %collective-permute-start.2 = (bf16[192,1024]{1,0:T(8,128)(2,1)S(1)}, bf16[192,1024]{1,0:T(8,128)(2,1)}, u32[]{:S(2)}, u32[]{:S(2)}) collective-permute-start(bf16[192,1024]{1,0:T(8,128)(2,1)S(1)} %collective-permute-done.1.refs_5_), channel_id=1, source_target_pairs={{0,4},{4,0},{8,12},{12,8},{16,20},{20,16},{24,28},{28,24},{1,5},{5... | collective-permute-start | bytes 1179656 | tf_op jit(solution)/shard_map/ppermute | solution.py:29
  25.1 10.3 %collective-permute-start.10 = (bf16[64,1280]{1,0:T(8,128)(2,1)S(1)}, bf16[64,1280]{1,0:T(8,128)(2,1)S(1)}, u32[]{:S(2)}, u32[]{:S(2)}) collective-permute-start(bf16[64,1280]{1,0:T(8,128)(2,1)S(1)} %get-tuple-element.62), channel_id=1, source_target_pairs={{0,8},{4,12},{8,0},{12,4},{16,24},{20,28},{24,16},{28,20},{1,9},{5... | collective-permute-start | bytes 491528 | tf_op jit(solution)/shard_map/ppermute | solution.py:29
  26.9 11.0 %collective-permute-start.11 = (bf16[64,1280]{1,0:T(8,128)(2,1)S(1)}, bf16[64,1280]{1,0:T(8,128)(2,1)S(1)}, u32[]{:S(2)}, u32[]{:S(2)}) collective-permute-start(bf16[64,1280]{1,0:T(8,128)(2,1)S(1)} %get-tuple-element.63), channel_id=1, source_target_pairs={{0,16},{4,20},{8,24},{12,28},{16,0},{20,4},{24,8},{28,12},{1,17},{... | collective-permute-start | bytes 491528 | tf_op jit(solution)/shard_map/ppermute | solution.py:29
  27.6 10.7 %collective-permute-start.12 = (bf16[64,1280]{1,0:T(8,128)(2,1)S(1)}, bf16[64,1280]{1,0:T(8,128)(2,1)S(1)}, u32[]{:S(2)}, u32[]{:S(2)}) collective-permute-start(bf16[64,1280]{1,0:T(8,128)(2,1)S(1)} %get-tuple-element.64), channel_id=1, source_target_pairs={{0,24},{4,28},{8,16},{12,20},{16,8},{20,12},{24,0},{28,4},{1,25},{... | collective-permute-start | bytes 491528 | tf_op jit(solution)/shard_map/ppermute | solution.py:29
  31.0 12.7 %collective-permute-start.17 = (bf16[80,1024]{1,0:T(8,128)(2,1)S(1)}, bf16[80,1024]{1,0:T(8,128)(2,1)S(1)}, u32[]{:S(2)}, u32[]{:S(2)}) collective-permute-start(bf16[80,1024]{1,0:T(8,128)(2,1)S(1)} %get-tuple-element.69), channel_id=1, source_target_pairs={{0,8},{4,12},{8,0},{12,4},{16,24},{20,28},{24,16},{28,20},{1,9},{5... | collective-permute-start | bytes 491528 | tf_op jit(solution)/shard_map/ppermute | solution.py:29
  33.7 5.5 %collective-permute-start.9 = (bf16[32,1024]{1,0:T(8,128)(2,1)S(1)}, bf16[32,1024]{1,0:T(8,128)(2,1)S(1)}, u32[]{:S(2)}, u32[]{:S(2)}) collective-permute-start(bf16[32,1024]{1,0:T(8,128)(2,1)S(1)} %get-tuple-element.57), channel_id=1, source_target_pairs={{0,1},{1,0},{2,3},{3,2},{4,5},{5,4},{6,7},{7,6},{8,9},{9,8},{10,11... | collective-permute-start | bytes 196616 | tf_op jit(solution)/shard_map/ppermute | solution.py:29
  35.4 6.1 %collective-permute-start.7 = (bf16[32,1024]{1,0:T(8,128)(2,1)S(1)}, bf16[32,1024]{1,0:T(8,128)(2,1)S(1)}, u32[]{:S(2)}, u32[]{:S(2)}) collective-permute-start(bf16[32,1024]{1,0:T(8,128)(2,1)S(1)} %get-tuple-element.55), channel_id=1, source_target_pairs={{0,3},{1,2},{2,1},{3,0},{4,7},{5,6},{6,5},{7,4},{8,11},{9,10},{10,... | collective-permute-start | bytes 196616 | tf_op jit(solution)/shard_map/ppermute | solution.py:29
  37.8 5.9 %collective-permute-start.8 = (bf16[32,1024]{1,0:T(8,128)(2,1)S(1)}, bf16[32,1024]{1,0:T(8,128)(2,1)S(1)}, u32[]{:S(2)}, u32[]{:S(2)}) collective-permute-start(bf16[32,1024]{1,0:T(8,128)(2,1)S(1)} %get-tuple-element.56), channel_id=1, source_target_pairs={{0,2},{1,3},{2,0},{3,1},{4,6},{5,7},{6,4},{7,5},{8,10},{9,11},{10,... | collective-permute-start | bytes 196616 | tf_op jit(solution)/shard_map/ppermute | solution.py:29
  38.2 7.8 %collective-permute-start.18 = (bf16[80,1024]{1,0:T(8,128)(2,1)S(1)}, bf16[80,1024]{1,0:T(8,128)(2,1)S(1)}, u32[]{:S(2)}, u32[]{:S(2)}) collective-permute-start(bf16[80,1024]{1,0:T(8,128)(2,1)S(1)} %get-tuple-element.70), channel_id=1, source_target_pairs={{0,16},{4,20},{8,24},{12,28},{16,0},{20,4},{24,8},{28,12},{1,17},{... | collective-permute-start | bytes 491528 | tf_op jit(solution)/shard_map/ppermute | solution.py:29
  39.2 6.8 %collective-permute-start.19 = (bf16[80,1024]{1,0:T(8,128)(2,1)S(1)}, bf16[80,1024]{1,0:T(8,128)(2,1)S(1)}, u32[]{:S(2)}, u32[]{:S(2)}) collective-permute-start(bf16[80,1024]{1,0:T(8,128)(2,1)S(1)} %get-tuple-element.71), channel_id=1, source_target_pairs={{0,24},{4,28},{8,16},{12,20},{16,8},{20,12},{24,0},{28,4},{1,25},{... | collective-permute-start | bytes 491528 | tf_op jit(solution)/shard_map/ppermute | solution.py:29
  40.0 4.2 %copy-start.5 = (s32[1,1,4,16]{3,2,1,0:T(4,128)S(1)}, s32[1,1,4,16]{3,2,1,0:T(4,128)}, u32[]{:S(2)}) copy-start(s32[1,1,4,16]{3,2,1,0:T(4,128)} %param.8) | copy-start | bytes 772
  41.5 5.1 %collective-permute-start.13 = (bf16[64,1280]{1,0:T(8,128)(2,1)S(1)}, bf16[64,1280]{1,0:T(8,128)(2,1)S(1)}, u32[]{:S(2)}, u32[]{:S(2)}) collective-permute-start(bf16[64,1280]{1,0:T(8,128)(2,1)S(1)} %get-tuple-element.65.refs_0_), channel_id=1, source_target_pairs={{0,4},{4,0},{8,12},{12,8},{16,20},{20,16},{24,28},{28,24},{1,5},{5... | collective-permute-start | bytes 491528 | tf_op jit(solution)/shard_map/ppermute | solution.py:29
  43.7 2.9 %collective-permute-start.14 = (bf16[64,1280]{1,0:T(8,128)(2,1)S(1)}, bf16[64,1280]{1,0:T(8,128)(2,1)S(1)}, u32[]{:S(2)}, u32[]{:S(2)}) collective-permute-start(bf16[64,1280]{1,0:T(8,128)(2,1)S(1)} %collective-permute-done.10.refs_1_), channel_id=1, source_target_pairs={{0,4},{4,0},{8,12},{12,8},{16,20},{20,16},{24,28},{28,24},{1,5},{5... | collective-permute-start | bytes 491528 | tf_op jit(solution)/shard_map/ppermute | solution.py:29
  43.7 3.4 %collective-permute-start.15 = (bf16[64,1280]{1,0:T(8,128)(2,1)S(1)}, bf16[64,1280]{1,0:T(8,128)(2,1)S(1)}, u32[]{:S(2)}, u32[]{:S(2)}) collective-permute-start(bf16[64,1280]{1,0:T(8,128)(2,1)S(1)} %collective-permute-done.11.refs_2_), channel_id=1, source_target_pairs={{0,4},{4,0},{8,12},{12,8},{16,20},{20,16},{24,28},{28,24},{1,5},{5... | collective-permute-start | bytes 491528 | tf_op jit(solution)/shard_map/ppermute | solution.py:29
  46.1 1.4 %collective-permute-start.16 = (bf16[64,1280]{1,0:T(8,128)(2,1)S(1)}, bf16[64,1280]{1,0:T(8,128)(2,1)S(1)}, u32[]{:S(2)}, u32[]{:S(2)}) collective-permute-start(bf16[64,1280]{1,0:T(8,128)(2,1)S(1)} %collective-permute-done.12.refs_3_), channel_id=1, source_target_pairs={{0,4},{4,0},{8,12},{12,8},{16,20},{20,16},{24,28},{28,24},{1,5},{5... | collective-permute-start | bytes 491528 | tf_op jit(solution)/shard_map/ppermute | solution.py:29
  46.1 1.6 %collective-permute-start.20 = (bf16[80,1024]{1,0:T(8,128)(2,1)S(1)}, bf16[80,1024]{1,0:T(8,128)(2,1)S(1)}, u32[]{:S(2)}, u32[]{:S(2)}) collective-permute-start(bf16[80,1024]{1,0:T(8,128)(2,1)S(1)} %get-tuple-element.72.late_ref.refs_8_), channel_id=1, source_target_pairs={{0,4},{4,0},{8,12},{12,8},{16,20},{20,16},{24,28},{28,24},{1,5},{5... | collective-permute-start | bytes 491528 | tf_op jit(solution)/shard_map/ppermute | solution.py:29
  46.6 1.4 %collective-permute-start.21 = (bf16[80,1024]{1,0:T(8,128)(2,1)S(1)}, bf16[80,1024]{1,0:T(8,128)(2,1)S(1)}, u32[]{:S(2)}, u32[]{:S(2)}) collective-permute-start(bf16[80,1024]{1,0:T(8,128)(2,1)S(1)} %collective-permute-done.17.refs_9_), channel_id=1, source_target_pairs={{0,4},{4,0},{8,12},{12,8},{16,20},{20,16},{24,28},{28,24},{1,5},{5... | collective-permute-start | bytes 491528 | tf_op jit(solution)/shard_map/ppermute | solution.py:29
  46.6 1.6 %collective-permute-start.22 = (bf16[80,1024]{1,0:T(8,128)(2,1)S(1)}, bf16[80,1024]{1,0:T(8,128)(2,1)S(1)}, u32[]{:S(2)}, u32[]{:S(2)}) collective-permute-start(bf16[80,1024]{1,0:T(8,128)(2,1)S(1)} %collective-permute-done.18.refs_10_), channel_id=1, source_target_pairs={{0,4},{4,0},{8,12},{12,8},{16,20},{20,16},{24,28},{28,24},{1,5},{5... | collective-permute-start | bytes 491528 | tf_op jit(solution)/shard_map/ppermute | solution.py:29
  47.1 1.4 %collective-permute-start.23 = (bf16[80,1024]{1,0:T(8,128)(2,1)S(1)}, bf16[80,1024]{1,0:T(8,128)(2,1)S(1)}, u32[]{:S(2)}, u32[]{:S(2)}) collective-permute-start(bf16[80,1024]{1,0:T(8,128)(2,1)S(1)} %collective-permute-done.19.refs_11_), channel_id=1, source_target_pairs={{0,4},{4,0},{8,12},{12,8},{16,20},{20,16},{24,28},{28,24},{1,5},{5... | collective-permute-start | bytes 491528 | tf_op jit(solution)/shard_map/ppermute | solution.py:29

commit v5 on v4

--- a/solution.py
+++ b/solution.py
@@ -64,22 +64,6 @@
         sent_ref[e, slots:, :] = d_ref[e * slots : (e + 1) * slots, :]
 
 
-def prepare(slots, experts, chips, block, router_ref, *refs):
-    got_ref, x_ref, d_ref, *out_refs = refs
-    me = lax.axis_index("expert")
-    for k in range(experts):
-        x_ref[k * slots : (k + 1) * slots, :] = got_ref[me ^ k, :slots, :]
-        d_ref[k * slots : (k + 1) * slots, :] = got_ref[me ^ k, slots:, :]
-    gate_val = gate_of(x_ref, router_ref)
-    back = (gate_val * d_ref[...].astype(F32)).astype(BF16)
-    width = back.shape[1]
-    mine = lax.axis_index("dp") // 2
-    for k, ref in enumerate(out_refs):
-        start = ((mine ^ k) * (width // chips)) // block * block
-        ref[:, :width] = back
-        ref[:, width:] = x_ref[:, pl.ds(pl.multiple_of(start, 128), block)]
-
-
 def gate_of(x_ref, router_ref):
     logit = jnp.sum(
         x_ref[...].astype(F32) * router_ref[...].astype(F32), axis=1, keepdims=True
@@ -87,15 +71,44 @@
     return jax.nn.sigmoid(logit)
 
 
-def hidden_part(slots, experts, chips, block, *refs):
+def prepare(slots, chips, block, got_ref, router_ref, x_ref, d_ref, mid_ref):
+    here = lax.axis_index("expert")
+    for k in range(got_ref.shape[0]):
+        x_ref[k * slots : (k + 1) * slots, :] = got_ref[here ^ k, :slots, :]
+        d_ref[k * slots : (k + 1) * slots, :] = got_ref[here ^ k, slots:, :]
+    gate_val = gate_of(x_ref, router_ref)
+    back = (gate_val * d_ref[...].astype(F32)).astype(BF16)
+    fill_mid(mid_ref, back, x_ref, chips, chips - 1, block)
+
+
+def fill_mid(ref, back, x_ref, chips, k, block):
+    tall, width = back.shape
+    each = tall * block // width
+    ref[:tall, :] = back
+    mine = lax.axis_index("dp") // 2
+    start = ((mine ^ k) * (width // chips)) // block * block
+    cut = x_ref[:, pl.ds(pl.multiple_of(start, 128), block)]
+    ref[tall : tall + each, :] = lines_of(cut, each)
+
+
+def lines_of(value, rows):
+    count = value.shape[0] // rows
+    return jnp.concatenate([value[i * rows : (i + 1) * rows, :] for i in range(count)], axis=1)
+
+
+def rows_of(lines, columns):
+    count = lines.shape[1] // columns
+    return [lines[:, i * columns : (i + 1) * columns] for i in range(count)]
+
+
+def hidden_part(slots, experts, chips, block, hidden_block, *refs):
     devices = 2 * chips
     x_ref, d_ref, router_ref = refs[:3]
     parts = refs[3 : 3 + devices]
     outs = refs[3 + devices :]
     late_refs = outs[:chips]
-    hidden_ref, logit_ref, gate_w, up_w, down_w = outs[chips:]
-    width = x_ref.shape[1]
-    half = gate_w.shape[1]
+    hidden_ref, logit_ref, gate_ref, gate_w, up_w, down_w = outs[chips:]
+    width, half = gate_w.shape
     rows = width // devices
     down_rows = half // devices
     me = lax.axis_index("dp")
@@ -107,6 +120,7 @@
         down_w[at, :] = parts[r][rows:, :]
     x = x_ref[...]
     d = d_ref[...]
+    tall = x.shape[0]
     gate_val = gate_of(x_ref, router_ref)
     act_gate = dot(x, gate_w[...])
     act_up = dot(x, up_w[...])
@@ -121,30 +135,30 @@
     grad_gate = (hidden_grad * act_up * sigma * (1.0 + act_gate * (1.0 - sigma))).astype(BF16)
     grad_up = (hidden_grad * silu).astype(BF16)
     logit_ref[...] = jnp.broadcast_to(logit_grad, logit_ref.shape)
+    gate_ref[...] = jnp.broadcast_to(gate_val, gate_ref.shape)
+    back = (gate_val * d.astype(F32)).astype(BF16)
     term = jnp.sum(logit_grad * x.astype(F32), axis=0, keepdims=True)
     high = term.astype(BF16).astype(F32)
     low = term - high
-    tall = x.shape[0]
-    tall = x.shape[0]
     mine = me // 2
-    parts = width // block
-    each = tall // parts
-    tail = late_refs[0].shape[0] - tall
+    hidden_each = tall * hidden_block // width
+    tail = late_refs[-1].shape[0] - tall
+    empty = jnp.zeros((tail - hidden_each - 2, width), F32)
     for k, ref in enumerate(late_refs):
-        start = ((mine ^ k) * (half // chips)) // block * block
-        cut = hidden_ref[:, pl.ds(pl.multiple_of(start, 128), block)].astype(F32)
-        lines = jnp.concatenate([cut[i * each : (i + 1) * each, :] for i in range(parts)], axis=1)
-        empty = jnp.zeros((tail - each - 2, width), F32)
-        ref[:tall, :half] = grad_gate
-        ref[:tall, half:] = grad_up
-        ref[tall:, :] = jnp.concatenate([lines, high, low, empty], axis=0).astype(BF16)
-
-
-def row_part(slots, x_ref, router_ref, late_ref, hidden_ref, logit_ref, gate_w, up_w, down_w, *outs):
-    tall = x_ref.shape[0]
-    half = gate_w.shape[1]
-    gate_val = gate_of(x_ref, router_ref)
-    out_rows = (gate_val * dot(hidden_ref[...], down_w[...])).astype(BF16)
+        at = ref.shape[0] - tail - tall
+        if at:
+            fill_mid(ref, back, x_ref, chips, k, block)
+        ref[at : at + tall, :half] = grad_gate
+        ref[at : at + tall, half:] = grad_up
+        start = ((mine ^ k) * (half // chips)) // hidden_block * hidden_block
+        cut = hidden_ref[:, pl.ds(pl.multiple_of(start, 128), hidden_block)].astype(F32)
+        lines = lines_of(cut, hidden_each)
+        ref[at + tall :, :] = jnp.concatenate([lines, high, low, empty], axis=0).astype(BF16)
+
+
+def row_part(slots, router_ref, late_ref, hidden_ref, logit_ref, gate_ref, gate_w, up_w, down_w, *outs):
+    tall, half = hidden_ref.shape
+    out_rows = (gate_ref[:, :1] * dot(hidden_ref[...], down_w[...])).astype(BF16)
     row_grads = dot_cols(late_ref[:tall, :half], gate_w[...])
     row_grads = row_grads + dot_cols(late_ref[:tall, half:], up_w[...])
     row_grads = (row_grads + logit_ref[:, :1] * router_ref[...].astype(F32)).astype(BF16)
@@ -153,35 +167,34 @@
         ref[slots:, :] = row_grads[k * slots : (k + 1) * slots, :]
 
 
-def weight_grads(chips, block, hidden_block, *refs):
+def weight_grads(tall, chips, block, hidden_block, *refs):
     devices = 2 * chips
-    mids, lates = refs[:devices], refs[devices : 2 * devices]
-    gate_ref, up_ref, down_ref, router_ref, sum_ref, down_sum_ref = refs[2 * devices :]
+    pairs, rest = [], list(refs)
+    for i in range(devices):
+        first = rest.pop(0)
+        pairs.append((first, rest.pop(0) if i % chips == chips - 1 else first))
+    gate_ref, up_ref, down_ref, router_ref, sum_ref, down_sum_ref = rest
     width = router_ref.shape[1]
     half = gate_ref.shape[2]
-    tall = mids[0].shape[0]
     scale = 1.0 / devices
-    parts = width // hidden_block
-    each = tall // parts
+    each = tall * block // width
+    hidden_each = tall * hidden_block // width
     me = lax.axis_index("dp")
     total = None
     count = devices if devices * tall <= 1024 else chips
     for c in range(devices // count):
-        mid = mids[c * count : (c + 1) * count]
-        late = lates[c * count : (c + 1) * count]
-        feats = jnp.concatenate([m[:, width:] for m in mid], axis=0)
-        backs = jnp.concatenate([m[:, :width] for m in mid], axis=0)
-        grads = jnp.concatenate([t[:tall, :] for t in late], axis=0)
+        mids = [m for m, _ in pairs[c * count : (c + 1) * count]]
+        lates = [(t, tall + each if m is t else 0) for m, t in pairs[c * count : (c + 1) * count]]
+        backs = jnp.concatenate([m[:tall, :] for m in mids], axis=0)
+        feats = jnp.concatenate(
+            [p for m in mids for p in rows_of(m[tall : tall + each, :], block)], axis=0
+        )
+        grads = jnp.concatenate([t[at : at + tall, :] for t, at in lates], axis=0)
         term = dot_rows(feats, grads)
         sum_ref[...] = term if c == 0 else sum_ref[...] + term
-        tails = [t[tall:, :].astype(F32) for t in late]
+        tails = [t[at + tall :, :].astype(F32) for t, at in lates]
         hidden = jnp.concatenate(
-            [
-                t[:each, i * hidden_block : (i + 1) * hidden_block]
-                for t in tails
-                for i in range(parts)
-            ],
-            axis=0,
+            [p for t in tails for p in rows_of(t[:hidden_each, :], hidden_block)], axis=0
         ).astype(BF16)
         term = dot_rows(hidden, backs)
         down_sum_ref[...] = term if c == 0 else down_sum_ref[...] + term
@@ -194,7 +207,8 @@
     rows = down_ref.shape[1]
     at = pl.ds(pl.multiple_of((me * rows) % hidden_block, rows), rows)
     down_ref[0] = down_sum_ref[at, :] * scale
-    router_ref[...] = (total[each : each + 1, :] + total[each + 1 : each + 2, :]) * scale
+    line = total[hidden_each : hidden_each + 1, :] + total[hidden_each + 1 : hidden_each + 2, :]
+    router_ref[...] = line * scale
 
 
 def combine(slots, chosen_ref, *refs):
@@ -242,21 +256,22 @@
         jax.ShapeDtypeStruct((experts, 2 * slots, width), BF16),
         (x_sent, d_sent),
     )
-    got = [lax.all_to_all(sent, "expert", 0, 0, tiled=True)]
-    x_rows, d_rows, *mids = call(
-        functools.partial(prepare, slots, experts, chips, block),
-        (shape(taken, width, BF16),) * 2 + (shape(taken, width + block, BF16),) * chips,
-        (router, *got),
-    )
-    mids = [mids[0]] + [swap(mids[k], "dp", 2 * k) for k in range(1, chips)]
-
-    lines = taken * hidden_block // width
-    late_rows = taken + -(-(lines + 2) // 16) * 16
+    got = lax.all_to_all(sent, "expert", 0, 0, tiled=True)
+    mid_rows = taken + taken * block // width
+    late_rows = taken + -(-(taken * hidden_block // width + 2) // 16) * 16
+    x_rows, d_rows, far_mid = call(
+        functools.partial(prepare, slots, chips, block),
+        (shape(taken, width, BF16),) * 2 + (shape(mid_rows, width, BF16),),
+        (got, router),
+    )
+    far_mid = swap(far_mid, "dp", devices - 2)
     outs = call(
-        functools.partial(hidden_part, slots, experts, chips, hidden_block),
-        (shape(late_rows, width, BF16),) * chips
+        functools.partial(hidden_part, slots, experts, chips, block, hidden_block),
+        (shape(mid_rows + late_rows, width, BF16),) * (chips - 1)
+        + (shape(late_rows, width, BF16),)
         + (
             shape(taken, half, BF16),
+            shape(taken, 128, F32),
             shape(taken, 128, F32),
             shape(width, half, BF16),
             shape(width, half, BF16),
@@ -269,10 +284,12 @@
     returned = call(
         functools.partial(row_part, slots),
         (shape(2 * slots, width, BF16),) * experts,
-        (x_rows, router, lates[0], *outs[chips:]),
+        (router, lates[-1], *outs[chips:]),
         limit=16 if taken <= 64 else 40,
     )
-    own_late = lates[0]
+    other_mid = swap(far_mid, "dp", 1)
+    returned = list(returned)
+    returned[-1] = after(returned[-1:], other_mid)[0]
     returned = [returned[0]] + [swap(returned[k], "expert", k) for k in range(experts - 1, 0, -1)][::-1]
     mixed, grad_tokens = call(
         functools.partial(combine, slots),
@@ -281,20 +298,19 @@
         [pltpu.VMEM((taken, width), BF16)] * 2,
     )
     lates = [lates[0]] + [swap(lates[k], "dp", 2 * k) for k in range(1, chips)]
-    mids = after(mids, returned[1])
-    mids = mids + [swap(m, "dp", 1) for m in mids]
-    near = after(lates[:-1], *returned)
-    far = after(lates[-1:], mixed)
-    lates = lates + [swap(t, "dp", 1) for t in near + far]
+    own_late = swap(lates[0], "dp", 1)
+    lates = after(lates[:-1], *returned) + after(lates[-1:], mixed)
+    others = [own_late] + [swap(t, "dp", 1) for t in lates[1:]]
+    lates = lates[:-1] + [far_mid, lates[-1]] + others[:-1] + [other_mid, others[-1]]
     grad_gate, grad_up, grad_down, grad_router = call(
-        functools.partial(weight_grads, chips, block, hidden_block),
+        functools.partial(weight_grads, taken, chips, block, hidden_block),
         (
             jax.ShapeDtypeStruct(w_gate.shape, F32),
             jax.ShapeDtypeStruct(w_up.shape, F32),
             jax.ShapeDtypeStruct(w_down.shape, F32),
             jax.ShapeDtypeStruct(router.shape, F32),
         ),
-        (*mids, *lates),
+        (*lates,),
         [pltpu.VMEM((block, 2 * half), F32), pltpu.VMEM((hidden_block, width), F32)],
         limit=16 if taken <= 64 else 40,
     )

time: 50.2 us -> 50 us (level)
  starting transfers between devices: 23.4 us -> 21.2 us
  waiting for transfers between devices: 14 us -> 15.7 us
    ppermute x24 -> x19, starting transfers between devices: 18 us -> 15.7 us  [swap(): return lax.ppermute(value, axis, [(i, i ^ step) for i in range(size)])]
    ppermute x24 -> x19, waiting for transfers between devices: 14 us -> 15.7 us  [swap(): return lax.ppermute(value, axis, [(i, i ^ step) for i in range(size)])]
  transfers between devices with their start and end apart: 25 -> 20, of which waited for: 10 -> 9; matrix products, arithmetic and copies ran while one was open for 4% -> 4% of each run, Pallas kernels for 12% -> 12%
where the time goes in v5:
time: 50 us; the launch traced here: 49.4 us
  starting transfers between devices  21.2 us (42%)
  waiting for transfers between devices  15.7 us (31%)
  Pallas kernels  7.33 us (15%)
  local copies, waits for them, and re-layouts  4.42 us (9%)
  between operations  0.72 us (1%)
    ppermute x19, waiting for transfers between devices, swap(): return lax.ppermute(value, axis, [(i, i ^ step) for i in range(size)])  15.7 us
    ppermute x19, starting transfers between devices, swap(): return lax.ppermute(value, axis, [(i, i ^ step) for i in range(size)])  15.7 us
    pallas_call x7, Pallas kernels, call(): pl.pallas_call(body, out_shape=out_shape, in_specs=[VMEM] * len(args), ou...  7.33 us
    all_to_all x1, starting transfers between devices, local(): got = lax.all_to_all(sent, 'expert', 0, 0, tiled=True)  5.46 us
    gather x1, local copies, waits for them, and re-layouts, local(): d_sent = cotangent.at[flat].get(mode='promise_in_bounds')  2.15 us
  transfers between devices with their start and end apart: 20, of which 9 were waited for; matrix products, arithmetic and copies ran while one was open for 4% of the time, Pallas kernels for 12%

profile of v5, /device:TPU:0, one launch (start us, length us, event | category | flops | bytes accessed | tf_op | source)
XLA Modules:
  0.0 49.4 jit_solution(4077805743715404743)
XLA Ops:
  0.6 0.0 copy-start
  0.6 0.9 %reshape.43 = s32[64,1]{0,1:T(1,128)S(1)} reshape(s32[1,1,4,16]{3,2,1,0:T(4,128)} %param.8) | data formatting | bytes 512 | tf_op jit(solution)/shard_map/reshape | solution.py:241
  1.5 0.4 copy-done
  1.9 0.0 copy-start.1
  1.9 0.0 copy-start.2
  1.9 0.0 copy-start.3
  1.9 0.7 %gather_fusion = bf16[64,1024]{1,0:T(8,128)(2,1)S(1)} fusion(bf16[512,1024]{1,0:T(8,128)(2,1)S(1)} %copy-done, s32[1024]{0:T(1024)S(1)} %pad_clamp_fusion), kind=kCustom, calls=%fused_computation | custom fusion | bytes 262400 | tf_op jit(solution)/shard_map/gather | solution.py:242
  2.6 0.2 copy-done.1
  2.8 0.1 copy-done.2
  2.8 0.1 copy-done.3
  2.9 3.0 %collective-permute-start.1 = (bf16[192,1024]{1,0:T(8,128)(2,1)S(1)}, bf16[192,1024]{1,0:T(8,128)(2,1)S(1)}, u32[]{:S(2)}, u32[]{:S(2)}) collective-permute-start(bf16[192,1024]{1,0:T(8,128)(2,1)S(1)} %shard_map.120.refs_3_), channel_id=1, source_target_pairs={{0,8},{4,12},{8,0},{12,4},{16,24},{20,28},{24,16},{28,20},{1,9},{5... | collective-permute-start | bytes 1179656 | tf_op jit(solution)/shard_map/ppermute | solution.py:29
  5.9 1.5 %collective-permute-start.3 = (bf16[192,1024]{1,0:T(8,128)(2,1)S(1)}, bf16[192,1024]{1,0:T(8,128)(2,1)S(1)}, u32[]{:S(2)}, u32[]{:S(2)}) collective-permute-start(bf16[192,1024]{1,0:T(8,128)(2,1)S(1)} %shard_map.120.refs_3_), channel_id=1, source_target_pairs={{0,16},{4,20},{8,24},{12,28},{16,0},{20,4},{24,8},{28,12},{1,17},{... | collective-permute-start | bytes 1179656 | tf_op jit(solution)/shard_map/ppermute | solution.py:29
  7.5 0.0 collective-permute-start.5
  7.5 2.2 %gather_fusion.1 = bf16[64,1024]{1,0:T(8,128)(2,1)S(1)} fusion(bf16[512,1024]{1,0:T(8,128)(2,1)} %param.13, s32[1024]{0:T(1024)S(1)} %pad_clamp_fusion), kind=kCustom, calls=%fused_computation.1 | custom fusion | bytes 262400 | tf_op jit(solution)/shard_map/gather | solution.py:243
  9.6 0.7 %shard_map.118 = bf16[4,32,1024]{2,1,0:T(8,128)(2,1)} custom-call(bf16[64,1024]{1,0:T(8,128)(2,1)S(1)} %gather_fusion, bf16[64,1024]{1,0:T(8,128)(2,1)S(1)} %gather_fusion.1), custom_call_target="tpu_custom_call" | custom-call | tf_op jit(solution)/shard_map/pallas_call | solution.py:41
  10.4 0.0 copy-start.4
  10.4 5.5 %all-to-all-start = ((bf16[4,32,1024]{2,1,0:T(8,128)(2,1)}), bf16[4,32,1024]{2,1,0:T(8,128)(2,1)S(1)}, u32[]{:S(2)}, u32[]{:S(2)}) async-start(bf16[4,32,1024]{2,1,0:T(8,128)(2,1)} %shard_map.118), calls=%async_computation | async-start | bytes 524288 | tf_op jit(solution)/shard_map/all_to_all | solution.py:259
  15.8 0.0 collective-permute-start
  15.8 0.1 collective-permute-done.1.refs_5_
  15.9 0.5 collective-permute-start.2
  16.3 8.6 %collective-permute-done.3.refs_7_ = bf16[192,1024]{1,0:T(8,128)(2,1)S(1)} collective-permute-done((bf16[192,1024]{1,0:T(8,128)(2,1)S(1)}, bf16[192,1024]{1,0:T(8,128)(2,1)S(1)}, u32[]{:S(2)}, u32[]{:S(2)}) %collective-permute-start.3) | collective-permute-done | bytes 393248 | tf_op jit(solution)/shard_map/ppermute | solution.py:29
  24.9 0.0 collective-permute-start.4
  24.9 0.0 collective-permute-done.5.refs_9_
  25.0 0.5 %collective-permute-start.6 = (bf16[192,1024]{1,0:T(8,128)(2,1)S(1)}, bf16[192,1024]{1,0:T(8,128)(2,1)}, u32[]{:S(2)}, u32[]{:S(2)}) collective-permute-start(bf16[192,1024]{1,0:T(8,128)(2,1)S(1)} %collective-permute-done.5.refs_9_), channel_id=1, source_target_pairs={{0,4},{4,0},{8,12},{12,8},{16,20},{20,16},{24,28},{28,24},{1,5},{5... | collective-permute-start | bytes 1179656 | tf_op jit(solution)/shard_map/ppermute | solution.py:29
  25.5 0.0 all-to-all-done.got_ref
  25.5 0.0 copy-done.4
  25.5 0.1 shard_map.119
  25.6 1.6 %collective-permute-start.7 = (bf16[80,1024]{1,0:T(8,128)(2,1)S(1)}, bf16[80,1024]{1,0:T(8,128)(2,1)S(1)}, u32[]{:S(2)}, u32[]{:S(2)}) collective-permute-start(bf16[80,1024]{1,0:T(8,128)(2,1)S(1)} %get-tuple-element.52), channel_id=1, source_target_pairs={{0,24},{4,28},{8,16},{12,20},{16,8},{20,12},{24,0},{28,4},{1,25},{... | collective-permute-start | bytes 491528 | tf_op jit(solution)/shard_map/ppermute | solution.py:29
  27.1 0.0 collective-permute-done.refs_4_
  27.2 0.0 collective-permute-done.2.refs_6_
  27.2 0.0 collective-permute-done.4.refs_8_
  27.2 0.2 collective-permute-done.6.refs_10_
  27.4 2.4 %shard_map.121 = (bf16[160,1024]{1,0:T(8,128)(2,1)S(1)}, bf16[160,1024]{1,0:T(8,128)(2,1)S(1)}, bf16[160,1024]{1,0:T(8,128)(2,1)S(1)}, bf16[80,1024]{1,0:T(8,128...) custom-call(bf16[64,1024]{1,0:T(8,128)(2,1)S(1)} %get-tuple-element., ...), custom_call_target="tpu_custom_call" | custom-call | tf_op jit(solution)/shard_map/pallas_call | solution.py:41
  29.7 1.4 %collective-permute-start.12 = (bf16[160,1024]{1,0:T(8,128)(2,1)S(1)}, bf16[160,1024]{1,0:T(8,128)(2,1)S(1)}, u32[]{:S(2)}, u32[]{:S(2)}) collective-permute-start(bf16[160,1024]{1,0:T(8,128)(2,1)S(1)} %get-tuple-element.60), channel_id=1, source_target_pairs={{0,8},{4,12},{8,0},{12,4},{16,24},{20,28},{24,16},{28,20},{1,9},{5... | collective-permute-start | bytes 983048 | tf_op jit(solution)/shard_map/ppermute | solution.py:29
  31.1 0.7 %collective-permute-start.13 = (bf16[160,1024]{1,0:T(8,128)(2,1)S(1)}, bf16[160,1024]{1,0:T(8,128)(2,1)S(1)}, u32[]{:S(2)}, u32[]{:S(2)}) collective-permute-start(bf16[160,1024]{1,0:T(8,128)(2,1)S(1)} %get-tuple-element.61), channel_id=1, source_target_pairs={{0,16},{4,20},{8,24},{12,28},{16,0},{20,4},{24,8},{28,12},{1,17},{... | collective-permute-start | bytes 983048 | tf_op jit(solution)/shard_map/ppermute | solution.py:29
  31.8 0.8 %collective-permute-done.7.refs_3_ = bf16[80,1024]{1,0:T(8,128)(2,1)S(1)} collective-permute-done((bf16[80,1024]{1,0:T(8,128)(2,1)S(1)}, bf16[80,1024]{1,0:T(8,128)(2,1)S(1)}, u32[]{:S(2)}, u32[]{:S(2)}) %collective-permute-start.7) | collective-permute-done | bytes 163872 | tf_op jit(solution)/shard_map/ppermute | solution.py:29
  32.7 0.0 collective-permute-start.8
  32.7 0.9 %shard_map.122 = (bf16[32,1024]{1,0:T(8,128)(2,1)S(1)}, bf16[32,1024]{1,0:T(8,128)(2,1)S(1)}, bf16[32,1024]{1,0:T(8,128)(2,1)S(1)}, bf16[32,1024]{1,0:T(8,128)(2,1)S(1)}) custom-call(bf16[1,1024]{1,0:T(2,128)(2,1)S(1)} %copy-done.4, bf16[80,1024]{1,0:T(8,128)(2,1)S(1)} %get-tuple-element.44.late_ref, bf16[64,512]{1,0:T(8,128)(2,1)S(1)} %get-tuple-element.45.hidden_ref, ...), custom_call_target="tpu_custom_call" | custom-call | tf_op jit(solution)/shard_map/pallas_call | solution.py:41
  33.6 0.5 collective-permute-done.8.refs_8_
  34.1 3.6 %collective-permute-start.9 = (bf16[32,1024]{1,0:T(8,128)(2,1)S(1)}, bf16[32,1024]{1,0:T(8,128)(2,1)S(1)}, u32[]{:S(2)}, u32[]{:S(2)}) collective-permute-start(bf16[32,1024]{1,0:T(8,128)(2,1)S(1)} %get-tuple-element.53), channel_id=1, source_target_pairs={{0,3},{1,2},{2,1},{3,0},{4,7},{5,6},{6,5},{7,4},{8,11},{9,10},{10,... | collective-permute-start | bytes 196616 | tf_op jit(solution)/shard_map/ppermute | solution.py:29
  37.7 0.0 collective-permute-start.10
  37.7 0.8 %collective-permute-start.11 = (bf16[32,1024]{1,0:T(8,128)(2,1)S(1)}, bf16[32,1024]{1,0:T(8,128)(2,1)S(1)}, u32[]{:S(2)}, u32[]{:S(2)}) collective-permute-start(bf16[32,1024]{1,0:T(8,128)(2,1)S(1)} %get-tuple-element.55), channel_id=1, source_target_pairs={{0,1},{1,0},{2,3},{3,2},{4,5},{5,4},{6,7},{7,6},{8,9},{9,8},{10,11... | collective-permute-start | bytes 196616 | tf_op jit(solution)/shard_map/ppermute | solution.py:29
  38.5 1.9 %collective-permute-done.9.refs_0_ = bf16[32,1024]{1,0:T(8,128)(2,1)S(1)} collective-permute-done((bf16[32,1024]{1,0:T(8,128)(2,1)S(1)}, bf16[32,1024]{1,0:T(8,128)(2,1)S(1)}, u32[]{:S(2)}, u32[]{:S(2)}) %collective-permute-start.9) | collective-permute-done | bytes 65568 | tf_op jit(solution)/shard_map/ppermute | solution.py:29
  40.4 1.5 %collective-permute-start.14 = (bf16[80,1024]{1,0:T(8,128)(2,1)S(1)}, bf16[80,1024]{1,0:T(8,128)(2,1)S(1)}, u32[]{:S(2)}, u32[]{:S(2)}) collective-permute-start(bf16[80,1024]{1,0:T(8,128)(2,1)S(1)} %get-tuple-element.44.late_ref), channel_id=1, source_target_pairs={{0,24},{4,28},{8,16},{12,20},{16,8},{20,12},{24,0},{28,4},{1,25},{... | collective-permute-start | bytes 491528 | tf_op jit(solution)/shard_map/ppermute | solution.py:29
  41.9 1.7 %collective-permute-done.10.refs_1_ = bf16[32,1024]{1,0:T(8,128)(2,1)S(1)} collective-permute-done((bf16[32,1024]{1,0:T(8,128)(2,1)S(1)}, bf16[32,1024]{1,0:T(8,128)(2,1)S(1)}, u32[]{:S(2)}, u32[]{:S(2)}) %collective-permute-start.10) | collective-permute-done | bytes 65568 | tf_op jit(solution)/shard_map/ppermute | solution.py:29
  43.6 0.0 copy-start.5
  43.6 0.0 collective-permute-start.15
  43.6 0.0 collective-permute-done.11.refs_2_
  43.6 0.0 collective-permute-done.12.refs_1_
  43.6 0.0 collective-permute-done.13.refs_2_
  43.6 0.6 %collective-permute-start.16 = (bf16[160,1024]{1,0:T(8,128)(2,1)S(1)}, bf16[160,1024]{1,0:T(8,128)(2,1)S(1)}, u32[]{:S(2)}, u32[]{:S(2)}) collective-permute-start(bf16[160,1024]{1,0:T(8,128)(2,1)S(1)} %collective-permute-done.12.refs_1_), channel_id=1, source_target_pairs={{0,4},{4,0},{8,12},{12,8},{16,20},{20,16},{24,28},{28,24},{1,5},{5... | collective-permute-start | bytes 983048 | tf_op jit(solution)/shard_map/ppermute | solution.py:29
  44.2 0.1 collective-permute-start.17
  44.2 0.0 copy-done.5
  44.2 1.8 %shard_map.123 = (bf16[512,1024]{1,0:T(8,128)(2,1)}, bf16[512,1024]{1,0:T(8,128)(2,1)}) custom-call(s32[4,16]{1,0:T(4,128)S(1)} %bitcast.3, bf16[32,1024]{1,0:T(8,128)(2,1)S(1)} %collective-permute-done.9.refs_0_, bf16[32,1024]{1,0:T(8,128)(2,1)S(1)} %collective-permute-done.10.refs_1_, bf16[32,1024]{1,0:T(8,128)(2,1)S(1)} %collective-permute-done.11.refs_2_, ...), custom_call_target="tpu_custom_call" | custom-call | tf_op jit(solution)/shard_map/pallas_call | solution.py:41
  46.0 0.6 %collective-permute-done.14.refs_4_ = bf16[80,1024]{1,0:T(8,128)(2,1)S(1)} collective-permute-done((bf16[80,1024]{1,0:T(8,128)(2,1)S(1)}, bf16[80,1024]{1,0:T(8,128)(2,1)S(1)}, u32[]{:S(2)}, u32[]{:S(2)}) %collective-permute-start.14) | collective-permute-done | bytes 163872 | tf_op jit(solution)/shard_map/ppermute | solution.py:29
  46.6 0.0 collective-permute-start.18
  46.6 1.4 %collective-permute-done.18.refs_9_ = bf16[80,1024]{1,0:T(8,128)(2,1)S(1)} collective-permute-done((bf16[80,1024]{1,0:T(8,128)(2,1)S(1)}, bf16[80,1024]{1,0:T(8,128)(2,1)S(1)}, u32[]{:S(2)}, u32[]{:S(2)}) %collective-permute-start.18) | collective-permute-done | bytes 163872 | tf_op jit(solution)/shard_map/ppermute | solution.py:29
  48.0 0.0 collective-permute-done.15.refs_5_
  48.0 0.0 collective-permute-done.16.refs_6_
  48.0 0.0 collective-permute-done.17.refs_7_
  48.0 1.4 %shard_map.124 = (f32[1,128,512]{2,1,0:T(8,128)}, f32[1,128,512]{2,1,0:T(8,128)}, f32[1,64,1024]{2,1,0:T(8,128)}, f32[1,1024]{1,0:T(1,128)}) custom-call(bf16[160,1024]{1,0:T(8,128)(2,1)S(1)} %get-tuple-element.62.refs_0_, bf16[160,1024]{1,0:T(8,128)(2,1)S(1)} %collective-permute-done.12.refs_1_, bf16[160,1024]{1,0:T(8,128)(2,1)S(1)} %collective-permute-done.13.refs_2_, ...), custom_call_target="tpu_custom_call" | custom-call | tf_op jit(solution)/shard_map/pallas_call | solution.py:41
  (3 shorter events, 0.0 us)
Async XLA Ops:
  0.6 1.2 %copy-start = (bf16[512,1024]{1,0:T(8,128)(2,1)S(1)}, bf16[512,1024]{1,0:T(8,128)(2,1)}, u32[]{:S(2)}) copy-start(bf16[512,1024]{1,0:T(8,128)(2,1)} %param.7) | copy-start | bytes 3145732
  1.9 0.9 %copy-start.1 = (bf16[1,128,512]{2,1,0:T(8,128)(2,1)S(1)}, bf16[1,128,512]{2,1,0:T(8,128)(2,1)}, u32[]{:S(2)}) copy-start(bf16[1,128,512]{2,1,0:T(8,128)(2,1)} %gate_ref) | copy-start | bytes 393220
  1.9 1.0 %copy-start.2 = (bf16[1,128,512]{2,1,0:T(8,128)(2,1)S(1)}, bf16[1,128,512]{2,1,0:T(8,128)(2,1)}, u32[]{:S(2)}) copy-start(bf16[1,128,512]{2,1,0:T(8,128)(2,1)} %up_ref) | copy-start | bytes 393220
  1.9 1.0 %copy-start.3 = (bf16[1,64,1024]{2,1,0:T(8,128)(2,1)S(1)}, bf16[1,64,1024]{2,1,0:T(8,128)(2,1)}, u32[]{:S(2)}) copy-start(bf16[1,64,1024]{2,1,0:T(8,128)(2,1)} %down_ref) | copy-start | bytes 393220
  2.9 12.9 %collective-permute-start.1 = (bf16[192,1024]{1,0:T(8,128)(2,1)S(1)}, bf16[192,1024]{1,0:T(8,128)(2,1)S(1)}, u32[]{:S(2)}, u32[]{:S(2)}) collective-permute-start(bf16[192,1024]{1,0:T(8,128)(2,1)S(1)} %shard_map.120.refs_3_), channel_id=1, source_target_pairs={{0,8},{4,12},{8,0},{12,4},{16,24},{20,28},{24,16},{28,20},{1,9},{5... | collective-permute-start | bytes 1179656 | tf_op jit(solution)/shard_map/ppermute | solution.py:29
  5.9 19.0 %collective-permute-start.3 = (bf16[192,1024]{1,0:T(8,128)(2,1)S(1)}, bf16[192,1024]{1,0:T(8,128)(2,1)S(1)}, u32[]{:S(2)}, u32[]{:S(2)}) collective-permute-start(bf16[192,1024]{1,0:T(8,128)(2,1)S(1)} %shard_map.120.refs_3_), channel_id=1, source_target_pairs={{0,16},{4,20},{8,24},{12,28},{16,0},{20,4},{24,8},{28,12},{1,17},{... | collective-permute-start | bytes 1179656 | tf_op jit(solution)/shard_map/ppermute | solution.py:29
  7.5 17.5 %collective-permute-start.5 = (bf16[192,1024]{1,0:T(8,128)(2,1)S(1)}, bf16[192,1024]{1,0:T(8,128)(2,1)S(1)}, u32[]{:S(2)}, u32[]{:S(2)}) collective-permute-start(bf16[192,1024]{1,0:T(8,128)(2,1)S(1)} %shard_map.120.refs_3_), channel_id=1, source_target_pairs={{0,24},{4,28},{8,16},{12,20},{16,8},{20,12},{24,0},{28,4},{1,25},{... | collective-permute-start | bytes 1179656 | tf_op jit(solution)/shard_map/ppermute | solution.py:29
  10.4 15.1 %copy-start.4 = (bf16[1,1024]{1,0:T(2,128)(2,1)S(1)}, bf16[1,1024]{1,0:T(2,128)(2,1)}, u32[]{:S(2)}) copy-start(bf16[1,1024]{1,0:T(2,128)(2,1)} %router_ref.3) | copy-start | bytes 6148
  10.4 15.1 %all-to-all-start = ((bf16[4,32,1024]{2,1,0:T(8,128)(2,1)}), bf16[4,32,1024]{2,1,0:T(8,128)(2,1)S(1)}, u32[]{:S(2)}, u32[]{:S(2)}) async-start(bf16[4,32,1024]{2,1,0:T(8,128)(2,1)} %shard_map.118), calls=%async_computation | async-start | bytes 524288 | tf_op jit(solution)/shard_map/all_to_all | solution.py:259
  15.8 11.3 %collective-permute-start = (bf16[192,1024]{1,0:T(8,128)(2,1)S(1)}, bf16[192,1024]{1,0:T(8,128)(2,1)S(1)}, u32[]{:S(2)}, u32[]{:S(2)}) collective-permute-start(bf16[192,1024]{1,0:T(8,128)(2,1)S(1)} %shard_map.120.refs_3_), channel_id=1, source_target_pairs={{0,4},{4,0},{8,12},{12,8},{16,20},{20,16},{24,28},{28,24},{1,5},{5... | collective-permute-start | bytes 1179656 | tf_op jit(solution)/shard_map/ppermute | solution.py:29
  15.9 11.3 %collective-permute-start.2 = (bf16[192,1024]{1,0:T(8,128)(2,1)S(1)}, bf16[192,1024]{1,0:T(8,128)(2,1)}, u32[]{:S(2)}, u32[]{:S(2)}) collective-permute-start(bf16[192,1024]{1,0:T(8,128)(2,1)S(1)} %collective-permute-done.1.refs_5_), channel_id=1, source_target_pairs={{0,4},{4,0},{8,12},{12,8},{16,20},{20,16},{24,28},{28,24},{1,5},{5... | collective-permute-start | bytes 1179656 | tf_op jit(solution)/shard_map/ppermute | solution.py:29
  24.9 2.2 %collective-permute-start.4 = (bf16[192,1024]{1,0:T(8,128)(2,1)S(1)}, bf16[192,1024]{1,0:T(8,128)(2,1)}, u32[]{:S(2)}, u32[]{:S(2)}) collective-permute-start(bf16[192,1024]{1,0:T(8,128)(2,1)S(1)} %collective-permute-done.3.refs_7_), channel_id=1, source_target_pairs={{0,4},{4,0},{8,12},{12,8},{16,20},{20,16},{24,28},{28,24},{1,5},{5... | collective-permute-start | bytes 1179656 | tf_op jit(solution)/shard_map/ppermute | solution.py:29
  25.0 2.4 %collective-permute-start.6 = (bf16[192,1024]{1,0:T(8,128)(2,1)S(1)}, bf16[192,1024]{1,0:T(8,128)(2,1)}, u32[]{:S(2)}, u32[]{:S(2)}) collective-permute-start(bf16[192,1024]{1,0:T(8,128)(2,1)S(1)} %collective-permute-done.5.refs_9_), channel_id=1, source_target_pairs={{0,4},{4,0},{8,12},{12,8},{16,20},{20,16},{24,28},{28,24},{1,5},{5... | collective-permute-start | bytes 1179656 | tf_op jit(solution)/shard_map/ppermute | solution.py:29
  25.6 7.1 %collective-permute-start.7 = (bf16[80,1024]{1,0:T(8,128)(2,1)S(1)}, bf16[80,1024]{1,0:T(8,128)(2,1)S(1)}, u32[]{:S(2)}, u32[]{:S(2)}) collective-permute-start(bf16[80,1024]{1,0:T(8,128)(2,1)S(1)} %get-tuple-element.52), channel_id=1, source_target_pairs={{0,24},{4,28},{8,16},{12,20},{16,8},{20,12},{24,0},{28,4},{1,25},{... | collective-permute-start | bytes 491528 | tf_op jit(solution)/shard_map/ppermute | solution.py:29
  29.7 13.9 %collective-permute-start.12 = (bf16[160,1024]{1,0:T(8,128)(2,1)S(1)}, bf16[160,1024]{1,0:T(8,128)(2,1)S(1)}, u32[]{:S(2)}, u32[]{:S(2)}) collective-permute-start(bf16[160,1024]{1,0:T(8,128)(2,1)S(1)} %get-tuple-element.60), channel_id=1, source_target_pairs={{0,8},{4,12},{8,0},{12,4},{16,24},{20,28},{24,16},{28,20},{1,9},{5... | collective-permute-start | bytes 983048 | tf_op jit(solution)/shard_map/ppermute | solution.py:29
  31.1 12.5 %collective-permute-start.13 = (bf16[160,1024]{1,0:T(8,128)(2,1)S(1)}, bf16[160,1024]{1,0:T(8,128)(2,1)S(1)}, u32[]{:S(2)}, u32[]{:S(2)}) collective-permute-start(bf16[160,1024]{1,0:T(8,128)(2,1)S(1)} %get-tuple-element.61), channel_id=1, source_target_pairs={{0,16},{4,20},{8,24},{12,28},{16,0},{20,4},{24,8},{28,12},{1,17},{... | collective-permute-start | bytes 983048 | tf_op jit(solution)/shard_map/ppermute | solution.py:29
  32.7 1.4 %collective-permute-start.8 = (bf16[80,1024]{1,0:T(8,128)(2,1)S(1)}, bf16[80,1024]{1,0:T(8,128)(2,1)S(1)}, u32[]{:S(2)}, u32[]{:S(2)}) collective-permute-start(bf16[80,1024]{1,0:T(8,128)(2,1)S(1)} %collective-permute-done.7.refs_3_), channel_id=1, source_target_pairs={{0,4},{4,0},{8,12},{12,8},{16,20},{20,16},{24,28},{28,24},{1,5},{5... | collective-permute-start | bytes 491528 | tf_op jit(solution)/shard_map/ppermute | solution.py:29
  34.1 6.3 %collective-permute-start.9 = (bf16[32,1024]{1,0:T(8,128)(2,1)S(1)}, bf16[32,1024]{1,0:T(8,128)(2,1)S(1)}, u32[]{:S(2)}, u32[]{:S(2)}) collective-permute-start(bf16[32,1024]{1,0:T(8,128)(2,1)S(1)} %get-tuple-element.53), channel_id=1, source_target_pairs={{0,3},{1,2},{2,1},{3,0},{4,7},{5,6},{6,5},{7,4},{8,11},{9,10},{10,... | collective-permute-start | bytes 196616 | tf_op jit(solution)/shard_map/ppermute | solution.py:29
  37.7 5.9 %collective-permute-start.10 = (bf16[32,1024]{1,0:T(8,128)(2,1)S(1)}, bf16[32,1024]{1,0:T(8,128)(2,1)S(1)}, u32[]{:S(2)}, u32[]{:S(2)}) collective-permute-start(bf16[32,1024]{1,0:T(8,128)(2,1)S(1)} %get-tuple-element.54), channel_id=1, source_target_pairs={{0,2},{1,3},{2,0},{3,1},{4,6},{5,7},{6,4},{7,5},{8,10},{9,11},{10,... | collective-permute-start | bytes 196616 | tf_op jit(solution)/shard_map/ppermute | solution.py:29
  37.7 5.9 %collective-permute-start.11 = (bf16[32,1024]{1,0:T(8,128)(2,1)S(1)}, bf16[32,1024]{1,0:T(8,128)(2,1)S(1)}, u32[]{:S(2)}, u32[]{:S(2)}) collective-permute-start(bf16[32,1024]{1,0:T(8,128)(2,1)S(1)} %get-tuple-element.55), channel_id=1, source_target_pairs={{0,1},{1,0},{2,3},{3,2},{4,5},{5,4},{6,7},{7,6},{8,9},{9,8},{10,11... | collective-permute-start | bytes 196616 | tf_op jit(solution)/shard_map/ppermute | solution.py:29
  40.4 6.2 %collective-permute-start.14 = (bf16[80,1024]{1,0:T(8,128)(2,1)S(1)}, bf16[80,1024]{1,0:T(8,128)(2,1)S(1)}, u32[]{:S(2)}, u32[]{:S(2)}) collective-permute-start(bf16[80,1024]{1,0:T(8,128)(2,1)S(1)} %get-tuple-element.44.late_ref), channel_id=1, source_target_pairs={{0,24},{4,28},{8,16},{12,20},{16,8},{20,12},{24,0},{28,4},{1,25},{... | collective-permute-start | bytes 491528 | tf_op jit(solution)/shard_map/ppermute | solution.py:29
  43.6 0.7 %copy-start.5 = (s32[1,1,4,16]{3,2,1,0:T(4,128)S(1)}, s32[1,1,4,16]{3,2,1,0:T(4,128)}, u32[]{:S(2)}) copy-start(s32[1,1,4,16]{3,2,1,0:T(4,128)} %param.8) | copy-start | bytes 772
  43.6 4.4 %collective-permute-start.15 = (bf16[160,1024]{1,0:T(8,128)(2,1)S(1)}, bf16[160,1024]{1,0:T(8,128)(2,1)S(1)}, u32[]{:S(2)}, u32[]{:S(2)}) collective-permute-start(bf16[160,1024]{1,0:T(8,128)(2,1)S(1)} %get-tuple-element.62.refs_0_), channel_id=1, source_target_pairs={{0,4},{4,0},{8,12},{12,8},{16,20},{20,16},{24,28},{28,24},{1,5},{5... | collective-permute-start | bytes 983048 | tf_op jit(solution)/shard_map/ppermute | solution.py:29
  43.6 4.4 %collective-permute-start.16 = (bf16[160,1024]{1,0:T(8,128)(2,1)S(1)}, bf16[160,1024]{1,0:T(8,128)(2,1)S(1)}, u32[]{:S(2)}, u32[]{:S(2)}) collective-permute-start(bf16[160,1024]{1,0:T(8,128)(2,1)S(1)} %collective-permute-done.12.refs_1_), channel_id=1, source_target_pairs={{0,4},{4,0},{8,12},{12,8},{16,20},{20,16},{24,28},{28,24},{1,5},{5... | collective-permute-start | bytes 983048 | tf_op jit(solution)/shard_map/ppermute | solution.py:29
  44.2 3.8 %collective-permute-start.17 = (bf16[160,1024]{1,0:T(8,128)(2,1)S(1)}, bf16[160,1024]{1,0:T(8,128)(2,1)S(1)}, u32[]{:S(2)}, u32[]{:S(2)}) collective-permute-start(bf16[160,1024]{1,0:T(8,128)(2,1)S(1)} %collective-permute-done.13.refs_2_), channel_id=1, source_target_pairs={{0,4},{4,0},{8,12},{12,8},{16,20},{20,16},{24,28},{28,24},{1,5},{5... | collective-permute-start | bytes 983048 | tf_op jit(solution)/shard_map/ppermute | solution.py:29
  46.6 1.4 %collective-permute-start.18 = (bf16[80,1024]{1,0:T(8,128)(2,1)S(1)}, bf16[80,1024]{1,0:T(8,128)(2,1)S(1)}, u32[]{:S(2)}, u32[]{:S(2)}) collective-permute-start(bf16[80,1024]{1,0:T(8,128)(2,1)S(1)} %collective-permute-done.14.refs_4_), channel_id=1, source_target_pairs={{0,4},{4,0},{8,12},{12,8},{16,20},{20,16},{24,28},{28,24},{1,5},{5... | collective-permute-start | bytes 491528 | tf_op jit(solution)/shard_map/ppermute | solution.py:29
